TPU v7x, 128 devices: a whole 4x4x4 slice. The times are simulated.
128 devices in a mesh: cls: 4 (over x_hi, core), img: 32 (over x_lo, z, y).
Axes of the slice: x: 4 (x_hi: 2, x_lo: 2; x = x_hi * 2 + x_lo), y: 4, z: 4, core: 2. Of those that a mesh axis runs over, the one named last changes fastest.
Arguments:
- particles: float32 [4096, 4096], P(('cls', 'img')), may hold values from -48 to 48
- rot_prior: int32 [4096], P(('cls', 'img')), may hold values from 0 to 11
- panels: bfloat16 [100, 12, 4096], P('cls', None, 'img'), may hold values from -4.5 to 4.5
- log_prior: float32 [100], P('cls'), may hold values from -0.5 to 3.7
- shift_table: int32 [11, 2], replicated, may hold values from -4 to 4, as said below
Outputs:
- class_sums: float32 [100, 12, 4096], P('cls', None, 'img')
- weight_totals: float32 [100, 12], P('cls')
- log_evidence: float32 [4096], P(('cls', 'img'))
Inputs may be any that keep to these rules, and one draw needn't show every extreme that they name: `shift_table`: the 11 rows are distinct offsets; each entry lies within -4 to 4.
All inputs are finite; a program needn't handle non-finite values.
Results may differ from a plain program's by a relative error of at most 0.0085.
Values may be sent and summed in bfloat16 or wider, within the bound.
No kernel may reach another device: no remote copies, remote signals or barrier semaphores. Data moves between devices by JAX's collectives and lax.ppermute only.
A program may use at most 128 MiB of HBM per device.

v0:
```python
import math

import jax
import jax.numpy as jnp
from jax import lax
from jax.experimental import pallas as pl
from jax.experimental.pallas import tpu as pltpu
from jax.sharding import PartitionSpec as P

SCORE_GAIN = 2.5
PRIOR_WEIGHT = 1.0
AXES = ("cls", "img")
SIDE = 64
PIX = SIDE * SIDE
LANES = 128
BLOCKS = PIX // LANES
ROT = 12
HALF_ROT = ROT // 2
CLS = 25
USED = HALF_ROT * CLS
ROWS = 160
OWN = 32
ROW_IMAGES = 8 * OWN
SHIFTS = 11
MARGIN = 8
NEG = -1.0e30
Z_ORDER = (0, -1, 1, 2)


def flat(x, core, z, y):
    x %= 4
    return ((x // 2) * 2 + core % 2) * 32 + (x % 2) * 16 + (z % 4) * 4 + y % 4


COORDS = [(x, c, z, y) for x in range(4) for c in range(2) for z in range(4) for y in range(4)]
X_ROWS = [[flat(x, c, z, y) for x in range(4) for c in range(2)] for z in range(4) for y in range(4)]


def move(value, x=0, core=0, z=0, y=0):
    route = [(flat(*a), flat(a[0] + x, a[1] + core, a[2] + z, a[3] + y)) for a in COORDS]
    return lax.ppermute(value, AXES, route)


def swap_x(value):
    route = [(flat(x, c, z, y), flat(x ^ 1, c, z, y)) for x, c, z, y in COORDS]
    return lax.ppermute(value, AXES, route)


def position():
    cls, img = lax.axis_index("cls"), lax.axis_index("img")
    x_lo, z, y = img // 16, (img // 4) % 4, img % 4
    return (cls // 2) * 2 + x_lo, cls % 2, x_lo, z, y


def shifted_pixels(t_ref, rows, dy, dx):
    parts = []
    for row in rows:
        at = jnp.bitwise_and(row + dy, SIDE - 1)
        tiles = [t_ref[t, at, pl.ds(MARGIN + dx, SIDE), :] for t in range(2)]
        parts.append(jnp.concatenate(tiles, axis=1).astype(jnp.bfloat16))
    return jnp.concatenate(parts, axis=0)


def score_kernel(shift_ref, *refs):
    images = refs[:10]
    pc, py1, py3, pw0, pw1, info_ref, e_ref, st_ref, t_ref, x_ref = refs[10:]
    x, core, x_lo, z, y = position()
    gain = SCORE_GAIN / math.sqrt(PIX)

    def put(ref, dx, dc, part=0):
        slot = jnp.bitwise_and(x + dx, 3) * 2 + jnp.bitwise_xor(core, dc)
        start = pl.multiple_of(slot * OWN + part * 16, 16)
        x_ref[pl.ds(start, ref.shape[0]), :] = ref[...]

    own, a1, a2, c0, b1, b2, c1, c2, d1, d2 = images
    put(own, 0, 0)
    put(a1, -1, 0)
    put(a2, 1, 0)
    put(c0, 0, 1)
    put(c1, -1, 1)
    put(c2, 1, 1)
    put(b1, 2, 0, 0)
    put(b2, 2, 0, 1)
    put(d1, 2, 1, 0)
    put(d2, 2, 1, 1)

    def transpose_block(block, carry):
        for t in range(2):
            lanes = pl.ds(pl.multiple_of(block * LANES, LANES), LANES)
            tile = x_ref[pl.ds(t * LANES, LANES), lanes].astype(jnp.float32).T
            for half in range(2):
                line = tile[half * SIDE : (half + 1) * SIDE]
                t_ref[t, 2 * block + half, pl.ds(MARGIN, SIDE), :] = line
                t_ref[t, 2 * block + half, pl.ds(0, MARGIN), :] = line[SIDE - MARGIN :]
                t_ref[t, 2 * block + half, pl.ds(MARGIN + SIDE, MARGIN), :] = line[:MARGIN]
        return carry

    lax.fori_loop(0, BLOCKS, transpose_block, 0)

    pairs = [(pc, 2 * i, dz, 0) for i, dz in enumerate(Z_ORDER)]
    pairs += [(py1, 2 * i, dz, -1) for i, dz in enumerate(Z_ORDER)]
    pairs += [(py3, 2 * i, dz, 1) for i, dz in enumerate(Z_ORDER)]
    pairs += [(pw0, 2 * i, dz, 2) for i, dz in enumerate(Z_ORDER[:2])]
    pairs += [(pw1, 2 * i, dz, 2) for i, dz in enumerate(Z_ORDER[2:])]

    squares = jnp.zeros((ROWS, LANES), jnp.float32)
    for ref, at, _, _ in pairs:
        for k in range(2):
            value = ref[at + k].astype(jnp.float32)
            squares = squares + value * value
    norms = jnp.sum(squares, axis=1, keepdims=True)
    rots = [
        x_ref[pl.ds(t * LANES, LANES), PIX : PIX + LANES].astype(jnp.float32).T[0:1]
        for t in range(2)
    ]
    angle = jnp.concatenate(rots, axis=1) * (2.0 * math.pi / ROT)
    info = info_ref[...]
    prior = info[:, 1:2] * jnp.cos(angle) + info[:, 2:3] * jnp.sin(angle)
    bias = info[:, 0:1] - 0.5 * gain * norms + PRIOR_WEIGHT * prior

    def one_shift(s, peak):
        dy, dx = shift_ref[s, 0], shift_ref[s, 1]
        acc = jnp.zeros((ROWS, ROW_IMAGES), jnp.float32)
        for ref, at, dz, dyy in pairs:
            base = jnp.bitwise_and(z + dz, 3) * 4 + jnp.bitwise_and(y + dyy, 3)
            j0 = x_lo * 16 + base
            j1 = (1 - x_lo) * 16 + base
            moved = shifted_pixels(t_ref, (2 * j0, 2 * j0 + 1, 2 * j1, 2 * j1 + 1), dy, dx)
            panel = jnp.concatenate([ref[at], ref[at + 1]], axis=1)
            acc = acc + jnp.dot(panel, moved, preferred_element_type=jnp.float32)
        scores = gain * acc + bias
        e_ref[s] = scores
        return jnp.maximum(peak, jnp.max(scores, axis=0, keepdims=True))

    peak = lax.fori_loop(0, SHIFTS, one_shift, jnp.full((1, ROW_IMAGES), NEG, jnp.float32))

    def one_exp(s, total):
        value = jnp.exp(e_ref[s] - peak)
        e_ref[s] = value
        return total + jnp.sum(value, axis=0, keepdims=True)

    total = lax.fori_loop(0, SHIFTS, one_exp, jnp.zeros((1, ROW_IMAGES), jnp.float32))
    stats = jnp.concatenate(
        [
            peak[:, :LANES],
            peak[:, LANES:],
            total[:, :LANES],
            total[:, LANES:],
            jnp.zeros((4, LANES), jnp.float32),
        ],
        axis=0,
    )
    for k in range(8):
        st_ref[k] = stats


def sum_kernel(shift_ref, e_ref, st_ref, all_ref, t_ref, out_ref, ev_ref, w_ref):
    x, core, _, _, _ = position()
    stats = [all_ref[k] for k in range(8)]
    peak = stats[0][0:2]
    for k in range(1, 8):
        peak = jnp.maximum(peak, stats[k][0:2])
    total = jnp.zeros((2, LANES), jnp.float32)
    for k in range(8):
        total = total + stats[k][2:4] * jnp.exp(stats[k][0:2] - peak)
    evidence = peak + jnp.log(total)
    slot = x * 2 + core
    mine = jnp.where(slot >= 4, evidence[1:2], evidence[0:1])
    groups = [mine[:, k * OWN : (k + 1) * OWN] for k in range(4)]
    at = jnp.bitwise_and(slot, 3)
    picked = groups[0]
    for k in range(1, 4):
        picked = jnp.where(at == k, groups[k], picked)
    ev_ref[...] = picked
    factor = jnp.exp(st_ref[0][0:2] - peak) / total
    factor = jnp.concatenate([factor[0:1], factor[1:2]], axis=1)

    def one_weight(s, totals):
        weight = (e_ref[s] * factor).astype(jnp.bfloat16)
        w_ref[s] = weight
        ones = jnp.ones((8, ROW_IMAGES), jnp.bfloat16)
        return totals + lax.dot_general(
            ones, weight, (((1,), (1,)), ((), ())), preferred_element_type=jnp.float32
        )

    totals = lax.fori_loop(0, SHIFTS, one_weight, jnp.zeros((8, ROWS), jnp.float32))[0:1]
    totals = jnp.concatenate([totals, jnp.zeros((1, 2 * LANES - ROWS), jnp.float32)], axis=1)
    pieces = []
    for _ in range(3):
        part = totals.astype(jnp.bfloat16).astype(jnp.float32)
        totals = totals - part
        pieces += [part[:, :LANES], part[:, LANES:]]
    tail = jnp.concatenate(
        [jnp.zeros((6, LANES), jnp.float32)] + pieces + [jnp.zeros((4, LANES), jnp.float32)], axis=0
    )

    def one_block(pair, carry):
        rows = tuple(4 * pair + k for k in range(4))
        acc = jnp.zeros((ROWS, 2 * LANES), jnp.float32)
        for s in range(SHIFTS):
            moved = shifted_pixels(t_ref, rows, shift_ref[s, 0], shift_ref[s, 1])
            acc = acc + lax.dot_general(
                w_ref[s], moved, (((1,), (1,)), ((), ())), preferred_element_type=jnp.float32
            )
        for k in range(2):
            part = acc[:, k * LANES : (k + 1) * LANES]
            out_ref[2 * pair + k, 0 : ROWS - 16, :] = part[: ROWS - 16].astype(jnp.bfloat16)
            out_ref[2 * pair + k, ROWS - 16 : ROWS, :] = (part[ROWS - 16 :] + tail).astype(
                jnp.bfloat16
            )
        return carry

    lax.fori_loop(0, BLOCKS // 2, one_block, 0)


def finish_kernel(in_ref, out_ref, wt_ref):
    for half in range(2):
        acc = jnp.zeros((ROWS, LANES), jnp.float32)
        for k in range(16):
            acc = acc + in_ref[half * 16 + k].astype(jnp.float32)
        for r in range(HALF_ROT):
            out_ref[half * HALF_ROT + r] = acc[r * CLS : (r + 1) * CLS]
        wide = [
            acc[USED + k : USED + k + 1] + acc[USED + 2 + k : USED + 3 + k]
            + acc[USED + 4 + k : USED + 5 + k]
            for k in range(2)
        ]
        totals = jnp.concatenate(wide, axis=1)
        for r in range(HALF_ROT):
            row = half * HALF_ROT + r
            wt_ref[row : row + 1, :] = totals[:, r * CLS : (r + 1) * CLS]


VMEM = pl.BlockSpec(memory_space=pltpu.VMEM)
SMEM = pl.BlockSpec(memory_space=pltpu.SMEM)
PARAMS = pltpu.CompilerParams(vmem_limit_bytes=40 * 1024 * 1024)


def shards(particles, rot_prior, panels, log_prior, shift_table):
    x_lo = lax.axis_index("img") // 16

    by_rot = jnp.transpose(panels, (1, 0, 2)).reshape(2, USED, LANES)
    by_rot = jnp.pad(by_rot, ((0, 0), (0, ROWS - USED), (0, 0)))
    keep = jnp.where(x_lo == 0, by_rot[0], by_rot[1])
    give = jnp.where(x_lo == 0, by_rot[1], by_rot[0])
    images = jnp.concatenate(
        [
            particles.astype(jnp.bfloat16),
            jnp.broadcast_to(rot_prior.astype(jnp.bfloat16)[:, None], (OWN, LANES)),
        ],
        axis=1,
    )
    got = swap_x(give)
    a1 = move(images, x=1)
    a2 = move(images, x=-1)
    c0 = move(images, core=1)
    first = jnp.stack([keep, got])
    u = move(first, z=1)
    v = move(first, z=-1)
    b1 = move(a1[:16], x=1)
    b2 = move(a2[16:], x=-1)
    w0 = move(u[0], z=1)
    w1 = move(v[1], z=-1)
    c1 = move(a1, core=1)
    c2 = move(a2, core=1)
    column = jnp.concatenate([first, u, v, w0[None], w1[None]], axis=0)
    y1 = move(column, y=1)
    y3 = move(column, y=-1)
    d1 = move(b1, core=1)
    d2 = move(b2, core=1)
    yw0 = move(y1[:4], y=1)
    yw1 = move(y3[4:], y=-1)

    row = jnp.arange(ROWS)
    rot = (row // CLS + HALF_ROT * x_lo).astype(jnp.float32) * (2.0 * math.pi / ROT)
    logs = jnp.pad(jnp.tile(log_prior, HALF_ROT), (0, ROWS - USED), constant_values=NEG)
    info = jnp.stack([logs, jnp.cos(rot), jnp.sin(rot)], axis=1)

    scores, stats, flipped = pl.pallas_call(
        score_kernel,
        out_shape=(
            jax.ShapeDtypeStruct((SHIFTS, ROWS, ROW_IMAGES), jnp.float32),
            jax.ShapeDtypeStruct((8, 8, LANES), jnp.float32),
            jax.ShapeDtypeStruct((2, SIDE, SIDE + 2 * MARGIN, LANES), jnp.float32),
        ),
        in_specs=[SMEM] + [VMEM] * 16,
        out_specs=(VMEM, VMEM, VMEM),
        scratch_shapes=[pltpu.VMEM((ROW_IMAGES, PIX + LANES), jnp.bfloat16)],
        compiler_params=PARAMS,
        name="scores",
    )(
        shift_table, images, a1, a2, c0, b1, b2, c1, c2, d1, d2, column, y1, y3, yw0, yw1, info
    )
    all_stats = lax.all_to_all(stats, AXES, 0, 0, axis_index_groups=X_ROWS)
    blocks, evidence = pl.pallas_call(
        sum_kernel,
        out_shape=(
            jax.ShapeDtypeStruct((BLOCKS, ROWS, LANES), jnp.bfloat16),
            jax.ShapeDtypeStruct((1, OWN), jnp.float32),
        ),
        in_specs=[SMEM] + [VMEM] * 4,
        out_specs=(VMEM, VMEM),
        scratch_shapes=[pltpu.VMEM((SHIFTS, ROWS, ROW_IMAGES), jnp.bfloat16)],
        compiler_params=PARAMS,
        name="sums",
    )(shift_table, scores, stats, all_stats, flipped)
    shares = lax.all_to_all(blocks, "img", 0, 0)
    sums, totals = pl.pallas_call(
        finish_kernel,
        out_shape=(
            jax.ShapeDtypeStruct((ROT, CLS, LANES), jnp.float32),
            jax.ShapeDtypeStruct((ROT, CLS), jnp.float32),
        ),
        in_specs=[VMEM],
        out_specs=(VMEM, VMEM),
        compiler_params=PARAMS,
        name="finish",
    )(shares)
    return jnp.transpose(sums, (1, 0, 2)), totals.T, evidence.reshape(OWN)


def solution(mesh):
    placed = (P(AXES, None), P(AXES), P("cls", None, "img"), P("cls"), P())
    return jax.shard_map(
        shards,
        mesh=mesh,
        in_specs=placed,
        out_specs=(P("cls", None, "img"), P("cls", None), P(AXES)),
        check_vma=False,
    )
```

profile of v0, /device:TPU:0, one launch (start us, length us, event | category | flops | bytes accessed | tf_op | source)
XLA Modules:
  0.0 107.2 jit_solution(4140402341332347095)
XLA Ops:
  0.6 0.9 reshape.66
  1.6 1.7 %collective-permute-start.9 = (bf16[160,128]{1,0:T(8,128)(2,1)S(1)}, bf16[160,128]{1,0:T(8,128)(2,1)S(1)}, u32[]{:S(2)}, u32[]{:S(2)}) collective-permute-start(bf16[160,128]{1,0:T(8,128)(2,1)S(1)} %get-tuple-element.19), channel_id=1, source_target_pairs={{0,16},{1,17},{2,18},{3,19},{4,20},{5,21},{6,22},{7,23},{8,24},{9,... | collective-permute-start | bytes 122888 | tf_op jit(solution)/shard_map/ppermute | solution.py:46
  3.3 0.7 convert_element_type.23
  3.9 1.1 convert_element_type.22
  5.0 0.1 broadcast_in_dim.12
  5.1 2.2 %collective-permute-start.1 = (bf16[32,4224]{1,0:T(8,128)(2,1)S(1)}, bf16[32,4224]{1,0:T(8,128)(2,1)S(1)}, u32[]{:S(2)}, u32[]{:S(2)}) collective-permute-start(bf16[32,4224]{1,0:T(8,128)(2,1)S(1)} %pad_maximum_fusion.refs_0_), channel_id=1, source_target_pairs={{0,80},{1,81},{2,82},{3,83},{4,84},{5,85},{6,86},{7,87},{8,88},{9,... | collective-permute-start | bytes 811016 | tf_op jit(solution)/shard_map/ppermute | solution.py:41
  7.3 4.1 %collective-permute-start.11 = (bf16[2,160,128]{2,1,0:T(8,128)(2,1)S(1)}, bf16[2,160,128]{2,1,0:T(8,128)(2,1)S(1)}, u32[]{:S(2)}, u32[]{:S(2)}) collective-permute-start(bf16[2,160,128]{2,1,0:T(8,128)(2,1)S(1)} %pad_maximum_fusion.1), channel_id=1, source_target_pairs={{0,12},{1,13},{2,14},{3,15},{4,0},{5,1},{6,2},{7,3},{8,4},{9,5},{1... | collective-permute-start | bytes 245768 | tf_op jit(solution)/shard_map/ppermute | solution.py:41
  11.4 2.0 %collective-permute-done.11 = bf16[2,160,128]{2,1,0:T(8,128)(2,1)S(1)} collective-permute-done((bf16[2,160,128]{2,1,0:T(8,128)(2,1)S(1)}, bf16[2,160,128]{2,1,0:T(8,128)(2,1)S(1)}, u32[]{:S(2)}, u32[]{:S(2)}) %collective-permute-start.11) | collective-permute-done | bytes 81952 | tf_op jit(solution)/shard_map/ppermute | solution.py:41
  13.5 3.6 %collective-permute-start.13 = (bf16[160,128]{1,0:T(8,128)(2,1)S(1)}, bf16[160,128]{1,0:T(8,128)(2,1)S(1)}, u32[]{:S(2)}, u32[]{:S(2)}) collective-permute-start(bf16[160,128]{1,0:T(8,128)(2,1)S(1)} %slice_bitcast_fusion), channel_id=1, source_target_pairs={{0,12},{1,13},{2,14},{3,15},{4,0},{5,1},{6,2},{7,3},{8,4},{9,5},{1... | collective-permute-start | bytes 122888 | tf_op jit(solution)/shard_map/ppermute | solution.py:41
  17.1 5.2 %collective-permute-done.12 = bf16[160,128]{1,0:T(8,128)(2,1)S(1)} collective-permute-done((bf16[160,128]{1,0:T(8,128)(2,1)S(1)}, bf16[160,128]{1,0:T(8,128)(2,1)S(1)}, u32[]{:S(2)}, u32[]{:S(2)}) %collective-permute-start.12) | collective-permute-done | bytes 40992 | tf_op jit(solution)/shard_map/ppermute | solution.py:41
  22.3 3.1 %collective-permute-start.15 = (bf16[8,160,128]{2,1,0:T(8,128)(2,1)S(1)}, bf16[8,160,128]{2,1,0:T(8,128)(2,1)S(1)}, u32[]{:S(2)}, u32[]{:S(2)}) collective-permute-start(bf16[8,160,128]{2,1,0:T(8,128)(2,1)S(1)} %bitcast_dynamic-update-slice_fusion.refs_10_), channel_id=1, source_target_pairs={{0,3},{1,0},{2,1},{3,2},{4,7},{5,4},{6,5},{7,6},{8,11},{9,8},{10,9... | collective-permute-start | bytes 983048 | tf_op jit(solution)/shard_map/ppermute | solution.py:41
  25.4 3.3 %collective-permute-start.4 = (bf16[16,4224]{1,0:T(8,128)(2,1)S(1)}, bf16[16,4224]{1,0:T(8,128)(2,1)S(1)}, u32[]{:S(2)}, u32[]{:S(2)}) collective-permute-start(bf16[16,4224]{1,0:T(8,128)(2,1)S(1)} %slice.35), channel_id=1, source_target_pairs={{0,80},{1,81},{2,82},{3,83},{4,84},{5,85},{6,86},{7,87},{8,88},{9,... | collective-permute-start | bytes 405512 | tf_op jit(solution)/shard_map/ppermute | solution.py:41
  28.7 0.1 collective-permute-start.3
  28.8 3.4 %collective-permute-done.4.refs_5_ = bf16[16,4224]{1,0:T(8,128)(2,1)S(1)} collective-permute-done((bf16[16,4224]{1,0:T(8,128)(2,1)S(1)}, bf16[16,4224]{1,0:T(8,128)(2,1)S(1)}, u32[]{:S(2)}, u32[]{:S(2)}) %collective-permute-start.4) | collective-permute-done | bytes 135200 | tf_op jit(solution)/shard_map/ppermute | solution.py:41
  32.2 3.5 %collective-permute-done.3.refs_4_ = bf16[16,4224]{1,0:T(8,128)(2,1)S(1)} collective-permute-done((bf16[16,4224]{1,0:T(8,128)(2,1)S(1)}, bf16[16,4224]{1,0:T(8,128)(2,1)S(1)}, u32[]{:S(2)}, u32[]{:S(2)}) %collective-permute-start.3) | collective-permute-done | bytes 135200 | tf_op jit(solution)/shard_map/ppermute | solution.py:41
  35.7 0.5 collective-permute-start.5
  36.3 0.7 slice.39
  36.9 0.7 slice.38
  37.6 3.2 %collective-permute-start.17 = (bf16[4,160,128]{2,1,0:T(8,128)(2,1)}, bf16[4,160,128]{2,1,0:T(8,128)(2,1)S(1)}, u32[]{:S(2)}, u32[]{:S(2)}) collective-permute-start(bf16[4,160,128]{2,1,0:T(8,128)(2,1)} %slice.39), channel_id=1, source_target_pairs={{0,3},{1,0},{2,1},{3,2},{4,7},{5,4},{6,5},{7,6},{8,11},{9,8},{10,9... | collective-permute-start | bytes 491528 | tf_op jit(solution)/shard_map/ppermute | solution.py:41
  40.9 0.1 fusion.3
  40.9 0.1 tile.10
  41.0 0.7 copy.15.shift_ref
  41.7 0.6 pad_maximum_fusion.2
  42.3 0.8 copy.14.refs_15_
  43.1 2.2 %collective-permute-done.17.refs_14_ = bf16[4,160,128]{2,1,0:T(8,128)(2,1)S(1)} collective-permute-done((bf16[4,160,128]{2,1,0:T(8,128)(2,1)}, bf16[4,160,128]{2,1,0:T(8,128)(2,1)S(1)}, u32[]{:S(2)}, u32[]{:S(2)}) %collective-permute-start.17) | collective-permute-done | bytes 163872 | tf_op jit(solution)/shard_map/ppermute | solution.py:41
  45.3 3.3 %collective-permute-done.16.refs_13_ = bf16[4,160,128]{2,1,0:T(8,128)(2,1)S(1)} collective-permute-done((bf16[4,160,128]{2,1,0:T(8,128)(2,1)}, bf16[4,160,128]{2,1,0:T(8,128)(2,1)S(1)}, u32[]{:S(2)}, u32[]{:S(2)}) %collective-permute-start.16) | collective-permute-done | bytes 163872 | tf_op jit(solution)/shard_map/ppermute | solution.py:41
  48.6 0.7 copy-done
  49.3 11.9 %scores.1 = (f32[11,160,256]{2,1,0:T(8,128)S(1)}, f32[8,8,128]{2,1,0:T(8,128)S(1)}, f32[2,64,80,128]{3,2,1,0:T(8,128)S(1)}) custom-call(s32[11,2]{1,0:T(8,128)S(1)} %copy-done, bf16[32,4224]{1,0:T(8,128)(2,1)S(1)} %pad_maximum_fusion.refs_0_, bf16[32,4224]{1,0:T(8,128)(2,1)S(1)} %collective-permute-done.refs_1_, ...), custom_call_target="tpu_custom_call" | custom-call | tf_op jit(solution)/shard_map/scores/pallas_call | solution.py:279
  61.2 7.8 %all_to_all.10.all_ref = f32[8,8,128]{2,1,0:T(8,128)S(1)} all-to-all(f32[8,8,128]{2,1,0:T(8,128)S(1)} %get-tuple-element.11.st_ref), channel_id=1, replica_groups={{0,32,16,48,64,96,80,112},{1,33,17,49,65,97,81,113},{2,34,18,50,66,98,8..., dimensions={0} | all-to-all | bytes 65536 | tf_op jit(solution)/shard_map/all_to_all | solution.py:294
  69.0 13.8 %sums.1 = (bf16[32,160,128]{2,1,0:T(8,128)(2,1)S(1)}, f32[1,32]{1,0:T(1,128)}) custom-call(s32[11,2]{1,0:T(8,128)S(1)} %copy-done.1, f32[11,160,256]{2,1,0:T(8,128)S(1)} %get-tuple-element.10.e_ref, f32[8,8,128]{2,1,0:T(8,128)S(1)} %get-tuple-element.11.st_ref, f32[8,8,128]{2,1,0:T(8,128)S(1)} %all_to_all.10.all_ref, ...), custom_call_target="tpu_custom_call" | custom-call | tf_op jit(solution)/shard_map/sums/pallas_call | solution.py:295
  82.8 23.5 %all_to_all.11.in_ref = bf16[32,160,128]{2,1,0:T(8,128)(2,1)S(1)} all-to-all(bf16[32,160,128]{2,1,0:T(8,128)(2,1)S(1)} %get-tuple-element.13), channel_id=1, replica_groups=mesh['cls'=4,'img'=32] {'img'}, dimensions={0} | all-to-all | bytes 2621440 | tf_op jit(solution)/shard_map/all_to_all | solution.py:307
  106.3 0.9 finish.1
  (42 shorter events, 0.2 us)
Async XLA Ops:
  1.6 39.4 %copy-start.3 = (f32[25]{0:T(128)S(1)}, f32[25]{0:T(128)}, u32[]{:S(2)}) copy-start(f32[25]{0:T(128)} %param.8) | copy-start | bytes 304
  1.6 39.4 %copy-start.2 = (s32[11,2]{0,1:T(2,128)S(1)}, s32[11,2]{0,1:T(2,128)}, u32[]{:S(2)}) copy-start(s32[11,2]{0,1:T(2,128)} %param.9) | copy-start | bytes 268
  1.6 5.7 %collective-permute-start.9 = (bf16[160,128]{1,0:T(8,128)(2,1)S(1)}, bf16[160,128]{1,0:T(8,128)(2,1)S(1)}, u32[]{:S(2)}, u32[]{:S(2)}) collective-permute-start(bf16[160,128]{1,0:T(8,128)(2,1)S(1)} %get-tuple-element.19), channel_id=1, source_target_pairs={{0,16},{1,17},{2,18},{3,19},{4,20},{5,21},{6,22},{7,23},{8,24},{9,... | collective-permute-start | bytes 122888 | tf_op jit(solution)/shard_map/ppermute | solution.py:46
  5.1 20.3 %collective-permute-start.1 = (bf16[32,4224]{1,0:T(8,128)(2,1)S(1)}, bf16[32,4224]{1,0:T(8,128)(2,1)S(1)}, u32[]{:S(2)}, u32[]{:S(2)}) collective-permute-start(bf16[32,4224]{1,0:T(8,128)(2,1)S(1)} %pad_maximum_fusion.refs_0_), channel_id=1, source_target_pairs={{0,80},{1,81},{2,82},{3,83},{4,84},{5,85},{6,86},{7,87},{8,88},{9,... | collective-permute-start | bytes 811016 | tf_op jit(solution)/shard_map/ppermute | solution.py:41
  7.3 21.5 %collective-permute-start = (bf16[32,4224]{1,0:T(8,128)(2,1)S(1)}, bf16[32,4224]{1,0:T(8,128)(2,1)S(1)}, u32[]{:S(2)}, u32[]{:S(2)}) collective-permute-start(bf16[32,4224]{1,0:T(8,128)(2,1)S(1)} %pad_maximum_fusion.refs_0_), channel_id=1, source_target_pairs={{0,16},{1,17},{2,18},{3,19},{4,20},{5,21},{6,22},{7,23},{8,24},{9,... | collective-permute-start | bytes 811016 | tf_op jit(solution)/shard_map/ppermute | solution.py:41
  7.3 6.2 %collective-permute-start.11 = (bf16[2,160,128]{2,1,0:T(8,128)(2,1)S(1)}, bf16[2,160,128]{2,1,0:T(8,128)(2,1)S(1)}, u32[]{:S(2)}, u32[]{:S(2)}) collective-permute-start(bf16[2,160,128]{2,1,0:T(8,128)(2,1)S(1)} %pad_maximum_fusion.1), channel_id=1, source_target_pairs={{0,12},{1,13},{2,14},{3,15},{4,0},{5,1},{6,2},{7,3},{8,4},{9,5},{1... | collective-permute-start | bytes 245768 | tf_op jit(solution)/shard_map/ppermute | solution.py:41
  11.4 5.7 %collective-permute-start.10 = (bf16[2,160,128]{2,1,0:T(8,128)(2,1)S(1)}, bf16[2,160,128]{2,1,0:T(8,128)(2,1)S(1)}, u32[]{:S(2)}, u32[]{:S(2)}) collective-permute-start(bf16[2,160,128]{2,1,0:T(8,128)(2,1)S(1)} %pad_maximum_fusion.1), channel_id=1, source_target_pairs={{0,4},{1,5},{2,6},{3,7},{4,8},{5,9},{6,10},{7,11},{8,12},{9,13},{1... | collective-permute-start | bytes 245768 | tf_op jit(solution)/shard_map/ppermute | solution.py:41
  13.5 8.8 %collective-permute-start.13 = (bf16[160,128]{1,0:T(8,128)(2,1)S(1)}, bf16[160,128]{1,0:T(8,128)(2,1)S(1)}, u32[]{:S(2)}, u32[]{:S(2)}) collective-permute-start(bf16[160,128]{1,0:T(8,128)(2,1)S(1)} %slice_bitcast_fusion), channel_id=1, source_target_pairs={{0,12},{1,13},{2,14},{3,15},{4,0},{5,1},{6,2},{7,3},{8,4},{9,5},{1... | collective-permute-start | bytes 122888 | tf_op jit(solution)/shard_map/ppermute | solution.py:41
  17.1 5.2 %collective-permute-start.12 = (bf16[160,128]{1,0:T(8,128)(2,1)S(1)}, bf16[160,128]{1,0:T(8,128)(2,1)S(1)}, u32[]{:S(2)}, u32[]{:S(2)}) collective-permute-start(bf16[160,128]{1,0:T(8,128)(2,1)S(1)} %slice_bitcast_fusion.1), channel_id=1, source_target_pairs={{0,4},{1,5},{2,6},{3,7},{4,8},{5,9},{6,10},{7,11},{8,12},{9,13},{1... | collective-permute-start | bytes 122888 | tf_op jit(solution)/shard_map/ppermute | solution.py:41
  22.3 13.4 %collective-permute-start.15 = (bf16[8,160,128]{2,1,0:T(8,128)(2,1)S(1)}, bf16[8,160,128]{2,1,0:T(8,128)(2,1)S(1)}, u32[]{:S(2)}, u32[]{:S(2)}) collective-permute-start(bf16[8,160,128]{2,1,0:T(8,128)(2,1)S(1)} %bitcast_dynamic-update-slice_fusion.refs_10_), channel_id=1, source_target_pairs={{0,3},{1,0},{2,1},{3,2},{4,7},{5,4},{6,5},{7,6},{8,11},{9,8},{10,9... | collective-permute-start | bytes 983048 | tf_op jit(solution)/shard_map/ppermute | solution.py:41
  25.4 11.5 %collective-permute-start.14 = (bf16[8,160,128]{2,1,0:T(8,128)(2,1)S(1)}, bf16[8,160,128]{2,1,0:T(8,128)(2,1)S(1)}, u32[]{:S(2)}, u32[]{:S(2)}) collective-permute-start(bf16[8,160,128]{2,1,0:T(8,128)(2,1)S(1)} %bitcast_dynamic-update-slice_fusion.refs_10_), channel_id=1, source_target_pairs={{0,1},{1,2},{2,3},{3,0},{4,5},{5,6},{6,7},{7,4},{8,9},{9,10},{10,1... | collective-permute-start | bytes 983048 | tf_op jit(solution)/shard_map/ppermute | solution.py:41
  25.4 12.2 %collective-permute-start.2 = (bf16[32,4224]{1,0:T(8,128)(2,1)S(1)}, bf16[32,4224]{1,0:T(8,128)(2,1)S(1)}, u32[]{:S(2)}, u32[]{:S(2)}) collective-permute-start(bf16[32,4224]{1,0:T(8,128)(2,1)S(1)} %pad_maximum_fusion.refs_0_), channel_id=1, source_target_pairs={{0,32},{1,33},{2,34},{3,35},{4,36},{5,37},{6,38},{7,39},{8,40},{9,... | collective-permute-start | bytes 811016 | tf_op jit(solution)/shard_map/ppermute | solution.py:41
  25.4 6.8 %collective-permute-start.4 = (bf16[16,4224]{1,0:T(8,128)(2,1)S(1)}, bf16[16,4224]{1,0:T(8,128)(2,1)S(1)}, u32[]{:S(2)}, u32[]{:S(2)}) collective-permute-start(bf16[16,4224]{1,0:T(8,128)(2,1)S(1)} %slice.35), channel_id=1, source_target_pairs={{0,80},{1,81},{2,82},{3,83},{4,84},{5,85},{6,86},{7,87},{8,88},{9,... | collective-permute-start | bytes 405512 | tf_op jit(solution)/shard_map/ppermute | solution.py:41
  28.7 7.0 %collective-permute-start.3 = (bf16[16,4224]{1,0:T(8,128)(2,1)S(1)}, bf16[16,4224]{1,0:T(8,128)(2,1)S(1)}, u32[]{:S(2)}, u32[]{:S(2)}) collective-permute-start(bf16[16,4224]{1,0:T(8,128)(2,1)S(1)} %slice.34), channel_id=1, source_target_pairs={{0,16},{1,17},{2,18},{3,19},{4,20},{5,21},{6,22},{7,23},{8,24},{9,... | collective-permute-start | bytes 405512 | tf_op jit(solution)/shard_map/ppermute | solution.py:41
  32.2 8.6 %collective-permute-start.8 = (bf16[16,4224]{1,0:T(8,128)(2,1)S(1)}, bf16[16,4224]{1,0:T(8,128)(2,1)S(1)}, u32[]{:S(2)}, u32[]{:S(2)}) collective-permute-start(bf16[16,4224]{1,0:T(8,128)(2,1)S(1)} %collective-permute-done.4.refs_5_), channel_id=1, source_target_pairs={{0,32},{1,33},{2,34},{3,35},{4,36},{5,37},{6,38},{7,39},{8,40},{9,... | collective-permute-start | bytes 405512 | tf_op jit(solution)/shard_map/ppermute | solution.py:41
  35.7 7.4 %collective-permute-start.6 = (bf16[32,4224]{1,0:T(8,128)(2,1)S(1)}, bf16[32,4224]{1,0:T(8,128)(2,1)S(1)}, u32[]{:S(2)}, u32[]{:S(2)}) collective-permute-start(bf16[32,4224]{1,0:T(8,128)(2,1)S(1)} %collective-permute-done.1.refs_2_), channel_id=1, source_target_pairs={{0,32},{1,33},{2,34},{3,35},{4,36},{5,37},{6,38},{7,39},{8,40},{9,... | collective-permute-start | bytes 811016 | tf_op jit(solution)/shard_map/ppermute | solution.py:41
  35.7 7.4 %collective-permute-start.5 = (bf16[32,4224]{1,0:T(8,128)(2,1)S(1)}, bf16[32,4224]{1,0:T(8,128)(2,1)S(1)}, u32[]{:S(2)}, u32[]{:S(2)}) collective-permute-start(bf16[32,4224]{1,0:T(8,128)(2,1)S(1)} %collective-permute-done.refs_1_), channel_id=1, source_target_pairs={{0,32},{1,33},{2,34},{3,35},{4,36},{5,37},{6,38},{7,39},{8,40},{9,... | collective-permute-start | bytes 811016 | tf_op jit(solution)/shard_map/ppermute | solution.py:41
  36.9 6.2 %collective-permute-start.7 = (bf16[16,4224]{1,0:T(8,128)(2,1)S(1)}, bf16[16,4224]{1,0:T(8,128)(2,1)S(1)}, u32[]{:S(2)}, u32[]{:S(2)}) collective-permute-start(bf16[16,4224]{1,0:T(8,128)(2,1)S(1)} %collective-permute-done.3.refs_4_), channel_id=1, source_target_pairs={{0,32},{1,33},{2,34},{3,35},{4,36},{5,37},{6,38},{7,39},{8,40},{9,... | collective-permute-start | bytes 405512 | tf_op jit(solution)/shard_map/ppermute | solution.py:41
  37.6 7.7 %collective-permute-start.17 = (bf16[4,160,128]{2,1,0:T(8,128)(2,1)}, bf16[4,160,128]{2,1,0:T(8,128)(2,1)S(1)}, u32[]{:S(2)}, u32[]{:S(2)}) collective-permute-start(bf16[4,160,128]{2,1,0:T(8,128)(2,1)} %slice.39), channel_id=1, source_target_pairs={{0,3},{1,0},{2,1},{3,2},{4,7},{5,4},{6,5},{7,6},{8,11},{9,8},{10,9... | collective-permute-start | bytes 491528 | tf_op jit(solution)/shard_map/ppermute | solution.py:41
  40.9 7.8 %collective-permute-start.16 = (bf16[4,160,128]{2,1,0:T(8,128)(2,1)}, bf16[4,160,128]{2,1,0:T(8,128)(2,1)S(1)}, u32[]{:S(2)}, u32[]{:S(2)}) collective-permute-start(bf16[4,160,128]{2,1,0:T(8,128)(2,1)} %slice.38), channel_id=1, source_target_pairs={{0,1},{1,2},{2,3},{3,0},{4,5},{5,6},{6,7},{7,4},{8,9},{9,10},{10,1... | collective-permute-start | bytes 491528 | tf_op jit(solution)/shard_map/ppermute | solution.py:41
  48.6 0.7 copy-start
  49.3 19.7 %copy-start.1 = (s32[11,2]{1,0:T(8,128)S(1)}, s32[11,2]{1,0:T(8,128)}, u32[]{:S(2)}) copy-start(s32[11,2]{1,0:T(8,128)} %copy.15.shift_ref) | copy-start | bytes 268
where the time goes:
time: 108 us; the launch traced here: 107 us
  blocking collectives  31.3 us (29%)
  Pallas kernels  26.5 us (25%)
  starting transfers between devices  21.7 us (20%)
  waiting for transfers between devices  19.6 us (18%)
  local copies, waits for them, and re-layouts  4.71 us (4%)
  other arithmetic  2.44 us (2%)
    all_to_all x1, blocking collectives, shards(): shares = lax.all_to_all(blocks, 'img', 0, 0)  23.5 us
    ppermute x17, starting transfers between devices, move(): return lax.ppermute(value, AXES, route)  20.1 us
    ppermute x17, waiting for transfers between devices, move(): return lax.ppermute(value, AXES, route)  19.6 us
    pallas_call x1, Pallas kernels, shards(): pl.pallas_call(sum_kernel, out_shape=(jax.ShapeDtypeStruct((BLOCKS, ROWS,...  13.8 us
    pallas_call x1, Pallas kernels, shards(): pl.pallas_call(score_kernel, out_shape=(jax.ShapeDtypeStruct((SHIFTS, ROW...  11.9 us
    all_to_all x1, blocking collectives, shards(): all_stats = lax.all_to_all(stats, AXES, 0, 0, axis_index_groups=X_ROWS)  7.82 us
  transfers between devices with their start and end apart: 18, of which 6 were waited for; matrix products, arithmetic and copies ran while one was open for 5% of the time, Pallas kernels for 0%

commit v1 on v0

v1 whole, which is shorter than its diff:
```python
import math

import jax
import jax.numpy as jnp
from jax import lax
from jax.experimental import pallas as pl
from jax.experimental.pallas import tpu as pltpu
from jax.sharding import PartitionSpec as P

SCORE_GAIN = 2.5
PRIOR_WEIGHT = 1.0
AXES = ("cls", "img")
SIDE = 64
PIX = SIDE * SIDE
LANES = 128
BLOCKS = PIX // LANES
ROT = 12
HALF_ROT = ROT // 2
CLS = 25
USED = HALF_ROT * CLS
ROWS = 160
OWN = 32
ROW_IMAGES = 8 * OWN
SHIFTS = 11
MARGIN = 8
NEG = -1.0e30
UNROLL = 4
Z_ORDER = (0, -1, 1, 2)


def flat(x, core, z, y):
    x %= 4
    return ((x // 2) * 2 + core % 2) * 32 + (x % 2) * 16 + (z % 4) * 4 + y % 4


COORDS = [(x, c, z, y) for x in range(4) for c in range(2) for z in range(4) for y in range(4)]
X_ROWS = [[flat(x, c, z, y) for x in range(4) for c in range(2)] for z in range(4) for y in range(4)]


def move(value, x=0, core=0, z=0, y=0):
    route = [(flat(*a), flat(a[0] + x, a[1] + core, a[2] + z, a[3] + y)) for a in COORDS]
    return lax.ppermute(value, AXES, route)


def swap_x(value):
    route = [(flat(x, c, z, y), flat(x ^ 1, c, z, y)) for x, c, z, y in COORDS]
    return lax.ppermute(value, AXES, route)


def position():
    cls, img = lax.axis_index("cls"), lax.axis_index("img")
    x_lo, z, y = img // 16, (img // 4) % 4, img % 4
    return (cls // 2) * 2 + x_lo, cls % 2, x_lo, z, y


def shifted_pixels(t_ref, rows, dy, dx):
    parts = []
    for row in rows:
        at = jnp.bitwise_and(row + dy, SIDE - 1)
        tiles = [t_ref[t, at, pl.ds(MARGIN + dx, SIDE), :] for t in range(2)]
        parts.append(jnp.concatenate(tiles, axis=1).astype(jnp.bfloat16))
    return jnp.concatenate(parts, axis=0)


def prepare_kernel(*refs):
    sources, (keep_ref, give_ref, out_ref, info_ref) = refs[:4], refs[4:8]
    targets, half_ref, sems = refs[8:12], refs[12], refs[13]
    p_ref, x_ref, rot_ref, log_ref = targets
    _, _, x_lo, _, _ = position()
    copies = [
        pltpu.make_async_copy(sources[k], targets[k], sems.at[k]) for k in range(4)
    ]
    for copy in copies:
        copy.start()
    for copy in copies:
        copy.wait()
    for r in range(ROT):
        half, at = r // HALF_ROT, (r % HALF_ROT) * CLS
        half_ref[half, at : at + CLS, :] = p_ref[r].astype(jnp.float32)
    for half in range(2):
        half_ref[half, USED:ROWS, :] = jnp.zeros((ROWS - USED, LANES), jnp.float32)
    keep_ref[...] = half_ref[x_lo].astype(jnp.bfloat16)
    give_ref[...] = half_ref[1 - x_lo].astype(jnp.bfloat16)
    out_ref[:, 0:PIX] = x_ref[...].astype(jnp.bfloat16)
    rots = rot_ref[...].astype(jnp.float32)
    rots = jnp.concatenate([rots] * (LANES // OWN), axis=1)
    out_ref[:, PIX : PIX + LANES] = jnp.broadcast_to(rots, (OWN, LANES)).astype(jnp.bfloat16)
    diagonal = lax.broadcasted_iota(jnp.int32, (CLS, CLS), 0) == lax.broadcasted_iota(
        jnp.int32, (CLS, CLS), 1
    )
    logs = jnp.sum(jnp.where(diagonal, log_ref[...], 0.0), axis=1, keepdims=True)
    sign = (1 - 2 * x_lo).astype(jnp.float32)
    lane = lax.broadcasted_iota(jnp.int32, (CLS, LANES), 1)
    for r in range(HALF_ROT):
        turn = 2.0 * math.pi * r / ROT
        rows = jnp.where(lane == 1, math.cos(turn) * sign, math.sin(turn) * sign)
        info_ref[r * CLS : (r + 1) * CLS, :] = jnp.where(lane == 0, logs, rows)
    info_ref[USED:ROWS, :] = jnp.full((ROWS - USED, LANES), NEG, jnp.float32)


def turn_kernel(mine, other, t_ref, rot_ref, x_ref):
    x, core, _, _, _ = position()

    def put(value, dx, dc):
        slot = jnp.bitwise_and(x + dx, 3) * 2 + jnp.bitwise_xor(core, dc)
        x_ref[pl.ds(pl.multiple_of(slot * OWN, OWN), OWN), :] = value

    for k, dx in enumerate((0, -1, 1, 2)):
        put(mine[k * OWN : (k + 1) * OWN], dx, 0)
        put(other[k * OWN : (k + 1) * OWN], dx, 1)

    def turn_blocks(step, carry):
        for k in range(4):
            block = 4 * step + k
            lanes = pl.ds(pl.multiple_of(block * LANES, LANES), LANES)
            for t in range(2):
                tile = x_ref[pl.ds(t * LANES, LANES), lanes].astype(jnp.float32).T
                for half in range(2):
                    line = tile[half * SIDE : (half + 1) * SIDE]
                    t_ref[t, 2 * block + half, pl.ds(MARGIN, SIDE), :] = line
                    t_ref[t, 2 * block + half, pl.ds(0, MARGIN), :] = line[SIDE - MARGIN :]
                    t_ref[t, 2 * block + half, pl.ds(MARGIN + SIDE, MARGIN), :] = line[:MARGIN]
        return carry

    lax.fori_loop(0, BLOCKS // 4, turn_blocks, 0)
    lane_group = lax.broadcasted_iota(jnp.int32, (8, LANES), 1) // OWN
    for t in range(2):
        rots = jnp.zeros((8, LANES), jnp.float32)
        for k in range(4):
            start = t * LANES + k * OWN
            mine = x_ref[start : start + 16, PIX : PIX + LANES].astype(jnp.float32)[0:8]
            rots = jnp.where(lane_group == k, mine, rots)
        rot_ref[t] = rots


def add_scores(shift_ref, t_ref, pairs, s):
    _, _, x_lo, z, y = position()
    dy, dx = shift_ref[0, s], shift_ref[1, s]
    acc = jnp.zeros((ROWS, ROW_IMAGES), jnp.float32)
    for ref, at, dz, dyy in pairs:
        base = jnp.bitwise_and(z + dz, 3) * 4 + jnp.bitwise_and(y + dyy, 3)
        j0 = x_lo * 16 + base
        j1 = (1 - x_lo) * 16 + base
        moved = shifted_pixels(t_ref, (2 * j0, 2 * j0 + 1, 2 * j1, 2 * j1 + 1), dy, dx)
        panel = jnp.concatenate([ref[at], ref[at + 1]], axis=1)
        acc = acc + jnp.dot(panel, moved, preferred_element_type=jnp.float32)
    return acc


def squares_of(pairs):
    squares = jnp.zeros((ROWS, LANES), jnp.float32)
    for ref, at, _, _ in pairs:
        for k in range(2):
            value = ref[at + k].astype(jnp.float32)
            squares = squares + value * value
    return squares


def pairs_of(refs, offsets):
    return [
        (ref, 2 * i, dz, dy) for ref, dy in zip(refs, offsets) for i, dz in enumerate(Z_ORDER)
    ]


def first_kernel(shift_ref, t_ref, pc, py1, py3, s_ref, n_ref):
    pairs = pairs_of((pc, py1, py3), (0, -1, 1))
    n_ref[...] = squares_of(pairs)

    def one_shift(s, carry):
        s_ref[s] = add_scores(shift_ref, t_ref, pairs, s)
        return carry

    lax.fori_loop(0, SHIFTS, one_shift, 0, unroll=True)


def last_kernel(shift_ref, t_ref, py2, s_in, n_in, rot_ref, info_ref, e_ref, st_ref):
    gain = SCORE_GAIN / math.sqrt(PIX)
    pairs = pairs_of((py2,), (2,))
    norms = jnp.sum(n_in[...] + squares_of(pairs), axis=1, keepdims=True)
    rots = jnp.concatenate([rot_ref[0], rot_ref[1]], axis=1)
    angle = rots[0:1] * (2.0 * math.pi / ROT)
    info = info_ref[...]
    prior = info[:, 1:2] * jnp.cos(angle) + info[:, 2:3] * jnp.sin(angle)
    bias = info[:, 0:1] - 0.5 * gain * norms + PRIOR_WEIGHT * prior
    is_panel = lax.broadcasted_iota(jnp.int32, (ROWS, 1), 0) < USED
    bias = jnp.where(is_panel, bias, NEG)

    def one_shift(s, peak):
        scores = gain * (s_in[s] + add_scores(shift_ref, t_ref, pairs, s)) + bias
        e_ref[s] = scores
        return jnp.maximum(peak, jnp.max(scores, axis=0, keepdims=True))

    peak = lax.fori_loop(
        0, SHIFTS, one_shift, jnp.full((1, ROW_IMAGES), NEG, jnp.float32), unroll=True
    )

    def one_exp(s, total):
        value = jnp.exp(e_ref[s] - peak)
        e_ref[s] = value
        return total + jnp.sum(value, axis=0, keepdims=True)

    total = lax.fori_loop(
        0, SHIFTS, one_exp, jnp.zeros((1, ROW_IMAGES), jnp.float32), unroll=True
    )
    stats = jnp.concatenate(
        [
            peak[:, :LANES],
            peak[:, LANES:],
            total[:, :LANES],
            total[:, LANES:],
            jnp.zeros((4, LANES), jnp.float32),
        ],
        axis=0,
    )
    for k in range(8):
        st_ref[k] = stats


def sum_kernel(shift_ref, e_ref, st_ref, all_ref, t_ref, out_ref, ev_ref, w_ref):
    x, core, _, _, _ = position()
    stats = [all_ref[k] for k in range(8)]
    peak = stats[0][0:2]
    for k in range(1, 8):
        peak = jnp.maximum(peak, stats[k][0:2])
    total = jnp.zeros((2, LANES), jnp.float32)
    for k in range(8):
        total = total + stats[k][2:4] * jnp.exp(stats[k][0:2] - peak)
    evidence = peak + jnp.log(total)
    slot = x * 2 + core
    mine = jnp.where(slot >= 4, evidence[1:2], evidence[0:1])
    groups = [mine[:, k * OWN : (k + 1) * OWN] for k in range(4)]
    at = jnp.bitwise_and(slot, 3)
    picked = groups[0]
    for k in range(1, 4):
        picked = jnp.where(at == k, groups[k], picked)
    ev_ref[...] = picked
    factor = jnp.exp(st_ref[0][0:2] - peak) / total
    factor = jnp.concatenate([factor[0:1], factor[1:2]], axis=1)

    for s in range(SHIFTS):
        weight = (e_ref[s] * factor).astype(jnp.bfloat16)
        w_ref[s * ROW_IMAGES : (s + 1) * ROW_IMAGES, :] = weight.T

    ones = jnp.ones((16, SHIFTS * ROW_IMAGES), jnp.bfloat16)
    totals = jnp.dot(ones, w_ref[...], preferred_element_type=jnp.float32)[0:1]
    totals = jnp.concatenate([totals, jnp.zeros((1, 2 * LANES - ROWS), jnp.float32)], axis=1)
    pieces = []
    for _ in range(3):
        part = totals.astype(jnp.bfloat16).astype(jnp.float32)
        totals = totals - part
        pieces += [part[:, :LANES], part[:, LANES:]]
    tail = jnp.concatenate(
        [jnp.zeros((6, LANES), jnp.float32)] + pieces + [jnp.zeros((4, LANES), jnp.float32)], axis=0
    ).astype(jnp.bfloat16)
    is_tail = lax.broadcasted_iota(jnp.int32, (16, LANES), 0) >= 6

    def one_block(pair, carry):
        rows = tuple(4 * pair + k for k in range(4))
        moved = jnp.concatenate(
            [
                shifted_pixels(t_ref, rows, shift_ref[0, s], shift_ref[1, s])
                for s in range(SHIFTS)
            ],
            axis=1,
        )
        acc = jnp.dot(moved, w_ref[...], preferred_element_type=jnp.float32)
        turned = acc.astype(jnp.bfloat16).T
        for k in range(2):
            part = turned[:, k * LANES : (k + 1) * LANES]
            out_ref[2 * pair + k, 0 : ROWS - 16, :] = part[: ROWS - 16]
            out_ref[2 * pair + k, ROWS - 16 : ROWS, :] = jnp.where(is_tail, tail, part[ROWS - 16 :])
        return carry

    lax.fori_loop(0, BLOCKS // 2, one_block, 0, unroll=UNROLL)


def finish_kernel(in_ref, out_ref, wt_ref):
    for half in range(2):
        acc = jnp.zeros((ROWS, LANES), jnp.float32)
        for k in range(16):
            acc = acc + in_ref[half * 16 + k].astype(jnp.float32)
        for r in range(HALF_ROT):
            out_ref[half * HALF_ROT + r] = acc[r * CLS : (r + 1) * CLS]
        wide = [
            acc[USED + k : USED + k + 1] + acc[USED + 2 + k : USED + 3 + k]
            + acc[USED + 4 + k : USED + 5 + k]
            for k in range(2)
        ]
        totals = jnp.concatenate(wide, axis=1)
        for r in range(HALF_ROT):
            row = half * HALF_ROT + r
            wt_ref[row : row + 1, :] = totals[:, r * CLS : (r + 1) * CLS]


VMEM = pl.BlockSpec(memory_space=pltpu.VMEM)
SMEM = pl.BlockSpec(memory_space=pltpu.SMEM)
PARAMS = pltpu.CompilerParams(vmem_limit_bytes=40 * 1024 * 1024)


def cost(quarters, megabytes):
    flops = 1000 * quarters
    return pl.CostEstimate(flops=flops, bytes_accessed=1000 * megabytes, transcendentals=0)


def shards(particles, rot_prior, panels, log_prior, shift_table):
    x_lo = lax.axis_index("img") // 16

    keep, give, images, info = pl.pallas_call(
        prepare_kernel,
        out_shape=(jax.ShapeDtypeStruct((ROWS, LANES), jnp.bfloat16),) * 2
        + (
            jax.ShapeDtypeStruct((OWN, PIX + LANES), jnp.bfloat16),
            jax.ShapeDtypeStruct((ROWS, LANES), jnp.float32),
        ),
        in_specs=[pl.BlockSpec(memory_space=pltpu.HBM)] * 4,
        out_specs=(VMEM,) * 4,
        scratch_shapes=[
            pltpu.VMEM((ROT, CLS, LANES), jnp.bfloat16),
            pltpu.VMEM((OWN, PIX), jnp.float32),
            pltpu.VMEM((1, OWN), jnp.int32),
            pltpu.VMEM((1, CLS), jnp.float32),
            pltpu.VMEM((2, ROWS, LANES), jnp.float32),
            pltpu.SemaphoreType.DMA((4,)),
        ],
        compiler_params=pltpu.CompilerParams(vmem_limit_bytes=60 * 1024 * 1024),
        cost_estimate=cost(0, 1),
        name="prepare",
    )(
        jnp.transpose(panels, (1, 0, 2)),
        particles,
        rot_prior.reshape(1, OWN),
        log_prior.reshape(1, CLS),
    )
    got = swap_x(give)
    first = jnp.stack([keep, got])
    z1 = move(first, z=1)
    z3 = move(first, z=-1)
    z2 = move(first, z=2)
    images, _ = lax.optimization_barrier((images, got))
    a1 = move(images, x=1)
    a2 = move(images, x=-1)
    a3 = move(images, x=2)
    column = jnp.concatenate([first, z1, z3, z2], axis=0)
    y1 = move(column, y=1)
    y3 = move(column, y=-1)
    y2 = move(column, y=2)
    mine = jnp.concatenate([images, a1, a2, a3], axis=0)
    mine, y1, y3 = lax.optimization_barrier((mine, y1, y3))
    cc = move(mine, core=1)

    turned, rots = pl.pallas_call(
        turn_kernel,
        out_shape=(
            jax.ShapeDtypeStruct((2, SIDE, SIDE + 2 * MARGIN, LANES), jnp.float32),
            jax.ShapeDtypeStruct((2, 8, LANES), jnp.float32),
        ),
        in_specs=[VMEM] * 2,
        out_specs=(VMEM, VMEM),
        scratch_shapes=[pltpu.VMEM((ROW_IMAGES, PIX + LANES), jnp.bfloat16)],
        compiler_params=PARAMS,
        cost_estimate=cost(0, 8),
        name="turn",
    )(mine, cc)

    shifts = shift_table.T
    score_shape = jax.ShapeDtypeStruct((SHIFTS, ROWS, ROW_IMAGES), jnp.float32)
    norm_shape = jax.ShapeDtypeStruct((ROWS, LANES), jnp.float32)
    scores, norms = pl.pallas_call(
        first_kernel,
        out_shape=(score_shape, norm_shape),
        in_specs=[SMEM] + [VMEM] * 4,
        out_specs=(VMEM, VMEM),
        compiler_params=PARAMS,
        cost_estimate=cost(3, 4),
        name="first",
    )(shifts, turned, column, y1, y3)

    scores, stats = pl.pallas_call(
        last_kernel,
        out_shape=(score_shape, jax.ShapeDtypeStruct((8, 8, LANES), jnp.float32)),
        in_specs=[SMEM] + [VMEM] * 6,
        out_specs=(VMEM, VMEM),
        input_output_aliases={3: 0},
        compiler_params=PARAMS,
        cost_estimate=cost(1, 8),
        name="last",
    )(shifts, turned, y2, scores, norms, rots, info)
    all_stats = lax.all_to_all(stats, AXES, 0, 0, axis_index_groups=X_ROWS)
    blocks, evidence = pl.pallas_call(
        sum_kernel,
        out_shape=(
            jax.ShapeDtypeStruct((BLOCKS, ROWS, LANES), jnp.bfloat16),
            jax.ShapeDtypeStruct((1, OWN), jnp.float32),
        ),
        in_specs=[SMEM] + [VMEM] * 4,
        out_specs=(VMEM, VMEM),
        scratch_shapes=[pltpu.VMEM((SHIFTS * ROW_IMAGES, ROWS), jnp.bfloat16)],
        compiler_params=PARAMS,
        cost_estimate=cost(4, 12),
        name="sums",
    )(shifts, scores, stats, all_stats, turned)
    shares = lax.all_to_all(blocks, "img", 0, 0)
    sums, totals = pl.pallas_call(
        finish_kernel,
        out_shape=(
            jax.ShapeDtypeStruct((ROT, CLS, LANES), jnp.float32),
            jax.ShapeDtypeStruct((ROT, CLS), jnp.float32),
        ),
        in_specs=[VMEM],
        out_specs=(VMEM, VMEM),
        compiler_params=PARAMS,
        name="finish",
    )(shares)
    return jnp.transpose(sums, (1, 0, 2)), totals.T, evidence.reshape(OWN)


def solution(mesh):
    placed = (P(AXES, None), P(AXES), P("cls", None, "img"), P("cls"), P())
    return jax.shard_map(
        shards,
        mesh=mesh,
        in_specs=placed,
        out_specs=(P("cls", None, "img"), P("cls", None), P(AXES)),
        check_vma=False,
    )
```

time: 108 us -> 88.7 us (0.82)
  Pallas kernels: 26.5 us -> 20 us
  waiting for transfers between devices: 19.6 us -> 14 us
  starting transfers between devices: 21.7 us -> 17.5 us
  local copies, waits for them, and re-layouts: 4.71 us -> 0.85 us
  blocking collectives: 31.3 us -> 33.4 us
    ppermute x17 -> x10, waiting for transfers between devices: 19.6 us -> 12.1 us  [move(): return lax.ppermute(value, AXES, route)]
    pallas_call x1, Pallas kernels: 13.8 us -> 9.01 us  [shards(): pl.pallas_call(sum_kernel, out_shape=(jax.ShapeDtypeStruct((BLOCKS, ROWS,...]
    ppermute x17 -> x10, starting transfers between devices: 20.1 us -> 15.9 us  [move(): return lax.ppermute(value, AXES, route)]
    ppermute x1, waiting for transfers between devices: 0.01 us -> 1.86 us  [swap_x(): return lax.ppermute(value, AXES, route)]
    pallas_call x1 -> x4, Pallas kernels: 11.9 us -> 10.1 us  [the longest x1 4.47 us: shards(): pl.pallas_call(first_kernel, out_shape=(score_shape, norm_shape), in_spec...]
    convert_element_type x2 -> x0, other arithmetic: 1.73 us -> none  [the longest x1 1.07 us: shards(): particles.astype(jnp.bfloat16)]
    all_to_all x1, blocking collectives: 7.82 us -> 9.25 us  [shards(): all_stats = lax.all_to_all(stats, AXES, 0, 0, axis_index_groups=X_ROWS)]
    slice x4 -> x0, local copies, waits for them, and re-layouts: 1.38 us -> none  [the longest x1 0.68 us: shards(): yw1 = move(y3[4:], y=-1)]
  transfers between devices with their start and end apart: 18 -> 11, of which waited for: 6 -> 8; matrix products, arithmetic and copies ran while one was open for 5% -> 2% of each run, Pallas kernels for 0% -> 7%
where the time goes in v1:
time: 88.7 us; the launch traced here: 88.4 us
  blocking collectives  33.4 us (38%)
  Pallas kernels  20 us (23%)
  starting transfers between devices  17.5 us (20%)
  waiting for transfers between devices  14 us (16%)
  other arithmetic  1.81 us (2%)
    all_to_all x1, blocking collectives, shards(): shares = lax.all_to_all(blocks, 'img', 0, 0)  24.2 us
    ppermute x10, starting transfers between devices, move(): return lax.ppermute(value, AXES, route)  15.9 us
    ppermute x10, waiting for transfers between devices, move(): return lax.ppermute(value, AXES, route)  12.1 us
    all_to_all x1, blocking collectives, shards(): all_stats = lax.all_to_all(stats, AXES, 0, 0, axis_index_groups=X_ROWS)  9.25 us
    pallas_call x1, Pallas kernels, shards(): pl.pallas_call(sum_kernel, out_shape=(jax.ShapeDtypeStruct((BLOCKS, ROWS,...  9.01 us
    pallas_call x1, Pallas kernels, shards(): pl.pallas_call(first_kernel, out_shape=(score_shape, norm_shape), in_spec...  4.47 us
    pallas_call x1, Pallas kernels, shards(): pl.pallas_call(last_kernel, out_shape=(score_shape, jax.ShapeDtypeStruct(...  2.43 us
    pallas_call x1, Pallas kernels, shards(): pl.pallas_call(prepare_kernel, out_shape=(jax.ShapeDtypeStruct((ROWS, LAN...  1.96 us
  transfers between devices with their start and end apart: 11, of which 8 were waited for; matrix products, arithmetic and copies ran while one was open for 2% of the time, Pallas kernels for 7%

profile of v1, /device:TPU:0, one launch (start us, length us, event | category | flops | bytes accessed | tf_op | source)
XLA Modules:
  0.0 88.4 jit_solution(5148944676220831005)
XLA Ops:
  0.6 2.0 %prepare.1 = (bf16[160,128]{1,0:T(8,128)(2,1)}, bf16[160,128]{1,0:T(8,128)(2,1)}, bf16[32,4224]{1,0:T(8,128)(2,1)}, f32[160,128]{1,0:T(8,128)}) custom-call(bf16[12,25,128]{2,1,0:T(8,128)(2,1)} %bitcast.16, f32[32,4096]{1,0:T(8,128)} %refs_1_.1, s32[1,32]{1,0:T(1,128)} %bitcast.17, f32[1,25]{1,0:T(1,128)} %bitcast.18), custom_call_target="tpu_custom_call" | custom-call | bytes 1000 | tf_op jit(solution)/shard_map/prepare/pallas_call | solution.py:308
  2.6 1.7 %collective-permute-start = (bf16[160,128]{1,0:T(8,128)(2,1)}, bf16[160,128]{1,0:T(8,128)(2,1)S(1)}, u32[]{:S(2)}, u32[]{:S(2)}) collective-permute-start(bf16[160,128]{1,0:T(8,128)(2,1)} %get-tuple-element.22), channel_id=1, source_target_pairs={{0,16},{1,17},{2,18},{3,19},{4,20},{5,21},{6,22},{7,23},{8,24},{9,... | collective-permute-start | bytes 122888 | tf_op jit(solution)/shard_map/ppermute | solution.py:47
  4.3 0.8 constant_dynamic-update-slice_fusion.4
  5.0 1.9 %collective-permute-done = bf16[160,128]{1,0:T(8,128)(2,1)S(1)} collective-permute-done((bf16[160,128]{1,0:T(8,128)(2,1)}, bf16[160,128]{1,0:T(8,128)(2,1)S(1)}, u32[]{:S(2)}, u32[]{:S(2)}) %collective-permute-start) | collective-permute-done | bytes 40992 | tf_op jit(solution)/shard_map/ppermute | solution.py:47
  6.9 0.8 pad_maximum_fusion.1
  7.7 4.0 %collective-permute-start.6 = (bf16[2,160,128]{2,1,0:T(8,128)(2,1)S(1)}, bf16[2,160,128]{2,1,0:T(8,128)(2,1)S(1)}, u32[]{:S(2)}, u32[]{:S(2)}) collective-permute-start(bf16[2,160,128]{2,1,0:T(8,128)(2,1)S(1)} %pad_maximum_fusion.1), channel_id=1, source_target_pairs={{0,8},{1,9},{2,10},{3,11},{4,12},{5,13},{6,14},{7,15},{8,0},{9,1},... | collective-permute-start | bytes 245768 | tf_op jit(solution)/shard_map/ppermute | solution.py:42
  11.7 0.7 collective-permute-start.5
  12.4 1.3 %collective-permute-start.4 = (bf16[2,160,128]{2,1,0:T(8,128)(2,1)S(1)}, bf16[2,160,128]{2,1,0:T(8,128)(2,1)S(1)}, u32[]{:S(2)}, u32[]{:S(2)}) collective-permute-start(bf16[2,160,128]{2,1,0:T(8,128)(2,1)S(1)} %pad_maximum_fusion.1), channel_id=1, source_target_pairs={{0,4},{1,5},{2,6},{3,7},{4,8},{5,9},{6,10},{7,11},{8,12},{9,13},{1... | collective-permute-start | bytes 245768 | tf_op jit(solution)/shard_map/ppermute | solution.py:42
  13.7 3.0 %collective-permute-start.3 = (bf16[32,4224]{1,0:T(8,128)(2,1)}, bf16[32,4224]{1,0:T(8,128)(2,1)S(1)}, u32[]{:S(2)}, u32[]{:S(2)}) collective-permute-start(bf16[32,4224]{1,0:T(8,128)(2,1)} %get-tuple-element.23), channel_id=1, source_target_pairs={{0,64},{1,65},{2,66},{3,67},{4,68},{5,69},{6,70},{7,71},{8,72},{9,... | collective-permute-start | bytes 811016 | tf_op jit(solution)/shard_map/ppermute | solution.py:42
  16.8 1.1 %collective-permute-start.2 = (bf16[32,4224]{1,0:T(8,128)(2,1)}, bf16[32,4224]{1,0:T(8,128)(2,1)S(1)}, u32[]{:S(2)}, u32[]{:S(2)}) collective-permute-start(bf16[32,4224]{1,0:T(8,128)(2,1)} %get-tuple-element.23), channel_id=1, source_target_pairs={{0,80},{1,81},{2,82},{3,83},{4,84},{5,85},{6,86},{7,87},{8,88},{9,... | collective-permute-start | bytes 811016 | tf_op jit(solution)/shard_map/ppermute | solution.py:42
  17.9 0.2 collective-permute-done.4
  18.1 1.5 %collective-permute-start.1 = (bf16[32,4224]{1,0:T(8,128)(2,1)}, bf16[32,4224]{1,0:T(8,128)(2,1)S(1)}, u32[]{:S(2)}, u32[]{:S(2)}) collective-permute-start(bf16[32,4224]{1,0:T(8,128)(2,1)} %get-tuple-element.23), channel_id=1, source_target_pairs={{0,16},{1,17},{2,18},{3,19},{4,20},{5,21},{6,22},{7,23},{8,24},{9,... | collective-permute-start | bytes 811016 | tf_op jit(solution)/shard_map/ppermute | solution.py:42
  19.6 0.0 collective-permute-done.5
  19.6 0.0 collective-permute-done.6
  19.6 0.0 copy-start.1
  19.7 3.1 %collective-permute-start.8 = (bf16[8,160,128]{2,1,0:T(8,128)(2,1)S(1)}, bf16[8,160,128]{2,1,0:T(8,128)(2,1)S(1)}, u32[]{:S(2)}, u32[]{:S(2)}) collective-permute-start(bf16[8,160,128]{2,1,0:T(8,128)(2,1)S(1)} %constant_dynamic-update-slice_fusion.pc), channel_id=1, source_target_pairs={{0,3},{1,0},{2,1},{3,2},{4,7},{5,4},{6,5},{7,6},{8,11},{9,8},{10,9... | collective-permute-start | bytes 983048 | tf_op jit(solution)/shard_map/ppermute | solution.py:42
  22.7 1.0 %collective-permute-done.3 = bf16[32,4224]{1,0:T(8,128)(2,1)S(1)} collective-permute-done((bf16[32,4224]{1,0:T(8,128)(2,1)}, bf16[32,4224]{1,0:T(8,128)(2,1)S(1)}, u32[]{:S(2)}, u32[]{:S(2)}) %collective-permute-start.3) | collective-permute-done | bytes 270368 | tf_op jit(solution)/shard_map/ppermute | solution.py:42
  23.7 3.9 %collective-permute-done.2 = bf16[32,4224]{1,0:T(8,128)(2,1)S(1)} collective-permute-done((bf16[32,4224]{1,0:T(8,128)(2,1)}, bf16[32,4224]{1,0:T(8,128)(2,1)S(1)}, u32[]{:S(2)}, u32[]{:S(2)}) %collective-permute-start.2) | collective-permute-done | bytes 270368 | tf_op jit(solution)/shard_map/ppermute | solution.py:42
  27.6 0.1 collective-permute-done.1
  27.7 1.0 %pad_maximum_fusion.mine = bf16[128,4224]{1,0:T(8,128)(2,1)S(1)} fusion(bf16[32,4224]{1,0:T(8,128)(2,1)S(1)} %collective-permute-done.3, bf16[32,4224]{1,0:T(8,128)(2,1)S(1)} %collective-permute-done.2, bf16[32,4224]{1,0:T(8,128)(2,1)S(1)} %collective-permute-done.1, bf16[32,4224]{1,0:T(8,128)(2,1)} %get-tuple-element.23), kind=kLoop, calls=%fused_computation | loop fusion | flops 4325376 | bytes 2162688 | tf_op jit(solution)/shard_map/concatenate | solution.py:347
  28.7 2.3 %collective-permute-done.7.py1 = bf16[8,160,128]{2,1,0:T(8,128)(2,1)S(1)} collective-permute-done((bf16[8,160,128]{2,1,0:T(8,128)(2,1)S(1)}, bf16[8,160,128]{2,1,0:T(8,128)(2,1)S(1)}, u32[]{:S(2)}, u32[]{:S(2)}) %collective-permute-start.7) | collective-permute-done | bytes 327712 | tf_op jit(solution)/shard_map/ppermute | solution.py:42
  31.0 1.1 %collective-permute-start.10 = (bf16[8,160,128]{2,1,0:T(8,128)(2,1)S(1)}, bf16[8,160,128]{2,1,0:T(8,128)(2,1)S(1)}, u32[]{:S(2)}, u32[]{:S(2)}) collective-permute-start(bf16[8,160,128]{2,1,0:T(8,128)(2,1)S(1)} %constant_dynamic-update-slice_fusion.pc), channel_id=1, source_target_pairs={{0,2},{1,3},{2,0},{3,1},{4,6},{5,7},{6,4},{7,5},{8,10},{9,11},{10,... | collective-permute-start | bytes 983048 | tf_op jit(solution)/shard_map/ppermute | solution.py:42
  32.1 1.6 %collective-permute-done.9.other = bf16[128,4224]{1,0:T(8,128)(2,1)S(1)} collective-permute-done((bf16[128,4224]{1,0:T(8,128)(2,1)S(1)}, bf16[128,4224]{1,0:T(8,128)(2,1)S(1)}, u32[]{:S(2)}, u32[]{:S(2)}) %collective-permute-start.9) | collective-permute-done | bytes 1081376 | tf_op jit(solution)/shard_map/ppermute | solution.py:42
  33.7 1.3 %turn.1 = (f32[2,64,80,128]{3,2,1,0:T(8,128)S(1)}, f32[2,8,128]{2,1,0:T(8,128)S(1)}) custom-call(bf16[128,4224]{1,0:T(8,128)(2,1)S(1)} %pad_maximum_fusion.mine, bf16[128,4224]{1,0:T(8,128)(2,1)S(1)} %collective-permute-done.9.other), custom_call_target="tpu_custom_call" | custom-call | bytes 8000 | tf_op jit(solution)/shard_map/turn/pallas_call | solution.py:351
  35.0 0.0 copy-start
  35.1 4.5 %first.1 = (f32[11,160,256]{2,1,0:T(8,128)S(1)}, f32[160,128]{1,0:T(8,128)S(1)}) custom-call(s32[2,11]{1,0:T(2,128)S(1)} %bitcast.11, f32[2,64,80,128]{3,2,1,0:T(8,128)S(1)} %get-tuple-element.26.t_ref, bf16[8,160,128]{2,1,0:T(8,128)(2,1)S(1)} %constant_dynamic-update-slice_fusion.pc, bf16[8,160,128]{2,1,0:T(8,128)(2,1)S(1)} %collective-permute-done.7.py1, ...), custom_call_target="tpu_custom_call" | custom-call | flops 3000 | bytes 4000 | tf_op jit(solution)/shard_map/first/pallas_call | solution.py:368
  39.5 3.1 %collective-permute-done.10.py2 = bf16[8,160,128]{2,1,0:T(8,128)(2,1)S(1)} collective-permute-done((bf16[8,160,128]{2,1,0:T(8,128)(2,1)S(1)}, bf16[8,160,128]{2,1,0:T(8,128)(2,1)S(1)}, u32[]{:S(2)}, u32[]{:S(2)}) %collective-permute-start.10) | collective-permute-done | bytes 327712 | tf_op jit(solution)/shard_map/ppermute | solution.py:42
  42.7 2.4 %last.1 = (f32[11,160,256]{2,1,0:T(8,128)S(1)}, f32[8,8,128]{2,1,0:T(8,128)S(1)}) custom-call(s32[2,11]{1,0:T(2,128)S(1)} %bitcast.12, f32[2,64,80,128]{3,2,1,0:T(8,128)S(1)} %get-tuple-element.26.t_ref, bf16[8,160,128]{2,1,0:T(8,128)(2,1)S(1)} %collective-permute-done.10.py2, ...), custom_call_target="tpu_custom_call", output_to_operand_aliasing={{0}: (3, {})} | custom-call | flops 1000 | bytes 8000 | tf_op jit(solution)/shard_map/last/pallas_call | solution.py:378
  45.1 9.2 %all_to_all.10.all_ref = f32[8,8,128]{2,1,0:T(8,128)S(1)} all-to-all(f32[8,8,128]{2,1,0:T(8,128)S(1)} %get-tuple-element.34.st_ref), channel_id=1, replica_groups={{0,32,16,48,64,96,80,112},{1,33,17,49,65,97,81,113},{2,34,18,50,66,98,8..., dimensions={0} | all-to-all | bytes 65536 | tf_op jit(solution)/shard_map/all_to_all | solution.py:388
  54.3 9.0 %sums.1 = (bf16[32,160,128]{2,1,0:T(8,128)(2,1)S(1)}, f32[1,32]{1,0:T(1,128)}) custom-call(s32[2,11]{1,0:T(2,128)S(1)} %bitcast.13, f32[11,160,256]{2,1,0:T(8,128)S(1)} %get-tuple-element.33.e_ref, f32[8,8,128]{2,1,0:T(8,128)S(1)} %get-tuple-element.34.st_ref, f32[8,8,128]{2,1,0:T(8,128)S(1)} %all_to_all.10.all_ref, ...), custom_call_target="tpu_custom_call" | custom-call | flops 4000 | bytes 12000 | tf_op jit(solution)/shard_map/sums/pallas_call | solution.py:389
  63.4 24.2 %all_to_all.11.in_ref = bf16[32,160,128]{2,1,0:T(8,128)(2,1)S(1)} all-to-all(bf16[32,160,128]{2,1,0:T(8,128)(2,1)S(1)} %get-tuple-element.35), channel_id=1, replica_groups=mesh['cls'=4,'img'=32] {'img'}, dimensions={0} | all-to-all | bytes 2621440 | tf_op jit(solution)/shard_map/all_to_all | solution.py:402
  87.5 0.9 finish.1
  (9 shorter events, 0.1 us)
Async XLA Ops:
  2.6 4.3 %collective-permute-start = (bf16[160,128]{1,0:T(8,128)(2,1)}, bf16[160,128]{1,0:T(8,128)(2,1)S(1)}, u32[]{:S(2)}, u32[]{:S(2)}) collective-permute-start(bf16[160,128]{1,0:T(8,128)(2,1)} %get-tuple-element.22), channel_id=1, source_target_pairs={{0,16},{1,17},{2,18},{3,19},{4,20},{5,21},{6,22},{7,23},{8,24},{9,... | collective-permute-start | bytes 122888 | tf_op jit(solution)/shard_map/ppermute | solution.py:47
  7.7 11.9 %collective-permute-start.6 = (bf16[2,160,128]{2,1,0:T(8,128)(2,1)S(1)}, bf16[2,160,128]{2,1,0:T(8,128)(2,1)S(1)}, u32[]{:S(2)}, u32[]{:S(2)}) collective-permute-start(bf16[2,160,128]{2,1,0:T(8,128)(2,1)S(1)} %pad_maximum_fusion.1), channel_id=1, source_target_pairs={{0,8},{1,9},{2,10},{3,11},{4,12},{5,13},{6,14},{7,15},{8,0},{9,1},... | collective-permute-start | bytes 245768 | tf_op jit(solution)/shard_map/ppermute | solution.py:42
  11.7 7.9 %collective-permute-start.5 = (bf16[2,160,128]{2,1,0:T(8,128)(2,1)S(1)}, bf16[2,160,128]{2,1,0:T(8,128)(2,1)S(1)}, u32[]{:S(2)}, u32[]{:S(2)}) collective-permute-start(bf16[2,160,128]{2,1,0:T(8,128)(2,1)S(1)} %pad_maximum_fusion.1), channel_id=1, source_target_pairs={{0,12},{1,13},{2,14},{3,15},{4,0},{5,1},{6,2},{7,3},{8,4},{9,5},{1... | collective-permute-start | bytes 245768 | tf_op jit(solution)/shard_map/ppermute | solution.py:42
  12.4 5.7 %collective-permute-start.4 = (bf16[2,160,128]{2,1,0:T(8,128)(2,1)S(1)}, bf16[2,160,128]{2,1,0:T(8,128)(2,1)S(1)}, u32[]{:S(2)}, u32[]{:S(2)}) collective-permute-start(bf16[2,160,128]{2,1,0:T(8,128)(2,1)S(1)} %pad_maximum_fusion.1), channel_id=1, source_target_pairs={{0,4},{1,5},{2,6},{3,7},{4,8},{5,9},{6,10},{7,11},{8,12},{9,13},{1... | collective-permute-start | bytes 245768 | tf_op jit(solution)/shard_map/ppermute | solution.py:42
  13.7 10.0 %collective-permute-start.3 = (bf16[32,4224]{1,0:T(8,128)(2,1)}, bf16[32,4224]{1,0:T(8,128)(2,1)S(1)}, u32[]{:S(2)}, u32[]{:S(2)}) collective-permute-start(bf16[32,4224]{1,0:T(8,128)(2,1)} %get-tuple-element.23), channel_id=1, source_target_pairs={{0,64},{1,65},{2,66},{3,67},{4,68},{5,69},{6,70},{7,71},{8,72},{9,... | collective-permute-start | bytes 811016 | tf_op jit(solution)/shard_map/ppermute | solution.py:42
  16.8 10.8 %collective-permute-start.2 = (bf16[32,4224]{1,0:T(8,128)(2,1)}, bf16[32,4224]{1,0:T(8,128)(2,1)S(1)}, u32[]{:S(2)}, u32[]{:S(2)}) collective-permute-start(bf16[32,4224]{1,0:T(8,128)(2,1)} %get-tuple-element.23), channel_id=1, source_target_pairs={{0,80},{1,81},{2,82},{3,83},{4,84},{5,85},{6,86},{7,87},{8,88},{9,... | collective-permute-start | bytes 811016 | tf_op jit(solution)/shard_map/ppermute | solution.py:42
  18.1 9.6 %collective-permute-start.1 = (bf16[32,4224]{1,0:T(8,128)(2,1)}, bf16[32,4224]{1,0:T(8,128)(2,1)S(1)}, u32[]{:S(2)}, u32[]{:S(2)}) collective-permute-start(bf16[32,4224]{1,0:T(8,128)(2,1)} %get-tuple-element.23), channel_id=1, source_target_pairs={{0,16},{1,17},{2,18},{3,19},{4,20},{5,21},{6,22},{7,23},{8,24},{9,... | collective-permute-start | bytes 811016 | tf_op jit(solution)/shard_map/ppermute | solution.py:42
  19.6 15.4 %copy-start.1 = (s32[11,2]{0,1:T(2,128)S(1)}, s32[11,2]{0,1:T(2,128)}, u32[]{:S(2)}) copy-start(s32[11,2]{0,1:T(2,128)} %param.9) | copy-start | bytes 268
  19.7 9.1 %collective-permute-start.8 = (bf16[8,160,128]{2,1,0:T(8,128)(2,1)S(1)}, bf16[8,160,128]{2,1,0:T(8,128)(2,1)S(1)}, u32[]{:S(2)}, u32[]{:S(2)}) collective-permute-start(bf16[8,160,128]{2,1,0:T(8,128)(2,1)S(1)} %constant_dynamic-update-slice_fusion.pc), channel_id=1, source_target_pairs={{0,3},{1,0},{2,1},{3,2},{4,7},{5,4},{6,5},{7,6},{8,11},{9,8},{10,9... | collective-permute-start | bytes 983048 | tf_op jit(solution)/shard_map/ppermute | solution.py:42
  22.7 8.3 %collective-permute-start.7 = (bf16[8,160,128]{2,1,0:T(8,128)(2,1)S(1)}, bf16[8,160,128]{2,1,0:T(8,128)(2,1)S(1)}, u32[]{:S(2)}, u32[]{:S(2)}) collective-permute-start(bf16[8,160,128]{2,1,0:T(8,128)(2,1)S(1)} %constant_dynamic-update-slice_fusion.pc), channel_id=1, source_target_pairs={{0,1},{1,2},{2,3},{3,0},{4,5},{5,6},{6,7},{7,4},{8,9},{9,10},{10,1... | collective-permute-start | bytes 983048 | tf_op jit(solution)/shard_map/ppermute | solution.py:42
  31.0 2.7 %collective-permute-start.9 = (bf16[128,4224]{1,0:T(8,128)(2,1)S(1)}, bf16[128,4224]{1,0:T(8,128)(2,1)S(1)}, u32[]{:S(2)}, u32[]{:S(2)}) collective-permute-start(bf16[128,4224]{1,0:T(8,128)(2,1)S(1)} %pad_maximum_fusion.mine), channel_id=1, source_target_pairs={{0,32},{1,33},{2,34},{3,35},{4,36},{5,37},{6,38},{7,39},{8,40},{9,... | collective-permute-start | bytes 3244040 | tf_op jit(solution)/shard_map/ppermute | solution.py:42
  31.0 11.6 %collective-permute-start.10 = (bf16[8,160,128]{2,1,0:T(8,128)(2,1)S(1)}, bf16[8,160,128]{2,1,0:T(8,128)(2,1)S(1)}, u32[]{:S(2)}, u32[]{:S(2)}) collective-permute-start(bf16[8,160,128]{2,1,0:T(8,128)(2,1)S(1)} %constant_dynamic-update-slice_fusion.pc), channel_id=1, source_target_pairs={{0,2},{1,3},{2,0},{3,1},{4,6},{5,7},{6,4},{7,5},{8,10},{9,11},{10,... | collective-permute-start | bytes 983048 | tf_op jit(solution)/shard_map/ppermute | solution.py:42
  35.0 7.6 %copy-start = (f32[160,128]{1,0:T(8,128)S(1)}, f32[160,128]{1,0:T(8,128)}, u32[]{:S(2)}) copy-start(f32[160,128]{1,0:T(8,128)} %get-tuple-element.32.info_ref) | copy-start | bytes 245764

commit v2 on v1

--- a/solution.py
+++ b/solution.py
@@ -25,7 +25,6 @@
 MARGIN = 8
 NEG = -1.0e30
 UNROLL = 4
-Z_ORDER = (0, -1, 1, 2)
 
 
 def flat(x, core, z, y):
@@ -34,16 +33,12 @@
 
 
 COORDS = [(x, c, z, y) for x in range(4) for c in range(2) for z in range(4) for y in range(4)]
+XZ_GROUPS = [[x * 16 + z * 4 + y for x in range(2) for z in range(4)] for y in range(4)]
 X_ROWS = [[flat(x, c, z, y) for x in range(4) for c in range(2)] for z in range(4) for y in range(4)]
 
 
 def move(value, x=0, core=0, z=0, y=0):
     route = [(flat(*a), flat(a[0] + x, a[1] + core, a[2] + z, a[3] + y)) for a in COORDS]
-    return lax.ppermute(value, AXES, route)
-
-
-def swap_x(value):
-    route = [(flat(x, c, z, y), flat(x ^ 1, c, z, y)) for x, c, z, y in COORDS]
     return lax.ppermute(value, AXES, route)
 
 
@@ -63,8 +58,8 @@
 
 
 def prepare_kernel(*refs):
-    sources, (keep_ref, give_ref, out_ref, info_ref) = refs[:4], refs[4:8]
-    targets, half_ref, sems = refs[8:12], refs[12], refs[13]
+    sources, (send_ref, out_ref, info_ref) = refs[:4], refs[4:7]
+    targets, half_ref, sems = refs[7:11], refs[11], refs[12]
     p_ref, x_ref, rot_ref, log_ref = targets
     _, _, x_lo, _, _ = position()
     copies = [
@@ -79,8 +74,10 @@
         half_ref[half, at : at + CLS, :] = p_ref[r].astype(jnp.float32)
     for half in range(2):
         half_ref[half, USED:ROWS, :] = jnp.zeros((ROWS - USED, LANES), jnp.float32)
-    keep_ref[...] = half_ref[x_lo].astype(jnp.bfloat16)
-    give_ref[...] = half_ref[1 - x_lo].astype(jnp.bfloat16)
+    for half in range(2):
+        value = half_ref[half].astype(jnp.bfloat16)
+        for k in range(4):
+            send_ref[4 * half + k] = value
     out_ref[:, 0:PIX] = x_ref[...].astype(jnp.bfloat16)
     rots = rot_ref[...].astype(jnp.float32)
     rots = jnp.concatenate([rots] * (LANES // OWN), axis=1)
@@ -134,36 +131,37 @@
 
 
 def add_scores(shift_ref, t_ref, pairs, s):
-    _, _, x_lo, z, y = position()
+    y = position()[4]
     dy, dx = shift_ref[0, s], shift_ref[1, s]
     acc = jnp.zeros((ROWS, ROW_IMAGES), jnp.float32)
-    for ref, at, dz, dyy in pairs:
-        base = jnp.bitwise_and(z + dz, 3) * 4 + jnp.bitwise_and(y + dyy, 3)
-        j0 = x_lo * 16 + base
-        j1 = (1 - x_lo) * 16 + base
+    for low, high, z, dyy in pairs:
+        j0 = z * 4 + jnp.bitwise_and(y + dyy, 3)
+        j1 = j0 + 16
         moved = shifted_pixels(t_ref, (2 * j0, 2 * j0 + 1, 2 * j1, 2 * j1 + 1), dy, dx)
-        panel = jnp.concatenate([ref[at], ref[at + 1]], axis=1)
+        panel = jnp.concatenate([low[z], high[z]], axis=1)
         acc = acc + jnp.dot(panel, moved, preferred_element_type=jnp.float32)
     return acc
 
 
 def squares_of(pairs):
     squares = jnp.zeros((ROWS, LANES), jnp.float32)
-    for ref, at, _, _ in pairs:
-        for k in range(2):
-            value = ref[at + k].astype(jnp.float32)
+    for low, high, z, _ in pairs:
+        for ref in (low, high):
+            value = ref[z].astype(jnp.float32)
             squares = squares + value * value
     return squares
 
 
 def pairs_of(refs, offsets):
-    return [
-        (ref, 2 * i, dz, dy) for ref, dy in zip(refs, offsets) for i, dz in enumerate(Z_ORDER)
-    ]
+    return [(*ref, z, dy) for ref, dy in zip(refs, offsets) for z in range(4)]
+
+
+def halves(ref):
+    return ref.at[0:4], ref.at[4:8]
 
 
 def first_kernel(shift_ref, t_ref, pc, py1, py3, s_ref, n_ref):
-    pairs = pairs_of((pc, py1, py3), (0, -1, 1))
+    pairs = pairs_of((halves(pc), halves(py1), halves(py3)), (0, -1, 1))
     n_ref[...] = squares_of(pairs)
 
     def one_shift(s, carry):
@@ -173,9 +171,9 @@
     lax.fori_loop(0, SHIFTS, one_shift, 0, unroll=True)
 
 
-def last_kernel(shift_ref, t_ref, py2, s_in, n_in, rot_ref, info_ref, e_ref, st_ref):
+def last_kernel(shift_ref, t_ref, pw0, pw1, s_in, n_in, rot_ref, info_ref, e_ref, st_ref):
     gain = SCORE_GAIN / math.sqrt(PIX)
-    pairs = pairs_of((py2,), (2,))
+    pairs = pairs_of(((pw0, pw1),), (2,))
     norms = jnp.sum(n_in[...] + squares_of(pairs), axis=1, keepdims=True)
     rots = jnp.concatenate([rot_ref[0], rot_ref[1]], axis=1)
     angle = rots[0:1] * (2.0 * math.pi / ROT)
@@ -303,17 +301,15 @@
 
 
 def shards(particles, rot_prior, panels, log_prior, shift_table):
-    x_lo = lax.axis_index("img") // 16
-
-    keep, give, images, info = pl.pallas_call(
+    spread, images, info = pl.pallas_call(
         prepare_kernel,
-        out_shape=(jax.ShapeDtypeStruct((ROWS, LANES), jnp.bfloat16),) * 2
-        + (
+        out_shape=(
+            jax.ShapeDtypeStruct((8, ROWS, LANES), jnp.bfloat16),
             jax.ShapeDtypeStruct((OWN, PIX + LANES), jnp.bfloat16),
             jax.ShapeDtypeStruct((ROWS, LANES), jnp.float32),
         ),
         in_specs=[pl.BlockSpec(memory_space=pltpu.HBM)] * 4,
-        out_specs=(VMEM,) * 4,
+        out_specs=(VMEM,) * 3,
         scratch_shapes=[
             pltpu.VMEM((ROT, CLS, LANES), jnp.bfloat16),
             pltpu.VMEM((OWN, PIX), jnp.float32),
@@ -331,22 +327,17 @@
         rot_prior.reshape(1, OWN),
         log_prior.reshape(1, CLS),
     )
-    got = swap_x(give)
-    first = jnp.stack([keep, got])
-    z1 = move(first, z=1)
-    z3 = move(first, z=-1)
-    z2 = move(first, z=2)
-    images, _ = lax.optimization_barrier((images, got))
     a1 = move(images, x=1)
     a2 = move(images, x=-1)
     a3 = move(images, x=2)
-    column = jnp.concatenate([first, z1, z3, z2], axis=0)
+    column = lax.all_to_all(spread, "img", 0, 0, axis_index_groups=XZ_GROUPS)
     y1 = move(column, y=1)
     y3 = move(column, y=-1)
-    y2 = move(column, y=2)
     mine = jnp.concatenate([images, a1, a2, a3], axis=0)
     mine, y1, y3 = lax.optimization_barrier((mine, y1, y3))
     cc = move(mine, core=1)
+    yw0 = move(y1[:4], y=1)
+    yw1 = move(y3[4:], y=-1)
 
     turned, rots = pl.pallas_call(
         turn_kernel,
@@ -378,13 +369,13 @@
     scores, stats = pl.pallas_call(
         last_kernel,
         out_shape=(score_shape, jax.ShapeDtypeStruct((8, 8, LANES), jnp.float32)),
-        in_specs=[SMEM] + [VMEM] * 6,
+        in_specs=[SMEM] + [VMEM] * 7,
         out_specs=(VMEM, VMEM),
-        input_output_aliases={3: 0},
+        input_output_aliases={4: 0},
         compiler_params=PARAMS,
         cost_estimate=cost(1, 8),
         name="last",
-    )(shifts, turned, y2, scores, norms, rots, info)
+    )(shifts, turned, yw0, yw1, scores, norms, rots, info)
     all_stats = lax.all_to_all(stats, AXES, 0, 0, axis_index_groups=X_ROWS)
     blocks, evidence = pl.pallas_call(
         sum_kernel,

time: 88.7 us -> 85.9 us (0.968)
  waiting for transfers between devices: 14 us -> 12.6 us
  blocking collectives: 33.4 us -> 34.4 us
  starting transfers between devices: 17.5 us -> 16.6 us
    all_to_all x0 -> x1, starting transfers between devices: none -> 6.34 us  [shards(): column = lax.all_to_all(spread, 'img', 0, 0, axis_index_groups=XZ_GROUPS)]
    ppermute x10 -> x8, starting transfers between devices: 15.9 us -> 10.3 us  [move(): return lax.ppermute(value, AXES, route)]
    all_to_all x0 -> x1, waiting for transfers between devices: none -> 3.8 us  [shards(): column = lax.all_to_all(spread, 'img', 0, 0, axis_index_groups=XZ_GROUPS)]
    ppermute x10 -> x8, waiting for transfers between devices: 12.1 us -> 8.82 us  [move(): return lax.ppermute(value, AXES, route)]
    ppermute x1 -> x0, waiting for transfers between devices: 1.86 us -> none  [swap_x(): return lax.ppermute(value, AXES, route)]
    ppermute x1 -> x0, starting transfers between devices: 1.65 us -> none  [swap_x(): return lax.ppermute(value, AXES, route)]
    all_to_all x1, blocking collectives: 24.2 us -> 25.8 us  [shards(): shares = lax.all_to_all(blocks, 'img', 0, 0)]
  transfers between devices with their start and end apart: 11 -> 9, of which waited for: 8 -> 7; matrix products, arithmetic and copies ran while one was open for 2% -> 1% of each run, Pallas kernels for 7% -> 7%
where the time goes in v2:
time: 85.9 us; the launch traced here: 85.7 us
  blocking collectives  34.4 us (40%)
  Pallas kernels  20.2 us (24%)
  starting transfers between devices  16.6 us (19%)
  waiting for transfers between devices  12.6 us (15%)
  other arithmetic  1.03 us (1%)
    all_to_all x1, blocking collectives, shards(): shares = lax.all_to_all(blocks, 'img', 0, 0)  25.8 us
    ppermute x8, starting transfers between devices, move(): return lax.ppermute(value, AXES, route)  10.3 us
    pallas_call x1, Pallas kernels, shards(): pl.pallas_call(sum_kernel, out_shape=(jax.ShapeDtypeStruct((BLOCKS, ROWS,...  9.02 us
    ppermute x8, waiting for transfers between devices, move(): return lax.ppermute(value, AXES, route)  8.82 us
    all_to_all x1, blocking collectives, shards(): all_stats = lax.all_to_all(stats, AXES, 0, 0, axis_index_groups=X_ROWS)  8.6 us
    all_to_all x1, starting transfers between devices, shards(): column = lax.all_to_all(spread, 'img', 0, 0, axis_index_groups=XZ_GROUPS)  6.34 us
    pallas_call x1, Pallas kernels, shards(): pl.pallas_call(first_kernel, out_shape=(score_shape, norm_shape), in_spec...  4.6 us
    all_to_all x1, waiting for transfers between devices, shards(): column = lax.all_to_all(spread, 'img', 0, 0, axis_index_groups=XZ_GROUPS)  3.8 us
  transfers between devices with their start and end apart: 9, of which 7 were waited for; matrix products, arithmetic and copies ran while one was open for 1% of the time, Pallas kernels for 7%

profile of v2, /device:TPU:0, one launch (start us, length us, event | category | flops | bytes accessed | tf_op | source)
XLA Modules:
  0.0 85.7 jit_solution(5490895997135719716)
XLA Ops:
  0.6 2.0 %prepare.1 = (bf16[8,160,128]{2,1,0:T(8,128)(2,1)}, bf16[32,4224]{1,0:T(8,128)(2,1)}, f32[160,128]{1,0:T(8,128)}) custom-call(bf16[12,25,128]{2,1,0:T(8,128)(2,1)} %bitcast.10, f32[32,4096]{1,0:T(8,128)} %refs_1_.1, s32[1,32]{1,0:T(1,128)} %bitcast.11, f32[1,25]{1,0:T(1,128)} %bitcast.12), custom_call_target="tpu_custom_call" | custom-call | bytes 1000 | tf_op jit(solution)/shard_map/prepare/pallas_call | solution.py:304
  2.7 6.3 %all-to-all-start = ((bf16[8,160,128]{2,1,0:T(8,128)(2,1)}), bf16[8,160,128]{2,1,0:T(8,128)(2,1)S(1)}, u32[]{:S(2)}, u32[]{:S(2)}) async-start(bf16[8,160,128]{2,1,0:T(8,128)(2,1)} %get-tuple-element.20), calls=%async_computation | async-start | bytes 655360 | tf_op jit(solution)/shard_map/all_to_all | solution.py:333
  9.0 2.7 %collective-permute-start.2 = (bf16[32,4224]{1,0:T(8,128)(2,1)}, bf16[32,4224]{1,0:T(8,128)(2,1)S(1)}, u32[]{:S(2)}, u32[]{:S(2)}) collective-permute-start(bf16[32,4224]{1,0:T(8,128)(2,1)} %get-tuple-element.19), channel_id=1, source_target_pairs={{0,64},{1,65},{2,66},{3,67},{4,68},{5,69},{6,70},{7,71},{8,72},{9,... | collective-permute-start | bytes 811016 | tf_op jit(solution)/shard_map/ppermute | solution.py:42
  11.7 2.0 %collective-permute-start.1 = (bf16[32,4224]{1,0:T(8,128)(2,1)}, bf16[32,4224]{1,0:T(8,128)(2,1)S(1)}, u32[]{:S(2)}, u32[]{:S(2)}) collective-permute-start(bf16[32,4224]{1,0:T(8,128)(2,1)} %get-tuple-element.19), channel_id=1, source_target_pairs={{0,80},{1,81},{2,82},{3,83},{4,84},{5,85},{6,86},{7,87},{8,88},{9,... | collective-permute-start | bytes 811016 | tf_op jit(solution)/shard_map/ppermute | solution.py:42
  13.7 0.1 collective-permute-start
  13.8 3.8 %all-to-all-done.pc = bf16[8,160,128]{2,1,0:T(8,128)(2,1)S(1)} async-done(((bf16[8,160,128]{2,1,0:T(8,128)(2,1)}), bf16[8,160,128]{2,1,0:T(8,128)(2,1)S(1)}, u32[]{:S(2)}, u32[]{:S(2)}) %all-to-all-start) | async-done | bytes 327712 | tf_op jit(solution)/shard_map/all_to_all | solution.py:333
  17.6 3.0 %collective-permute-start.4 = (bf16[8,160,128]{2,1,0:T(8,128)(2,1)S(1)}, bf16[8,160,128]{2,1,0:T(8,128)(2,1)S(1)}, u32[]{:S(2)}, u32[]{:S(2)}) collective-permute-start(bf16[8,160,128]{2,1,0:T(8,128)(2,1)S(1)} %all-to-all-done.pc), channel_id=1, source_target_pairs={{0,3},{1,0},{2,1},{3,2},{4,7},{5,4},{6,5},{7,6},{8,11},{9,8},{10,9... | collective-permute-start | bytes 983048 | tf_op jit(solution)/shard_map/ppermute | solution.py:42
  20.6 0.0 collective-permute-start.3
  20.6 2.3 %collective-permute-done.2 = bf16[32,4224]{1,0:T(8,128)(2,1)S(1)} collective-permute-done((bf16[32,4224]{1,0:T(8,128)(2,1)}, bf16[32,4224]{1,0:T(8,128)(2,1)S(1)}, u32[]{:S(2)}, u32[]{:S(2)}) %collective-permute-start.2) | collective-permute-done | bytes 270368 | tf_op jit(solution)/shard_map/ppermute | solution.py:42
  22.8 3.7 %collective-permute-done.1 = bf16[32,4224]{1,0:T(8,128)(2,1)S(1)} collective-permute-done((bf16[32,4224]{1,0:T(8,128)(2,1)}, bf16[32,4224]{1,0:T(8,128)(2,1)S(1)}, u32[]{:S(2)}, u32[]{:S(2)}) %collective-permute-start.1) | collective-permute-done | bytes 270368 | tf_op jit(solution)/shard_map/ppermute | solution.py:42
  26.5 0.7 collective-permute-done
  27.2 1.0 %pad_maximum_fusion.mine = bf16[128,4224]{1,0:T(8,128)(2,1)S(1)} fusion(bf16[32,4224]{1,0:T(8,128)(2,1)S(1)} %collective-permute-done.2, bf16[32,4224]{1,0:T(8,128)(2,1)S(1)} %collective-permute-done.1, bf16[32,4224]{1,0:T(8,128)(2,1)S(1)} %collective-permute-done, bf16[32,4224]{1,0:T(8,128)(2,1)} %get-tuple-element.19), kind=kLoop, calls=%fused_computation | loop fusion | flops 4325376 | bytes 2162688 | tf_op jit(solution)/shard_map/concatenate | solution.py:336
  28.2 0.0 copy-start.1
  28.2 0.0 collective-permute-done.4.py3
  28.2 0.7 collective-permute-done.3.py1
  28.9 0.0 collective-permute-start.5
  28.9 2.5 %collective-permute-start.7 = (bf16[4,160,128]{2,1,0:T(8,128)(2,1)S(1)}, bf16[4,160,128]{2,1,0:T(8,128)(2,1)S(1)}, u32[]{:S(2)}, u32[]{:S(2)}) collective-permute-start(bf16[4,160,128]{2,1,0:T(8,128)(2,1)S(1)} %slice.7), channel_id=1, source_target_pairs={{0,3},{1,0},{2,1},{3,2},{4,7},{5,4},{6,5},{7,6},{8,11},{9,8},{10,9... | collective-permute-start | bytes 491528 | tf_op jit(solution)/shard_map/ppermute | solution.py:42
  31.4 0.0 collective-permute-start.6
  31.4 0.1 collective-permute-done.5.other
  31.6 1.3 %turn.1 = (f32[2,64,80,128]{3,2,1,0:T(8,128)S(1)}, f32[2,8,128]{2,1,0:T(8,128)S(1)}) custom-call(bf16[128,4224]{1,0:T(8,128)(2,1)S(1)} %pad_maximum_fusion.mine, bf16[128,4224]{1,0:T(8,128)(2,1)S(1)} %collective-permute-done.5.other), custom_call_target="tpu_custom_call" | custom-call | bytes 8000 | tf_op jit(solution)/shard_map/turn/pallas_call | solution.py:342
  32.9 0.0 copy-done.1
  32.9 0.0 copy-start
  32.9 4.6 %first.1 = (f32[11,160,256]{2,1,0:T(8,128)S(1)}, f32[160,128]{1,0:T(8,128)S(1)}) custom-call(s32[2,11]{1,0:T(2,128)S(1)} %bitcast.7, f32[2,64,80,128]{3,2,1,0:T(8,128)S(1)} %get-tuple-element.22.t_ref, bf16[8,160,128]{2,1,0:T(8,128)(2,1)S(1)} %all-to-all-done.pc, bf16[8,160,128]{2,1,0:T(8,128)(2,1)S(1)} %collective-permute-done.3.py1, ...), custom_call_target="tpu_custom_call" | custom-call | flops 3000 | bytes 4000 | tf_op jit(solution)/shard_map/first/pallas_call | solution.py:359
  37.5 0.0 collective-permute-done.7.pw1
  37.5 1.5 %collective-permute-done.6.pw0 = bf16[4,160,128]{2,1,0:T(8,128)(2,1)S(1)} collective-permute-done((bf16[4,160,128]{2,1,0:T(8,128)(2,1)S(1)}, bf16[4,160,128]{2,1,0:T(8,128)(2,1)S(1)}, u32[]{:S(2)}, u32[]{:S(2)}) %collective-permute-start.6) | collective-permute-done | bytes 163872 | tf_op jit(solution)/shard_map/ppermute | solution.py:42
  39.0 0.0 copy-done
  39.0 2.4 %last.1 = (f32[11,160,256]{2,1,0:T(8,128)S(1)}, f32[8,8,128]{2,1,0:T(8,128)S(1)}) custom-call(s32[2,11]{1,0:T(2,128)S(1)} %bitcast.8, f32[2,64,80,128]{3,2,1,0:T(8,128)S(1)} %get-tuple-element.22.t_ref, bf16[4,160,128]{2,1,0:T(8,128)(2,1)S(1)} %collective-permute-done.6.pw0, ...), custom_call_target="tpu_custom_call", output_to_operand_aliasing={{0}: (4, {})} | custom-call | flops 1000 | bytes 8000 | tf_op jit(solution)/shard_map/last/pallas_call | solution.py:369
  41.4 8.6 %all_to_all.15.all_ref = f32[8,8,128]{2,1,0:T(8,128)S(1)} all-to-all(f32[8,8,128]{2,1,0:T(8,128)S(1)} %get-tuple-element.30.st_ref), channel_id=1, replica_groups={{0,32,16,48,64,96,80,112},{1,33,17,49,65,97,81,113},{2,34,18,50,66,98,8..., dimensions={0} | all-to-all | bytes 65536 | tf_op jit(solution)/shard_map/all_to_all | solution.py:379
  50.0 9.0 %sums.1 = (bf16[32,160,128]{2,1,0:T(8,128)(2,1)S(1)}, f32[1,32]{1,0:T(1,128)}) custom-call(s32[2,11]{1,0:T(2,128)S(1)} %bitcast.9, f32[11,160,256]{2,1,0:T(8,128)S(1)} %get-tuple-element.29.e_ref, f32[8,8,128]{2,1,0:T(8,128)S(1)} %get-tuple-element.30.st_ref, f32[8,8,128]{2,1,0:T(8,128)S(1)} %all_to_all.15.all_ref, ...), custom_call_target="tpu_custom_call" | custom-call | flops 4000 | bytes 12000 | tf_op jit(solution)/shard_map/sums/pallas_call | solution.py:380
  59.0 25.8 %all_to_all.16.in_ref = bf16[32,160,128]{2,1,0:T(8,128)(2,1)S(1)} all-to-all(bf16[32,160,128]{2,1,0:T(8,128)(2,1)S(1)} %get-tuple-element.31), channel_id=1, replica_groups=mesh['cls'=4,'img'=32] {'img'}, dimensions={0} | all-to-all | bytes 2621440 | tf_op jit(solution)/shard_map/all_to_all | solution.py:393
  84.8 0.9 finish.1
  (2 shorter events, 0.0 us)
Async XLA Ops:
  2.7 14.9 %all-to-all-start = ((bf16[8,160,128]{2,1,0:T(8,128)(2,1)}), bf16[8,160,128]{2,1,0:T(8,128)(2,1)S(1)}, u32[]{:S(2)}, u32[]{:S(2)}) async-start(bf16[8,160,128]{2,1,0:T(8,128)(2,1)} %get-tuple-element.20), calls=%async_computation | async-start | bytes 655360 | tf_op jit(solution)/shard_map/all_to_all | solution.py:333
  9.0 13.8 %collective-permute-start.2 = (bf16[32,4224]{1,0:T(8,128)(2,1)}, bf16[32,4224]{1,0:T(8,128)(2,1)S(1)}, u32[]{:S(2)}, u32[]{:S(2)}) collective-permute-start(bf16[32,4224]{1,0:T(8,128)(2,1)} %get-tuple-element.19), channel_id=1, source_target_pairs={{0,64},{1,65},{2,66},{3,67},{4,68},{5,69},{6,70},{7,71},{8,72},{9,... | collective-permute-start | bytes 811016 | tf_op jit(solution)/shard_map/ppermute | solution.py:42
  11.7 14.8 %collective-permute-start.1 = (bf16[32,4224]{1,0:T(8,128)(2,1)}, bf16[32,4224]{1,0:T(8,128)(2,1)S(1)}, u32[]{:S(2)}, u32[]{:S(2)}) collective-permute-start(bf16[32,4224]{1,0:T(8,128)(2,1)} %get-tuple-element.19), channel_id=1, source_target_pairs={{0,80},{1,81},{2,82},{3,83},{4,84},{5,85},{6,86},{7,87},{8,88},{9,... | collective-permute-start | bytes 811016 | tf_op jit(solution)/shard_map/ppermute | solution.py:42
  13.7 13.5 %collective-permute-start = (bf16[32,4224]{1,0:T(8,128)(2,1)}, bf16[32,4224]{1,0:T(8,128)(2,1)S(1)}, u32[]{:S(2)}, u32[]{:S(2)}) collective-permute-start(bf16[32,4224]{1,0:T(8,128)(2,1)} %get-tuple-element.19), channel_id=1, source_target_pairs={{0,16},{1,17},{2,18},{3,19},{4,20},{5,21},{6,22},{7,23},{8,24},{9,... | collective-permute-start | bytes 811016 | tf_op jit(solution)/shard_map/ppermute | solution.py:42
  17.6 10.6 %collective-permute-start.4 = (bf16[8,160,128]{2,1,0:T(8,128)(2,1)S(1)}, bf16[8,160,128]{2,1,0:T(8,128)(2,1)S(1)}, u32[]{:S(2)}, u32[]{:S(2)}) collective-permute-start(bf16[8,160,128]{2,1,0:T(8,128)(2,1)S(1)} %all-to-all-done.pc), channel_id=1, source_target_pairs={{0,3},{1,0},{2,1},{3,2},{4,7},{5,4},{6,5},{7,6},{8,11},{9,8},{10,9... | collective-permute-start | bytes 983048 | tf_op jit(solution)/shard_map/ppermute | solution.py:42
  20.6 8.3 %collective-permute-start.3 = (bf16[8,160,128]{2,1,0:T(8,128)(2,1)S(1)}, bf16[8,160,128]{2,1,0:T(8,128)(2,1)S(1)}, u32[]{:S(2)}, u32[]{:S(2)}) collective-permute-start(bf16[8,160,128]{2,1,0:T(8,128)(2,1)S(1)} %all-to-all-done.pc), channel_id=1, source_target_pairs={{0,1},{1,2},{2,3},{3,0},{4,5},{5,6},{6,7},{7,4},{8,9},{9,10},{10,1... | collective-permute-start | bytes 983048 | tf_op jit(solution)/shard_map/ppermute | solution.py:42
  28.2 4.7 %copy-start.1 = (s32[11,2]{0,1:T(2,128)S(1)}, s32[11,2]{0,1:T(2,128)}, u32[]{:S(2)}) copy-start(s32[11,2]{0,1:T(2,128)} %param.9) | copy-start | bytes 268
  28.9 2.7 %collective-permute-start.5 = (bf16[128,4224]{1,0:T(8,128)(2,1)S(1)}, bf16[128,4224]{1,0:T(8,128)(2,1)S(1)}, u32[]{:S(2)}, u32[]{:S(2)}) collective-permute-start(bf16[128,4224]{1,0:T(8,128)(2,1)S(1)} %pad_maximum_fusion.mine), channel_id=1, source_target_pairs={{0,32},{1,33},{2,34},{3,35},{4,36},{5,37},{6,38},{7,39},{8,40},{9,... | collective-permute-start | bytes 3244040 | tf_op jit(solution)/shard_map/ppermute | solution.py:42
  28.9 8.6 %collective-permute-start.7 = (bf16[4,160,128]{2,1,0:T(8,128)(2,1)S(1)}, bf16[4,160,128]{2,1,0:T(8,128)(2,1)S(1)}, u32[]{:S(2)}, u32[]{:S(2)}) collective-permute-start(bf16[4,160,128]{2,1,0:T(8,128)(2,1)S(1)} %slice.7), channel_id=1, source_target_pairs={{0,3},{1,0},{2,1},{3,2},{4,7},{5,4},{6,5},{7,6},{8,11},{9,8},{10,9... | collective-permute-start | bytes 491528 | tf_op jit(solution)/shard_map/ppermute | solution.py:42
  31.4 7.5 %collective-permute-start.6 = (bf16[4,160,128]{2,1,0:T(8,128)(2,1)S(1)}, bf16[4,160,128]{2,1,0:T(8,128)(2,1)S(1)}, u32[]{:S(2)}, u32[]{:S(2)}) collective-permute-start(bf16[4,160,128]{2,1,0:T(8,128)(2,1)S(1)} %slice.6), channel_id=1, source_target_pairs={{0,1},{1,2},{2,3},{3,0},{4,5},{5,6},{6,7},{7,4},{8,9},{9,10},{10,1... | collective-permute-start | bytes 491528 | tf_op jit(solution)/shard_map/ppermute | solution.py:42
  32.9 6.1 %copy-start = (f32[160,128]{1,0:T(8,128)S(1)}, f32[160,128]{1,0:T(8,128)}, u32[]{:S(2)}) copy-start(f32[160,128]{1,0:T(8,128)} %get-tuple-element.28.info_ref) | copy-start | bytes 245764

commit v3 on v2

--- a/solution.py
+++ b/solution.py
@@ -24,7 +24,6 @@
 SHIFTS = 11
 MARGIN = 8
 NEG = -1.0e30
-UNROLL = 4
 
 
 def flat(x, core, z, y):
@@ -214,7 +213,7 @@
         st_ref[k] = stats
 
 
-def sum_kernel(shift_ref, e_ref, st_ref, all_ref, t_ref, out_ref, ev_ref, w_ref):
+def far_kernel(shift_ref, e_ref, st_ref, all_ref, t_ref, out_ref, ev_ref, w_ref, tail_ref):
     x, core, _, _, _ = position()
     stats = [all_ref[k] for k in range(8)]
     peak = stats[0][0:2]
@@ -242,49 +241,94 @@
     ones = jnp.ones((16, SHIFTS * ROW_IMAGES), jnp.bfloat16)
     totals = jnp.dot(ones, w_ref[...], preferred_element_type=jnp.float32)[0:1]
     totals = jnp.concatenate([totals, jnp.zeros((1, 2 * LANES - ROWS), jnp.float32)], axis=1)
+    tail = split_tail(jnp.concatenate([totals[:, :LANES], totals[:, LANES:]], axis=0))
+    tail_ref[...] = tail
+    far = jnp.bitwise_and(position()[4] + 2, 3)
+    for z in range(4):
+        store_sums(out_ref, z, tile_sums(shift_ref, t_ref, w_ref, z, far), tail)
+
+
+def tile_sums(shift_ref, t_ref, w_ref, z, y):
+    low, high = 2 * (4 * z + y), 2 * (4 * z + y) + 2 * 16
+    rows = (low, low + 1, high, high + 1)
+    moved = jnp.concatenate(
+        [shifted_pixels(t_ref, rows, shift_ref[0, s], shift_ref[1, s]) for s in range(SHIFTS)],
+        axis=1,
+    )
+    return jnp.dot(moved, w_ref[...], preferred_element_type=jnp.float32)
+
+
+def is_tail():
+    row = lax.broadcasted_iota(jnp.int32, (16, LANES), 0)
+    return row >= USED - (ROWS - 16)
+
+
+def store_sums(out_ref, z, acc, tail):
+    turned = acc.astype(jnp.bfloat16).T
+    for k in range(2):
+        part = turned[:, k * LANES : (k + 1) * LANES]
+        out_ref[4 * k + z, 0 : ROWS - 16, :] = part[: ROWS - 16]
+        out_ref[4 * k + z, ROWS - 16 : ROWS, :] = jnp.where(is_tail(), tail, part[ROWS - 16 :])
+
+
+def near_kernel(shift_ref, w_ref, tail_ref, t_ref, up_ref, down_ref):
+    y = position()[4]
+    for step, out_ref in ((1, up_ref), (-1, down_ref)):
+        for z in range(4):
+            at = jnp.bitwise_and(y + step, 3)
+            acc = tile_sums(shift_ref, t_ref, w_ref, z, at)
+            store_sums(out_ref, z, acc, tail_ref[...])
+
+
+def own_kernel(shift_ref, w_ref, t_ref, after_ref, out_ref):
+    del after_ref
+    y = position()[4]
+    for z in range(4):
+        turned = tile_sums(shift_ref, t_ref, w_ref, z, y).T
+        for k in range(2):
+            out_ref[4 * k + z] = turned[:, k * LANES : (k + 1) * LANES]
+
+
+def split_tail(totals):
     pieces = []
     for _ in range(3):
         part = totals.astype(jnp.bfloat16).astype(jnp.float32)
         totals = totals - part
-        pieces += [part[:, :LANES], part[:, LANES:]]
-    tail = jnp.concatenate(
-        [jnp.zeros((6, LANES), jnp.float32)] + pieces + [jnp.zeros((4, LANES), jnp.float32)], axis=0
-    ).astype(jnp.bfloat16)
-    is_tail = lax.broadcasted_iota(jnp.int32, (16, LANES), 0) >= 6
-
-    def one_block(pair, carry):
-        rows = tuple(4 * pair + k for k in range(4))
-        moved = jnp.concatenate(
-            [
-                shifted_pixels(t_ref, rows, shift_ref[0, s], shift_ref[1, s])
-                for s in range(SHIFTS)
-            ],
-            axis=1,
-        )
-        acc = jnp.dot(moved, w_ref[...], preferred_element_type=jnp.float32)
-        turned = acc.astype(jnp.bfloat16).T
-        for k in range(2):
-            part = turned[:, k * LANES : (k + 1) * LANES]
-            out_ref[2 * pair + k, 0 : ROWS - 16, :] = part[: ROWS - 16]
-            out_ref[2 * pair + k, ROWS - 16 : ROWS, :] = jnp.where(is_tail, tail, part[ROWS - 16 :])
-        return carry
-
-    lax.fori_loop(0, BLOCKS // 2, one_block, 0, unroll=UNROLL)
+        pieces.append(part)
+    lead = jnp.zeros((USED - (ROWS - 16), LANES), jnp.float32)
+    rest = jnp.zeros((ROWS - USED - 6, LANES), jnp.float32)
+    return jnp.concatenate([lead] + pieces + [rest], axis=0).astype(jnp.bfloat16)
+
+
+def joined_tail(tail):
+    at = USED - (ROWS - 16)
+    return tail[at : at + 2] + tail[at + 2 : at + 4] + tail[at + 4 : at + 6]
+
+
+def add_kernel(own_ref, tail_ref, far_ref, up_ref, down_ref, out_ref):
+    others = (far_ref, up_ref, down_ref)
+    totals = joined_tail(tail_ref[...].astype(jnp.float32))
+    for ref in others:
+        totals = totals + joined_tail(ref[0, ROWS - 16 : ROWS, :].astype(jnp.float32))
+    tail = split_tail(totals)
+    for k in range(8):
+        acc = own_ref[k]
+        for ref in others:
+            acc = acc + ref[k].astype(jnp.float32)
+        acc = acc.astype(jnp.bfloat16)
+        out_ref[k, 0 : ROWS - 16, :] = acc[: ROWS - 16]
+        out_ref[k, ROWS - 16 : ROWS, :] = jnp.where(is_tail(), tail, acc[ROWS - 16 :])
 
 
 def finish_kernel(in_ref, out_ref, wt_ref):
     for half in range(2):
         acc = jnp.zeros((ROWS, LANES), jnp.float32)
-        for k in range(16):
-            acc = acc + in_ref[half * 16 + k].astype(jnp.float32)
+        for k in range(4):
+            acc = acc + in_ref[half * 4 + k].astype(jnp.float32)
         for r in range(HALF_ROT):
             out_ref[half * HALF_ROT + r] = acc[r * CLS : (r + 1) * CLS]
-        wide = [
-            acc[USED + k : USED + k + 1] + acc[USED + 2 + k : USED + 3 + k]
-            + acc[USED + 4 + k : USED + 5 + k]
-            for k in range(2)
-        ]
-        totals = jnp.concatenate(wide, axis=1)
+        wide = joined_tail(acc[ROWS - 16 :])
+        totals = jnp.concatenate([wide[0:1], wide[1:2]], axis=1)
         for r in range(HALF_ROT):
             row = half * HALF_ROT + r
             wt_ref[row : row + 1, :] = totals[:, r * CLS : (r + 1) * CLS]
@@ -377,20 +421,52 @@
         name="last",
     )(shifts, turned, yw0, yw1, scores, norms, rots, info)
     all_stats = lax.all_to_all(stats, AXES, 0, 0, axis_index_groups=X_ROWS)
-    blocks, evidence = pl.pallas_call(
-        sum_kernel,
+    block_shape = jax.ShapeDtypeStruct((8, ROWS, LANES), jnp.bfloat16)
+    far, evidence, weights, tail = pl.pallas_call(
+        far_kernel,
         out_shape=(
-            jax.ShapeDtypeStruct((BLOCKS, ROWS, LANES), jnp.bfloat16),
+            block_shape,
             jax.ShapeDtypeStruct((1, OWN), jnp.float32),
+            jax.ShapeDtypeStruct((SHIFTS * ROW_IMAGES, ROWS), jnp.bfloat16),
+            jax.ShapeDtypeStruct((16, LANES), jnp.bfloat16),
         ),
         in_specs=[SMEM] + [VMEM] * 4,
-        out_specs=(VMEM, VMEM),
-        scratch_shapes=[pltpu.VMEM((SHIFTS * ROW_IMAGES, ROWS), jnp.bfloat16)],
-        compiler_params=PARAMS,
-        cost_estimate=cost(4, 12),
-        name="sums",
+        out_specs=(VMEM,) * 4,
+        compiler_params=PARAMS,
+        cost_estimate=cost(1, 4),
+        name="far",
     )(shifts, scores, stats, all_stats, turned)
-    shares = lax.all_to_all(blocks, "img", 0, 0)
+    from_far = move(far, y=2)
+    up, down = pl.pallas_call(
+        near_kernel,
+        out_shape=(block_shape,) * 2,
+        in_specs=[SMEM] + [VMEM] * 3,
+        out_specs=(VMEM,) * 2,
+        compiler_params=PARAMS,
+        cost_estimate=cost(2, 4),
+        name="near",
+    )(shifts, weights, tail, turned)
+    from_down = move(up, y=1)
+    from_up = move(down, y=-1)
+    own = pl.pallas_call(
+        own_kernel,
+        out_shape=jax.ShapeDtypeStruct((8, ROWS, LANES), jnp.float32),
+        in_specs=[SMEM] + [VMEM] * 2 + [pl.BlockSpec(memory_space=pl.ANY)],
+        out_specs=VMEM,
+        compiler_params=PARAMS,
+        cost_estimate=cost(1, 4),
+        name="own",
+    )(shifts, weights, turned, up)
+    column_sums = pl.pallas_call(
+        add_kernel,
+        out_shape=block_shape,
+        in_specs=[VMEM] * 5,
+        out_specs=VMEM,
+        compiler_params=PARAMS,
+        cost_estimate=cost(0, 2),
+        name="add",
+    )(own, tail, from_far, from_down, from_up)
+    shares = lax.all_to_all(column_sums, "img", 0, 0, axis_index_groups=XZ_GROUPS)
     sums, totals = pl.pallas_call(
         finish_kernel,
         out_shape=(

time: 85.9 us -> 84.3 us (0.981)
  blocking collectives: 34.4 us -> 20.4 us
  waiting for transfers between devices: 12.6 us -> 20.9 us
  starting transfers between devices: 16.6 us -> 19.9 us
    all_to_all x1, blocking collectives: 25.8 us -> 11.8 us  [shards(): lax.all_to_all(column_sums, 'img', 0, 0, axis_index_groups=XZ_GROUPS)]
    ppermute x8 -> x11, waiting for transfers between devices: 8.82 us -> 17.1 us  [move(): return lax.ppermute(value, AXES, route)]
    ppermute x8 -> x11, starting transfers between devices: 10.3 us -> 13.6 us  [move(): return lax.ppermute(value, AXES, route)]
    pallas_call x1 -> x4, Pallas kernels: 9.02 us -> 9.92 us  [the longest x1 3.95 us: shards(): pl.pallas_call(near_kernel, out_shape=(block_shape,) * 2, in_specs=[SMEM]...]
  transfers between devices with their start and end apart: 9 -> 12, of which waited for: 7 -> 10; matrix products, arithmetic and copies ran while one was open for 1% -> 1% of each run, Pallas kernels for 7% -> 15%
where the time goes in v3:
time: 84.3 us; the launch traced here: 84 us
  Pallas kernels  20.9 us (25%)
  waiting for transfers between devices  20.9 us (25%)
  blocking collectives  20.4 us (24%)
  starting transfers between devices  19.9 us (24%)
  other arithmetic  1.03 us (1%)
    ppermute x11, waiting for transfers between devices, move(): return lax.ppermute(value, AXES, route)  17.1 us
    ppermute x11, starting transfers between devices, move(): return lax.ppermute(value, AXES, route)  13.6 us
    all_to_all x1, blocking collectives, shards(): lax.all_to_all(column_sums, 'img', 0, 0, axis_index_groups=XZ_GROUPS)  11.8 us
    all_to_all x1, blocking collectives, shards(): all_stats = lax.all_to_all(stats, AXES, 0, 0, axis_index_groups=X_ROWS)  8.6 us
    all_to_all x1, starting transfers between devices, shards(): column = lax.all_to_all(spread, 'img', 0, 0, axis_index_groups=XZ_GROUPS)  6.34 us
    pallas_call x1, Pallas kernels, shards(): pl.pallas_call(first_kernel, out_shape=(score_shape, norm_shape), in_spec...  4.57 us
    pallas_call x1, Pallas kernels, shards(): pl.pallas_call(near_kernel, out_shape=(block_shape,) * 2, in_specs=[SMEM]...  3.95 us
    all_to_all x1, waiting for transfers between devices, shards(): column = lax.all_to_all(spread, 'img', 0, 0, axis_index_groups=XZ_GROUPS)  3.8 us
  transfers between devices with their start and end apart: 12, of which 10 were waited for; matrix products, arithmetic and copies ran while one was open for 1% of the time, Pallas kernels for 15%

profile of v3, /device:TPU:0, one launch (start us, length us, event | category | flops | bytes accessed | tf_op | source)
XLA Modules:
  0.0 84.0 jit_solution(9819753990047032100)
XLA Ops:
  0.6 2.0 %prepare.1 = (bf16[8,160,128]{2,1,0:T(8,128)(2,1)}, bf16[32,4224]{1,0:T(8,128)(2,1)}, f32[160,128]{1,0:T(8,128)}) custom-call(bf16[12,25,128]{2,1,0:T(8,128)(2,1)} %bitcast.12, f32[32,4096]{1,0:T(8,128)} %refs_1_.1, s32[1,32]{1,0:T(1,128)} %bitcast.13, f32[1,25]{1,0:T(1,128)} %bitcast.14), custom_call_target="tpu_custom_call" | custom-call | bytes 1000 | tf_op jit(solution)/shard_map/prepare/pallas_call | solution.py:348
  2.7 6.3 %all-to-all-start = ((bf16[8,160,128]{2,1,0:T(8,128)(2,1)}), bf16[8,160,128]{2,1,0:T(8,128)(2,1)S(1)}, u32[]{:S(2)}, u32[]{:S(2)}) async-start(bf16[8,160,128]{2,1,0:T(8,128)(2,1)} %get-tuple-element.24), calls=%async_computation | async-start | bytes 655360 | tf_op jit(solution)/shard_map/all_to_all | solution.py:377
  9.0 2.7 %collective-permute-start.2 = (bf16[32,4224]{1,0:T(8,128)(2,1)}, bf16[32,4224]{1,0:T(8,128)(2,1)S(1)}, u32[]{:S(2)}, u32[]{:S(2)}) collective-permute-start(bf16[32,4224]{1,0:T(8,128)(2,1)} %get-tuple-element.23), channel_id=1, source_target_pairs={{0,64},{1,65},{2,66},{3,67},{4,68},{5,69},{6,70},{7,71},{8,72},{9,... | collective-permute-start | bytes 811016 | tf_op jit(solution)/shard_map/ppermute | solution.py:41
  11.7 2.0 %collective-permute-start.1 = (bf16[32,4224]{1,0:T(8,128)(2,1)}, bf16[32,4224]{1,0:T(8,128)(2,1)S(1)}, u32[]{:S(2)}, u32[]{:S(2)}) collective-permute-start(bf16[32,4224]{1,0:T(8,128)(2,1)} %get-tuple-element.23), channel_id=1, source_target_pairs={{0,80},{1,81},{2,82},{3,83},{4,84},{5,85},{6,86},{7,87},{8,88},{9,... | collective-permute-start | bytes 811016 | tf_op jit(solution)/shard_map/ppermute | solution.py:41
  13.7 0.1 collective-permute-start
  13.8 3.8 %all-to-all-done.pc = bf16[8,160,128]{2,1,0:T(8,128)(2,1)S(1)} async-done(((bf16[8,160,128]{2,1,0:T(8,128)(2,1)}), bf16[8,160,128]{2,1,0:T(8,128)(2,1)S(1)}, u32[]{:S(2)}, u32[]{:S(2)}) %all-to-all-start) | async-done | bytes 327712 | tf_op jit(solution)/shard_map/all_to_all | solution.py:377
  17.6 3.0 %collective-permute-start.4 = (bf16[8,160,128]{2,1,0:T(8,128)(2,1)S(1)}, bf16[8,160,128]{2,1,0:T(8,128)(2,1)S(1)}, u32[]{:S(2)}, u32[]{:S(2)}) collective-permute-start(bf16[8,160,128]{2,1,0:T(8,128)(2,1)S(1)} %all-to-all-done.pc), channel_id=1, source_target_pairs={{0,3},{1,0},{2,1},{3,2},{4,7},{5,4},{6,5},{7,6},{8,11},{9,8},{10,9... | collective-permute-start | bytes 983048 | tf_op jit(solution)/shard_map/ppermute | solution.py:41
  20.6 2.3 %collective-permute-done.2 = bf16[32,4224]{1,0:T(8,128)(2,1)S(1)} collective-permute-done((bf16[32,4224]{1,0:T(8,128)(2,1)}, bf16[32,4224]{1,0:T(8,128)(2,1)S(1)}, u32[]{:S(2)}, u32[]{:S(2)}) %collective-permute-start.2) | collective-permute-done | bytes 270368 | tf_op jit(solution)/shard_map/ppermute | solution.py:41
  22.8 3.7 %collective-permute-done.1 = bf16[32,4224]{1,0:T(8,128)(2,1)S(1)} collective-permute-done((bf16[32,4224]{1,0:T(8,128)(2,1)}, bf16[32,4224]{1,0:T(8,128)(2,1)S(1)}, u32[]{:S(2)}, u32[]{:S(2)}) %collective-permute-start.1) | collective-permute-done | bytes 270368 | tf_op jit(solution)/shard_map/ppermute | solution.py:41
  26.5 0.7 collective-permute-done
  27.2 1.0 %pad_maximum_fusion.mine = bf16[128,4224]{1,0:T(8,128)(2,1)S(1)} fusion(bf16[32,4224]{1,0:T(8,128)(2,1)S(1)} %collective-permute-done.2, bf16[32,4224]{1,0:T(8,128)(2,1)S(1)} %collective-permute-done.1, bf16[32,4224]{1,0:T(8,128)(2,1)S(1)} %collective-permute-done, bf16[32,4224]{1,0:T(8,128)(2,1)} %get-tuple-element.23), kind=kLoop, calls=%fused_computation | loop fusion | flops 4325376 | bytes 2162688 | tf_op jit(solution)/shard_map/concatenate | solution.py:380
  28.2 0.0 copy-start.1
  28.2 0.7 collective-permute-done.3.py1
  28.9 2.5 %collective-permute-start.7 = (bf16[4,160,128]{2,1,0:T(8,128)(2,1)S(1)}, bf16[4,160,128]{2,1,0:T(8,128)(2,1)S(1)}, u32[]{:S(2)}, u32[]{:S(2)}) collective-permute-start(bf16[4,160,128]{2,1,0:T(8,128)(2,1)S(1)} %slice.7), channel_id=1, source_target_pairs={{0,3},{1,0},{2,1},{3,2},{4,7},{5,4},{6,5},{7,6},{8,11},{9,8},{10,9... | collective-permute-start | bytes 491528 | tf_op jit(solution)/shard_map/ppermute | solution.py:41
  31.4 0.1 collective-permute-done.5.other
  31.6 1.3 %turn.1 = (f32[2,64,80,128]{3,2,1,0:T(8,128)S(1)}, f32[2,8,128]{2,1,0:T(8,128)S(1)}) custom-call(bf16[128,4224]{1,0:T(8,128)(2,1)S(1)} %pad_maximum_fusion.mine, bf16[128,4224]{1,0:T(8,128)(2,1)S(1)} %collective-permute-done.5.other), custom_call_target="tpu_custom_call" | custom-call | bytes 8000 | tf_op jit(solution)/shard_map/turn/pallas_call | solution.py:386
  32.9 4.6 %first.1 = (f32[11,160,256]{2,1,0:T(8,128)S(1)}, f32[160,128]{1,0:T(8,128)S(1)}) custom-call(s32[2,11]{1,0:T(2,128)S(1)} %bitcast.7, f32[2,64,80,128]{3,2,1,0:T(8,128)S(1)} %get-tuple-element.26.t_ref, bf16[8,160,128]{2,1,0:T(8,128)(2,1)S(1)} %all-to-all-done.pc, bf16[8,160,128]{2,1,0:T(8,128)(2,1)S(1)} %collective-permute-done.3.py1, ...), custom_call_target="tpu_custom_call" | custom-call | flops 3000 | bytes 4000 | tf_op jit(solution)/shard_map/first/pallas_call | solution.py:403
  37.5 1.5 %collective-permute-done.6.pw0 = bf16[4,160,128]{2,1,0:T(8,128)(2,1)S(1)} collective-permute-done((bf16[4,160,128]{2,1,0:T(8,128)(2,1)S(1)}, bf16[4,160,128]{2,1,0:T(8,128)(2,1)S(1)}, u32[]{:S(2)}, u32[]{:S(2)}) %collective-permute-start.6) | collective-permute-done | bytes 163872 | tf_op jit(solution)/shard_map/ppermute | solution.py:41
  39.0 2.4 %last.1 = (f32[11,160,256]{2,1,0:T(8,128)S(1)}, f32[8,8,128]{2,1,0:T(8,128)S(1)}) custom-call(s32[2,11]{1,0:T(2,128)S(1)} %bitcast.8, f32[2,64,80,128]{3,2,1,0:T(8,128)S(1)} %get-tuple-element.26.t_ref, bf16[4,160,128]{2,1,0:T(8,128)(2,1)S(1)} %collective-permute-done.6.pw0, ...), custom_call_target="tpu_custom_call", output_to_operand_aliasing={{0}: (4, {})} | custom-call | flops 1000 | bytes 8000 | tf_op jit(solution)/shard_map/last/pallas_call | solution.py:413
  41.4 8.6 %all_to_all.15.all_ref = f32[8,8,128]{2,1,0:T(8,128)S(1)} all-to-all(f32[8,8,128]{2,1,0:T(8,128)S(1)} %get-tuple-element.34.st_ref), channel_id=1, replica_groups={{0,32,16,48,64,96,80,112},{1,33,17,49,65,97,81,113},{2,34,18,50,66,98,8..., dimensions={0} | all-to-all | bytes 65536 | tf_op jit(solution)/shard_map/all_to_all | solution.py:423
  50.0 3.4 %far.1 = (bf16[8,160,128]{2,1,0:T(8,128)(2,1)S(1)}, f32[1,32]{1,0:T(1,128)}, bf16[2816,160]{1,0:T(8,128)(2,1)S(1)}, bf16[16,128]{1,0:T(8,128)(2,1)S(1)}) custom-call(s32[2,11]{1,0:T(2,128)S(1)} %bitcast.9, f32[11,160,256]{2,1,0:T(8,128)S(1)} %get-tuple-element.33.e_ref, f32[8,8,128]{2,1,0:T(8,128)S(1)} %get-tuple-element.34.st_ref, ...), custom_call_target="tpu_custom_call" | custom-call | flops 1000 | bytes 4000 | tf_op jit(solution)/shard_map/far/pallas_call | solution.py:425
  53.4 1.2 %collective-permute-start.8 = (bf16[8,160,128]{2,1,0:T(8,128)(2,1)S(1)}, bf16[8,160,128]{2,1,0:T(8,128)(2,1)S(1)}, u32[]{:S(2)}, u32[]{:S(2)}) collective-permute-start(bf16[8,160,128]{2,1,0:T(8,128)(2,1)S(1)} %get-tuple-element.38), channel_id=1, source_target_pairs={{0,2},{1,3},{2,0},{3,1},{4,6},{5,7},{6,4},{7,5},{8,10},{9,11},{10,... | collective-permute-start | bytes 983048 | tf_op jit(solution)/shard_map/ppermute | solution.py:41
  54.5 3.9 %near.1 = (bf16[8,160,128]{2,1,0:T(8,128)(2,1)S(1)}, bf16[8,160,128]{2,1,0:T(8,128)(2,1)S(1)}) custom-call(s32[2,11]{1,0:T(2,128)S(1)} %bitcast.10, bf16[2816,160]{1,0:T(8,128)(2,1)S(1)} %get-tuple-element.35.w_ref, bf16[16,128]{1,0:T(8,128)(2,1)S(1)} %get-tuple-element.36.tail_ref, f32[2,64,80,128]{3,2,1,0:T(8,128)S(1)} %get-tuple-element.26.t_ref), custom_call_target="tpu_custom_call" | custom-call | flops 2000 | bytes 4000 | tf_op jit(solution)/shard_map/near/pallas_call | solution.py:440
  58.5 1.1 %collective-permute-start.10 = (bf16[8,160,128]{2,1,0:T(8,128)(2,1)S(1)}, bf16[8,160,128]{2,1,0:T(8,128)(2,1)S(1)}, u32[]{:S(2)}, u32[]{:S(2)}) collective-permute-start(bf16[8,160,128]{2,1,0:T(8,128)(2,1)S(1)} %get-tuple-element.39), channel_id=1, source_target_pairs={{0,3},{1,0},{2,1},{3,2},{4,7},{5,4},{6,5},{7,6},{8,11},{9,8},{10,9... | collective-permute-start | bytes 983048 | tf_op jit(solution)/shard_map/ppermute | solution.py:41
  59.6 1.0 %collective-permute-start.9 = (bf16[8,160,128]{2,1,0:T(8,128)(2,1)S(1)}, bf16[8,160,128]{2,1,0:T(8,128)(2,1)S(1)}, u32[]{:S(2)}, u32[]{:S(2)}) collective-permute-start(bf16[8,160,128]{2,1,0:T(8,128)(2,1)S(1)} %get-tuple-element.37.after_ref), channel_id=1, source_target_pairs={{0,1},{1,2},{2,3},{3,0},{4,5},{5,6},{6,7},{7,4},{8,9},{9,10},{10,1... | collective-permute-start | bytes 983048 | tf_op jit(solution)/shard_map/ppermute | solution.py:41
  60.6 2.4 %own.1.own_ref = f32[8,160,128]{2,1,0:T(8,128)S(1)} custom-call(s32[2,11]{1,0:T(2,128)S(1)} %bitcast.11, bf16[2816,160]{1,0:T(8,128)(2,1)S(1)} %get-tuple-element.35.w_ref, f32[2,64,80,128]{3,2,1,0:T(8,128)S(1)} %get-tuple-element.26.t_ref, bf16[8,160,128]{2,1,0:T(8,128)(2,1)S(1)} %get-tuple-element.37.after_ref), custom_call_target="tpu_custom_call" | custom-call | flops 1000 | bytes 4000 | tf_op jit(solution)/shard_map/own/pallas_call | solution.py:451
  63.0 2.5 %collective-permute-done.8.far_ref = bf16[8,160,128]{2,1,0:T(8,128)(2,1)S(1)} collective-permute-done((bf16[8,160,128]{2,1,0:T(8,128)(2,1)S(1)}, bf16[8,160,128]{2,1,0:T(8,128)(2,1)S(1)}, u32[]{:S(2)}, u32[]{:S(2)}) %collective-permute-start.8) | collective-permute-done | bytes 327712 | tf_op jit(solution)/shard_map/ppermute | solution.py:41
  65.5 4.8 %collective-permute-done.10.down_ref = bf16[8,160,128]{2,1,0:T(8,128)(2,1)S(1)} collective-permute-done((bf16[8,160,128]{2,1,0:T(8,128)(2,1)S(1)}, bf16[8,160,128]{2,1,0:T(8,128)(2,1)S(1)}, u32[]{:S(2)}, u32[]{:S(2)}) %collective-permute-start.10) | collective-permute-done | bytes 327712 | tf_op jit(solution)/shard_map/ppermute | solution.py:41
  70.3 1.0 %collective-permute-done.9.up_ref = bf16[8,160,128]{2,1,0:T(8,128)(2,1)S(1)} collective-permute-done((bf16[8,160,128]{2,1,0:T(8,128)(2,1)S(1)}, bf16[8,160,128]{2,1,0:T(8,128)(2,1)S(1)}, u32[]{:S(2)}, u32[]{:S(2)}) %collective-permute-start.9) | collective-permute-done | bytes 327712 | tf_op jit(solution)/shard_map/ppermute | solution.py:41
  71.3 0.2 add.1
  71.4 11.8 %all_to_all.16.in_ref = bf16[8,160,128]{2,1,0:T(8,128)(2,1)S(1)} all-to-all(bf16[8,160,128]{2,1,0:T(8,128)(2,1)S(1)} %add.1), channel_id=1, replica_groups={{0,4,8,12,16,20,24,28},{1,5,9,13,17,21,25,29},{2,6,10,14,18,22,26,30},{..., dimensions={0} | all-to-all | bytes 655360 | tf_op jit(solution)/shard_map/all_to_all | solution.py:469
  83.2 0.7 finish.1
  (10 shorter events, 0.0 us)
Async XLA Ops:
  2.7 14.9 %all-to-all-start = ((bf16[8,160,128]{2,1,0:T(8,128)(2,1)}), bf16[8,160,128]{2,1,0:T(8,128)(2,1)S(1)}, u32[]{:S(2)}, u32[]{:S(2)}) async-start(bf16[8,160,128]{2,1,0:T(8,128)(2,1)} %get-tuple-element.24), calls=%async_computation | async-start | bytes 655360 | tf_op jit(solution)/shard_map/all_to_all | solution.py:377
  9.0 13.8 %collective-permute-start.2 = (bf16[32,4224]{1,0:T(8,128)(2,1)}, bf16[32,4224]{1,0:T(8,128)(2,1)S(1)}, u32[]{:S(2)}, u32[]{:S(2)}) collective-permute-start(bf16[32,4224]{1,0:T(8,128)(2,1)} %get-tuple-element.23), channel_id=1, source_target_pairs={{0,64},{1,65},{2,66},{3,67},{4,68},{5,69},{6,70},{7,71},{8,72},{9,... | collective-permute-start | bytes 811016 | tf_op jit(solution)/shard_map/ppermute | solution.py:41
  11.7 14.8 %collective-permute-start.1 = (bf16[32,4224]{1,0:T(8,128)(2,1)}, bf16[32,4224]{1,0:T(8,128)(2,1)S(1)}, u32[]{:S(2)}, u32[]{:S(2)}) collective-permute-start(bf16[32,4224]{1,0:T(8,128)(2,1)} %get-tuple-element.23), channel_id=1, source_target_pairs={{0,80},{1,81},{2,82},{3,83},{4,84},{5,85},{6,86},{7,87},{8,88},{9,... | collective-permute-start | bytes 811016 | tf_op jit(solution)/shard_map/ppermute | solution.py:41
  13.7 13.5 %collective-permute-start = (bf16[32,4224]{1,0:T(8,128)(2,1)}, bf16[32,4224]{1,0:T(8,128)(2,1)S(1)}, u32[]{:S(2)}, u32[]{:S(2)}) collective-permute-start(bf16[32,4224]{1,0:T(8,128)(2,1)} %get-tuple-element.23), channel_id=1, source_target_pairs={{0,16},{1,17},{2,18},{3,19},{4,20},{5,21},{6,22},{7,23},{8,24},{9,... | collective-permute-start | bytes 811016 | tf_op jit(solution)/shard_map/ppermute | solution.py:41
  17.6 10.6 %collective-permute-start.4 = (bf16[8,160,128]{2,1,0:T(8,128)(2,1)S(1)}, bf16[8,160,128]{2,1,0:T(8,128)(2,1)S(1)}, u32[]{:S(2)}, u32[]{:S(2)}) collective-permute-start(bf16[8,160,128]{2,1,0:T(8,128)(2,1)S(1)} %all-to-all-done.pc), channel_id=1, source_target_pairs={{0,3},{1,0},{2,1},{3,2},{4,7},{5,4},{6,5},{7,6},{8,11},{9,8},{10,9... | collective-permute-start | bytes 983048 | tf_op jit(solution)/shard_map/ppermute | solution.py:41
  20.6 8.3 %collective-permute-start.3 = (bf16[8,160,128]{2,1,0:T(8,128)(2,1)S(1)}, bf16[8,160,128]{2,1,0:T(8,128)(2,1)S(1)}, u32[]{:S(2)}, u32[]{:S(2)}) collective-permute-start(bf16[8,160,128]{2,1,0:T(8,128)(2,1)S(1)} %all-to-all-done.pc), channel_id=1, source_target_pairs={{0,1},{1,2},{2,3},{3,0},{4,5},{5,6},{6,7},{7,4},{8,9},{9,10},{10,1... | collective-permute-start | bytes 983048 | tf_op jit(solution)/shard_map/ppermute | solution.py:41
  28.2 4.7 %copy-start.1 = (s32[11,2]{0,1:T(2,128)S(1)}, s32[11,2]{0,1:T(2,128)}, u32[]{:S(2)}) copy-start(s32[11,2]{0,1:T(2,128)} %param.9) | copy-start | bytes 268
  28.9 2.7 %collective-permute-start.5 = (bf16[128,4224]{1,0:T(8,128)(2,1)S(1)}, bf16[128,4224]{1,0:T(8,128)(2,1)S(1)}, u32[]{:S(2)}, u32[]{:S(2)}) collective-permute-start(bf16[128,4224]{1,0:T(8,128)(2,1)S(1)} %pad_maximum_fusion.mine), channel_id=1, source_target_pairs={{0,32},{1,33},{2,34},{3,35},{4,36},{5,37},{6,38},{7,39},{8,40},{9,... | collective-permute-start | bytes 3244040 | tf_op jit(solution)/shard_map/ppermute | solution.py:41
  28.9 8.6 %collective-permute-start.7 = (bf16[4,160,128]{2,1,0:T(8,128)(2,1)S(1)}, bf16[4,160,128]{2,1,0:T(8,128)(2,1)S(1)}, u32[]{:S(2)}, u32[]{:S(2)}) collective-permute-start(bf16[4,160,128]{2,1,0:T(8,128)(2,1)S(1)} %slice.7), channel_id=1, source_target_pairs={{0,3},{1,0},{2,1},{3,2},{4,7},{5,4},{6,5},{7,6},{8,11},{9,8},{10,9... | collective-permute-start | bytes 491528 | tf_op jit(solution)/shard_map/ppermute | solution.py:41
  31.4 7.5 %collective-permute-start.6 = (bf16[4,160,128]{2,1,0:T(8,128)(2,1)S(1)}, bf16[4,160,128]{2,1,0:T(8,128)(2,1)S(1)}, u32[]{:S(2)}, u32[]{:S(2)}) collective-permute-start(bf16[4,160,128]{2,1,0:T(8,128)(2,1)S(1)} %slice.6), channel_id=1, source_target_pairs={{0,1},{1,2},{2,3},{3,0},{4,5},{5,6},{6,7},{7,4},{8,9},{9,10},{10,1... | collective-permute-start | bytes 491528 | tf_op jit(solution)/shard_map/ppermute | solution.py:41
  32.9 6.1 %copy-start = (f32[160,128]{1,0:T(8,128)S(1)}, f32[160,128]{1,0:T(8,128)}, u32[]{:S(2)}) copy-start(f32[160,128]{1,0:T(8,128)} %get-tuple-element.32.info_ref) | copy-start | bytes 245764
  53.4 12.1 %collective-permute-start.8 = (bf16[8,160,128]{2,1,0:T(8,128)(2,1)S(1)}, bf16[8,160,128]{2,1,0:T(8,128)(2,1)S(1)}, u32[]{:S(2)}, u32[]{:S(2)}) collective-permute-start(bf16[8,160,128]{2,1,0:T(8,128)(2,1)S(1)} %get-tuple-element.38), channel_id=1, source_target_pairs={{0,2},{1,3},{2,0},{3,1},{4,6},{5,7},{6,4},{7,5},{8,10},{9,11},{10,... | collective-permute-start | bytes 983048 | tf_op jit(solution)/shard_map/ppermute | solution.py:41
  58.5 11.8 %collective-permute-start.10 = (bf16[8,160,128]{2,1,0:T(8,128)(2,1)S(1)}, bf16[8,160,128]{2,1,0:T(8,128)(2,1)S(1)}, u32[]{:S(2)}, u32[]{:S(2)}) collective-permute-start(bf16[8,160,128]{2,1,0:T(8,128)(2,1)S(1)} %get-tuple-element.39), channel_id=1, source_target_pairs={{0,3},{1,0},{2,1},{3,2},{4,7},{5,4},{6,5},{7,6},{8,11},{9,8},{10,9... | collective-permute-start | bytes 983048 | tf_op jit(solution)/shard_map/ppermute | solution.py:41
  59.6 11.7 %collective-permute-start.9 = (bf16[8,160,128]{2,1,0:T(8,128)(2,1)S(1)}, bf16[8,160,128]{2,1,0:T(8,128)(2,1)S(1)}, u32[]{:S(2)}, u32[]{:S(2)}) collective-permute-start(bf16[8,160,128]{2,1,0:T(8,128)(2,1)S(1)} %get-tuple-element.37.after_ref), channel_id=1, source_target_pairs={{0,1},{1,2},{2,3},{3,0},{4,5},{5,6},{6,7},{7,4},{8,9},{9,10},{10,1... | collective-permute-start | bytes 983048 | tf_op jit(solution)/shard_map/ppermute | solution.py:41

commit v4 on v3

--- a/solution.py
+++ b/solution.py
@@ -94,14 +94,16 @@
     info_ref[USED:ROWS, :] = jnp.full((ROWS - USED, LANES), NEG, jnp.float32)
 
 
-def turn_kernel(mine, other, t_ref, rot_ref, x_ref):
+def turn_kernel(own, own_other, mine, other, t_ref, rot_ref, x_ref):
     x, core, _, _, _ = position()
 
     def put(value, dx, dc):
         slot = jnp.bitwise_and(x + dx, 3) * 2 + jnp.bitwise_xor(core, dc)
         x_ref[pl.ds(pl.multiple_of(slot * OWN, OWN), OWN), :] = value
 
-    for k, dx in enumerate((0, -1, 1, 2)):
+    put(own[...], 0, 0)
+    put(own_other[...], 0, 1)
+    for k, dx in enumerate((-1, 1, 2)):
         put(mine[k * OWN : (k + 1) * OWN], dx, 0)
         put(other[k * OWN : (k + 1) * OWN], dx, 1)
 
@@ -244,17 +246,28 @@
     tail = split_tail(jnp.concatenate([totals[:, :LANES], totals[:, LANES:]], axis=0))
     tail_ref[...] = tail
     far = jnp.bitwise_and(position()[4] + 2, 3)
-    for z in range(4):
+    for z in range(0, 4, GROUP):
         store_sums(out_ref, z, tile_sums(shift_ref, t_ref, w_ref, z, far), tail)
 
 
+GROUP = 4
+
+
 def tile_sums(shift_ref, t_ref, w_ref, z, y):
-    low, high = 2 * (4 * z + y), 2 * (4 * z + y) + 2 * 16
-    rows = (low, low + 1, high, high + 1)
-    moved = jnp.concatenate(
-        [shifted_pixels(t_ref, rows, shift_ref[0, s], shift_ref[1, s]) for s in range(SHIFTS)],
-        axis=1,
-    )
+    tiles = []
+    for k in range(GROUP):
+        low = 2 * (4 * (z + k) + y)
+        rows = (low, low + 1, low + 2 * 16, low + 2 * 16 + 1)
+        tiles.append(
+            jnp.concatenate(
+                [
+                    shifted_pixels(t_ref, rows, shift_ref[0, s], shift_ref[1, s])
+                    for s in range(SHIFTS)
+                ],
+                axis=1,
+            )
+        )
+    moved = jnp.concatenate(tiles, axis=0)
     return jnp.dot(moved, w_ref[...], preferred_element_type=jnp.float32)
 
 
@@ -265,16 +278,17 @@
 
 def store_sums(out_ref, z, acc, tail):
     turned = acc.astype(jnp.bfloat16).T
-    for k in range(2):
+    for k in range(2 * GROUP):
         part = turned[:, k * LANES : (k + 1) * LANES]
-        out_ref[4 * k + z, 0 : ROWS - 16, :] = part[: ROWS - 16]
-        out_ref[4 * k + z, ROWS - 16 : ROWS, :] = jnp.where(is_tail(), tail, part[ROWS - 16 :])
+        at = 4 * (k % 2) + z + k // 2
+        out_ref[at, 0 : ROWS - 16, :] = part[: ROWS - 16]
+        out_ref[at, ROWS - 16 : ROWS, :] = jnp.where(is_tail(), tail, part[ROWS - 16 :])
 
 
 def near_kernel(shift_ref, w_ref, tail_ref, t_ref, up_ref, down_ref):
     y = position()[4]
     for step, out_ref in ((1, up_ref), (-1, down_ref)):
-        for z in range(4):
+        for z in range(0, 4, GROUP):
             at = jnp.bitwise_and(y + step, 3)
             acc = tile_sums(shift_ref, t_ref, w_ref, z, at)
             store_sums(out_ref, z, acc, tail_ref[...])
@@ -283,10 +297,10 @@
 def own_kernel(shift_ref, w_ref, t_ref, after_ref, out_ref):
     del after_ref
     y = position()[4]
-    for z in range(4):
+    for z in range(0, 4, GROUP):
         turned = tile_sums(shift_ref, t_ref, w_ref, z, y).T
-        for k in range(2):
-            out_ref[4 * k + z] = turned[:, k * LANES : (k + 1) * LANES]
+        for k in range(2 * GROUP):
+            out_ref[4 * (k % 2) + z + k // 2] = turned[:, k * LANES : (k + 1) * LANES]
 
 
 def split_tail(totals):
@@ -371,13 +385,15 @@
         rot_prior.reshape(1, OWN),
         log_prior.reshape(1, CLS),
     )
+    c0 = move(images, core=1)
     a1 = move(images, x=1)
     a2 = move(images, x=-1)
     a3 = move(images, x=2)
     column = lax.all_to_all(spread, "img", 0, 0, axis_index_groups=XZ_GROUPS)
+    column, c0 = lax.optimization_barrier((column, c0))
     y1 = move(column, y=1)
     y3 = move(column, y=-1)
-    mine = jnp.concatenate([images, a1, a2, a3], axis=0)
+    mine = jnp.concatenate([a1, a2, a3], axis=0)
     mine, y1, y3 = lax.optimization_barrier((mine, y1, y3))
     cc = move(mine, core=1)
     yw0 = move(y1[:4], y=1)
@@ -389,13 +405,13 @@
             jax.ShapeDtypeStruct((2, SIDE, SIDE + 2 * MARGIN, LANES), jnp.float32),
             jax.ShapeDtypeStruct((2, 8, LANES), jnp.float32),
         ),
-        in_specs=[VMEM] * 2,
+        in_specs=[VMEM] * 4,
         out_specs=(VMEM, VMEM),
         scratch_shapes=[pltpu.VMEM((ROW_IMAGES, PIX + LANES), jnp.bfloat16)],
         compiler_params=PARAMS,
         cost_estimate=cost(0, 8),
         name="turn",
-    )(mine, cc)
+    )(images, c0, mine, cc)
 
     shifts = shift_table.T
     score_shape = jax.ShapeDtypeStruct((SHIFTS, ROWS, ROW_IMAGES), jnp.float32)

time: 84.3 us -> 83.3 us (0.988)
  waiting for transfers between devices: 20.9 us -> 21.9 us
  other arithmetic: 1.03 us -> 0.06 us
    ppermute x11 -> x12, waiting for transfers between devices: 17.1 us -> 18.9 us  [move(): return lax.ppermute(value, AXES, route)]
    concatenate x1, other arithmetic: 1.03 us -> 0.06 us  [shards(): mine = jnp.concatenate([a1, a2, a3], axis=0)]
    ppermute x11 -> x12, starting transfers between devices: 13.6 us -> 13 us  [move(): return lax.ppermute(value, AXES, route)]
  transfers between devices with their start and end apart: 12 -> 13, of which waited for: 10 -> 10; matrix products, arithmetic and copies ran while one was open for 1% -> 0% of each run, Pallas kernels for 15% -> 15%
where the time goes in v4:
time: 83.3 us; the launch traced here: 83 us
  waiting for transfers between devices  21.9 us (26%)
  Pallas kernels  20.6 us (25%)
  blocking collectives  20.2 us (24%)
  starting transfers between devices  19.5 us (23%)
    ppermute x12, waiting for transfers between devices, move(): return lax.ppermute(value, AXES, route)  18.9 us
    ppermute x12, starting transfers between devices, move(): return lax.ppermute(value, AXES, route)  13 us
    all_to_all x1, blocking collectives, shards(): lax.all_to_all(column_sums, 'img', 0, 0, axis_index_groups=XZ_GROUPS)  11.9 us
    all_to_all x1, blocking collectives, shards(): all_stats = lax.all_to_all(stats, AXES, 0, 0, axis_index_groups=X_ROWS)  8.31 us
    all_to_all x1, starting transfers between devices, shards(): column = lax.all_to_all(spread, 'img', 0, 0, axis_index_groups=XZ_GROUPS)  6.47 us
    pallas_call x1, Pallas kernels, shards(): pl.pallas_call(first_kernel, out_shape=(score_shape, norm_shape), in_spec...  4.65 us
    pallas_call x1, Pallas kernels, shards(): pl.pallas_call(near_kernel, out_shape=(block_shape,) * 2, in_specs=[SMEM]...  3.79 us
    pallas_call x1, Pallas kernels, shards(): pl.pallas_call(far_kernel, out_shape=(block_shape, jax.ShapeDtypeStruct((...  3.17 us
  transfers between devices with their start and end apart: 13, of which 10 were waited for; matrix products, arithmetic and copies ran while one was open for 0% of the time, Pallas kernels for 15%

profile of v4, /device:TPU:0, one launch (start us, length us, event | category | flops | bytes accessed | tf_op | source)
XLA Modules:
  0.0 83.0 jit_solution(17947438945133674542)
XLA Ops:
  0.6 2.0 %prepare.1 = (bf16[8,160,128]{2,1,0:T(8,128)(2,1)}, bf16[32,4224]{1,0:T(8,128)(2,1)}, f32[160,128]{1,0:T(8,128)}) custom-call(bf16[12,25,128]{2,1,0:T(8,128)(2,1)} %bitcast.12, f32[32,4096]{1,0:T(8,128)} %refs_1_.1, s32[1,32]{1,0:T(1,128)} %bitcast.13, f32[1,25]{1,0:T(1,128)} %bitcast.14), custom_call_target="tpu_custom_call" | custom-call | bytes 1000 | tf_op jit(solution)/shard_map/prepare/pallas_call | solution.py:362
  2.7 6.5 %all-to-all-start = ((bf16[8,160,128]{2,1,0:T(8,128)(2,1)}), bf16[8,160,128]{2,1,0:T(8,128)(2,1)S(1)}, u32[]{:S(2)}, u32[]{:S(2)}) async-start(bf16[8,160,128]{2,1,0:T(8,128)(2,1)} %get-tuple-element.26), calls=%async_computation | async-start | bytes 655360 | tf_op jit(solution)/shard_map/all_to_all | solution.py:392
  9.2 2.8 %collective-permute-start.3 = (bf16[32,4224]{1,0:T(8,128)(2,1)}, bf16[32,4224]{1,0:T(8,128)(2,1)S(1)}, u32[]{:S(2)}, u32[]{:S(2)}) collective-permute-start(bf16[32,4224]{1,0:T(8,128)(2,1)} %get-tuple-element.25.own), channel_id=1, source_target_pairs={{0,64},{1,65},{2,66},{3,67},{4,68},{5,69},{6,70},{7,71},{8,72},{9,... | collective-permute-start | bytes 811016 | tf_op jit(solution)/shard_map/ppermute | solution.py:41
  12.0 1.9 %collective-permute-start.2 = (bf16[32,4224]{1,0:T(8,128)(2,1)}, bf16[32,4224]{1,0:T(8,128)(2,1)S(1)}, u32[]{:S(2)}, u32[]{:S(2)}) collective-permute-start(bf16[32,4224]{1,0:T(8,128)(2,1)} %get-tuple-element.25.own), channel_id=1, source_target_pairs={{0,80},{1,81},{2,82},{3,83},{4,84},{5,85},{6,86},{7,87},{8,88},{9,... | collective-permute-start | bytes 811016 | tf_op jit(solution)/shard_map/ppermute | solution.py:41
  13.8 0.1 collective-permute-start.1
  14.0 3.0 %all-to-all-done.pc = bf16[8,160,128]{2,1,0:T(8,128)(2,1)S(1)} async-done(((bf16[8,160,128]{2,1,0:T(8,128)(2,1)}), bf16[8,160,128]{2,1,0:T(8,128)(2,1)S(1)}, u32[]{:S(2)}, u32[]{:S(2)}) %all-to-all-start) | async-done | bytes 327712 | tf_op jit(solution)/shard_map/all_to_all | solution.py:392
  17.0 3.0 %collective-permute-start.5 = (bf16[8,160,128]{2,1,0:T(8,128)(2,1)S(1)}, bf16[8,160,128]{2,1,0:T(8,128)(2,1)S(1)}, u32[]{:S(2)}, u32[]{:S(2)}) collective-permute-start(bf16[8,160,128]{2,1,0:T(8,128)(2,1)S(1)} %all-to-all-done.pc), channel_id=1, source_target_pairs={{0,3},{1,0},{2,1},{3,2},{4,7},{5,4},{6,5},{7,6},{8,11},{9,8},{10,9... | collective-permute-start | bytes 983048 | tf_op jit(solution)/shard_map/ppermute | solution.py:41
  20.0 3.0 %collective-permute-done.3 = bf16[32,4224]{1,0:T(8,128)(2,1)S(1)} collective-permute-done((bf16[32,4224]{1,0:T(8,128)(2,1)}, bf16[32,4224]{1,0:T(8,128)(2,1)S(1)}, u32[]{:S(2)}, u32[]{:S(2)}) %collective-permute-start.3) | collective-permute-done | bytes 270368 | tf_op jit(solution)/shard_map/ppermute | solution.py:41
  23.0 3.7 %collective-permute-done.2 = bf16[32,4224]{1,0:T(8,128)(2,1)S(1)} collective-permute-done((bf16[32,4224]{1,0:T(8,128)(2,1)}, bf16[32,4224]{1,0:T(8,128)(2,1)S(1)}, u32[]{:S(2)}, u32[]{:S(2)}) %collective-permute-start.2) | collective-permute-done | bytes 270368 | tf_op jit(solution)/shard_map/ppermute | solution.py:41
  26.6 0.9 %collective-permute-done.1 = bf16[32,4224]{1,0:T(8,128)(2,1)S(1)} collective-permute-done((bf16[32,4224]{1,0:T(8,128)(2,1)}, bf16[32,4224]{1,0:T(8,128)(2,1)S(1)}, u32[]{:S(2)}, u32[]{:S(2)}) %collective-permute-start.1) | collective-permute-done | bytes 270368 | tf_op jit(solution)/shard_map/ppermute | solution.py:41
  27.6 0.1 pad_maximum_fusion.mine
  27.6 0.0 copy-start.2
  27.7 1.0 %collective-permute-done.4.py1 = bf16[8,160,128]{2,1,0:T(8,128)(2,1)S(1)} collective-permute-done((bf16[8,160,128]{2,1,0:T(8,128)(2,1)S(1)}, bf16[8,160,128]{2,1,0:T(8,128)(2,1)S(1)}, u32[]{:S(2)}, u32[]{:S(2)}) %collective-permute-start.4) | collective-permute-done | bytes 327712 | tf_op jit(solution)/shard_map/ppermute | solution.py:41
  28.7 2.2 %collective-permute-start.8 = (bf16[4,160,128]{2,1,0:T(8,128)(2,1)S(1)}, bf16[4,160,128]{2,1,0:T(8,128)(2,1)S(1)}, u32[]{:S(2)}, u32[]{:S(2)}) collective-permute-start(bf16[4,160,128]{2,1,0:T(8,128)(2,1)S(1)} %slice.7), channel_id=1, source_target_pairs={{0,3},{1,0},{2,1},{3,2},{4,7},{5,4},{6,5},{7,6},{8,11},{9,8},{10,9... | collective-permute-start | bytes 491528 | tf_op jit(solution)/shard_map/ppermute | solution.py:41
  30.9 0.1 collective-permute-done.6.other
  31.0 1.3 %turn.1 = (f32[2,64,80,128]{3,2,1,0:T(8,128)S(1)}, f32[2,8,128]{2,1,0:T(8,128)S(1)}) custom-call(bf16[32,4224]{1,0:T(8,128)(2,1)S(1)} %copy-done, bf16[32,4224]{1,0:T(8,128)(2,1)S(1)} %collective-permute-done.own_other, bf16[96,4224]{1,0:T(8,128)(2,1)S(1)} %pad_maximum_fusion.mine, bf16[96,4224]{1,0:T(8,128)(2,1)S(1)} %collective-permute-done.6.other), custom_call_target="tpu_custom_call" | custom-call | bytes 8000 | tf_op jit(solution)/shard_map/turn/pallas_call | solution.py:402
  32.3 4.6 %first.1 = (f32[11,160,256]{2,1,0:T(8,128)S(1)}, f32[160,128]{1,0:T(8,128)S(1)}) custom-call(s32[2,11]{1,0:T(2,128)S(1)} %bitcast.7, f32[2,64,80,128]{3,2,1,0:T(8,128)S(1)} %get-tuple-element.30.t_ref, bf16[8,160,128]{2,1,0:T(8,128)(2,1)S(1)} %all-to-all-done.pc, bf16[8,160,128]{2,1,0:T(8,128)(2,1)S(1)} %collective-permute-done.4.py1, ...), custom_call_target="tpu_custom_call" | custom-call | flops 3000 | bytes 4000 | tf_op jit(solution)/shard_map/first/pallas_call | solution.py:419
  37.0 1.4 %collective-permute-done.7.pw0 = bf16[4,160,128]{2,1,0:T(8,128)(2,1)S(1)} collective-permute-done((bf16[4,160,128]{2,1,0:T(8,128)(2,1)S(1)}, bf16[4,160,128]{2,1,0:T(8,128)(2,1)S(1)}, u32[]{:S(2)}, u32[]{:S(2)}) %collective-permute-start.7) | collective-permute-done | bytes 163872 | tf_op jit(solution)/shard_map/ppermute | solution.py:41
  38.4 2.4 %last.1 = (f32[11,160,256]{2,1,0:T(8,128)S(1)}, f32[8,8,128]{2,1,0:T(8,128)S(1)}) custom-call(s32[2,11]{1,0:T(2,128)S(1)} %bitcast.8, f32[2,64,80,128]{3,2,1,0:T(8,128)S(1)} %get-tuple-element.30.t_ref, bf16[4,160,128]{2,1,0:T(8,128)(2,1)S(1)} %collective-permute-done.7.pw0, ...), custom_call_target="tpu_custom_call", output_to_operand_aliasing={{0}: (4, {})} | custom-call | flops 1000 | bytes 8000 | tf_op jit(solution)/shard_map/last/pallas_call | solution.py:429
  40.9 8.3 %all_to_all.15.all_ref = f32[8,8,128]{2,1,0:T(8,128)S(1)} all-to-all(f32[8,8,128]{2,1,0:T(8,128)S(1)} %get-tuple-element.38.st_ref), channel_id=1, replica_groups={{0,32,16,48,64,96,80,112},{1,33,17,49,65,97,81,113},{2,34,18,50,66,98,8..., dimensions={0} | all-to-all | bytes 65536 | tf_op jit(solution)/shard_map/all_to_all | solution.py:439
  49.2 3.2 %far.1 = (bf16[8,160,128]{2,1,0:T(8,128)(2,1)S(1)}, f32[1,32]{1,0:T(1,128)}, bf16[2816,160]{1,0:T(8,128)(2,1)S(1)}, bf16[16,128]{1,0:T(8,128)(2,1)S(1)}) custom-call(s32[2,11]{1,0:T(2,128)S(1)} %bitcast.9, f32[11,160,256]{2,1,0:T(8,128)S(1)} %get-tuple-element.37.e_ref, f32[8,8,128]{2,1,0:T(8,128)S(1)} %get-tuple-element.38.st_ref, ...), custom_call_target="tpu_custom_call" | custom-call | flops 1000 | bytes 4000 | tf_op jit(solution)/shard_map/far/pallas_call | solution.py:441
  52.3 0.9 %collective-permute-start.9 = (bf16[8,160,128]{2,1,0:T(8,128)(2,1)S(1)}, bf16[8,160,128]{2,1,0:T(8,128)(2,1)S(1)}, u32[]{:S(2)}, u32[]{:S(2)}) collective-permute-start(bf16[8,160,128]{2,1,0:T(8,128)(2,1)S(1)} %get-tuple-element.42), channel_id=1, source_target_pairs={{0,2},{1,3},{2,0},{3,1},{4,6},{5,7},{6,4},{7,5},{8,10},{9,11},{10,... | collective-permute-start | bytes 983048 | tf_op jit(solution)/shard_map/ppermute | solution.py:41
  53.2 3.8 %near.1 = (bf16[8,160,128]{2,1,0:T(8,128)(2,1)S(1)}, bf16[8,160,128]{2,1,0:T(8,128)(2,1)S(1)}) custom-call(s32[2,11]{1,0:T(2,128)S(1)} %bitcast.10, bf16[2816,160]{1,0:T(8,128)(2,1)S(1)} %get-tuple-element.39.w_ref, bf16[16,128]{1,0:T(8,128)(2,1)S(1)} %get-tuple-element.40.tail_ref, f32[2,64,80,128]{3,2,1,0:T(8,128)S(1)} %get-tuple-element.30.t_ref), custom_call_target="tpu_custom_call" | custom-call | flops 2000 | bytes 4000 | tf_op jit(solution)/shard_map/near/pallas_call | solution.py:456
  57.0 1.6 %collective-permute-start.11 = (bf16[8,160,128]{2,1,0:T(8,128)(2,1)S(1)}, bf16[8,160,128]{2,1,0:T(8,128)(2,1)S(1)}, u32[]{:S(2)}, u32[]{:S(2)}) collective-permute-start(bf16[8,160,128]{2,1,0:T(8,128)(2,1)S(1)} %get-tuple-element.43), channel_id=1, source_target_pairs={{0,3},{1,0},{2,1},{3,2},{4,7},{5,4},{6,5},{7,6},{8,11},{9,8},{10,9... | collective-permute-start | bytes 983048 | tf_op jit(solution)/shard_map/ppermute | solution.py:41
  58.6 0.5 collective-permute-start.10
  59.1 2.3 %own.1.own_ref = f32[8,160,128]{2,1,0:T(8,128)S(1)} custom-call(s32[2,11]{1,0:T(2,128)S(1)} %bitcast.11, bf16[2816,160]{1,0:T(8,128)(2,1)S(1)} %get-tuple-element.39.w_ref, f32[2,64,80,128]{3,2,1,0:T(8,128)S(1)} %get-tuple-element.30.t_ref, bf16[8,160,128]{2,1,0:T(8,128)(2,1)S(1)} %get-tuple-element.41.after_ref), custom_call_target="tpu_custom_call" | custom-call | flops 1000 | bytes 4000 | tf_op jit(solution)/shard_map/own/pallas_call | solution.py:467
  61.4 3.0 %collective-permute-done.9.far_ref = bf16[8,160,128]{2,1,0:T(8,128)(2,1)S(1)} collective-permute-done((bf16[8,160,128]{2,1,0:T(8,128)(2,1)S(1)}, bf16[8,160,128]{2,1,0:T(8,128)(2,1)S(1)}, u32[]{:S(2)}, u32[]{:S(2)}) %collective-permute-start.9) | collective-permute-done | bytes 327712 | tf_op jit(solution)/shard_map/ppermute | solution.py:41
  64.5 4.9 %collective-permute-done.11.down_ref = bf16[8,160,128]{2,1,0:T(8,128)(2,1)S(1)} collective-permute-done((bf16[8,160,128]{2,1,0:T(8,128)(2,1)S(1)}, bf16[8,160,128]{2,1,0:T(8,128)(2,1)S(1)}, u32[]{:S(2)}, u32[]{:S(2)}) %collective-permute-start.11) | collective-permute-done | bytes 327712 | tf_op jit(solution)/shard_map/ppermute | solution.py:41
  69.4 0.9 %collective-permute-done.10.up_ref = bf16[8,160,128]{2,1,0:T(8,128)(2,1)S(1)} collective-permute-done((bf16[8,160,128]{2,1,0:T(8,128)(2,1)S(1)}, bf16[8,160,128]{2,1,0:T(8,128)(2,1)S(1)}, u32[]{:S(2)}, u32[]{:S(2)}) %collective-permute-start.10) | collective-permute-done | bytes 327712 | tf_op jit(solution)/shard_map/ppermute | solution.py:41
  70.3 0.2 add.1
  70.4 11.9 %all_to_all.16.in_ref = bf16[8,160,128]{2,1,0:T(8,128)(2,1)S(1)} all-to-all(bf16[8,160,128]{2,1,0:T(8,128)(2,1)S(1)} %add.1), channel_id=1, replica_groups={{0,4,8,12,16,20,24,28},{1,5,9,13,17,21,25,29},{2,6,10,14,18,22,26,30},{..., dimensions={0} | all-to-all | bytes 655360 | tf_op jit(solution)/shard_map/all_to_all | solution.py:485
  82.3 0.7 finish.1
  (14 shorter events, 0.1 us)
Async XLA Ops:
  2.7 28.3 %copy-start = (bf16[32,4224]{1,0:T(8,128)(2,1)S(1)}, bf16[32,4224]{1,0:T(8,128)(2,1)}, u32[]{:S(2)}) copy-start(bf16[32,4224]{1,0:T(8,128)(2,1)} %get-tuple-element.25.own) | copy-start | bytes 811012
  2.7 14.3 %all-to-all-start = ((bf16[8,160,128]{2,1,0:T(8,128)(2,1)}), bf16[8,160,128]{2,1,0:T(8,128)(2,1)S(1)}, u32[]{:S(2)}, u32[]{:S(2)}) async-start(bf16[8,160,128]{2,1,0:T(8,128)(2,1)} %get-tuple-element.26), calls=%async_computation | async-start | bytes 655360 | tf_op jit(solution)/shard_map/all_to_all | solution.py:392
  9.1 4.8 %collective-permute-start = (bf16[32,4224]{1,0:T(8,128)(2,1)}, bf16[32,4224]{1,0:T(8,128)(2,1)S(1)}, u32[]{:S(2)}, u32[]{:S(2)}) collective-permute-start(bf16[32,4224]{1,0:T(8,128)(2,1)} %get-tuple-element.25.own), channel_id=1, source_target_pairs={{0,32},{1,33},{2,34},{3,35},{4,36},{5,37},{6,38},{7,39},{8,40},{9,... | collective-permute-start | bytes 811016 | tf_op jit(solution)/shard_map/ppermute | solution.py:41
  9.2 13.8 %collective-permute-start.3 = (bf16[32,4224]{1,0:T(8,128)(2,1)}, bf16[32,4224]{1,0:T(8,128)(2,1)S(1)}, u32[]{:S(2)}, u32[]{:S(2)}) collective-permute-start(bf16[32,4224]{1,0:T(8,128)(2,1)} %get-tuple-element.25.own), channel_id=1, source_target_pairs={{0,64},{1,65},{2,66},{3,67},{4,68},{5,69},{6,70},{7,71},{8,72},{9,... | collective-permute-start | bytes 811016 | tf_op jit(solution)/shard_map/ppermute | solution.py:41
  12.0 14.7 %collective-permute-start.2 = (bf16[32,4224]{1,0:T(8,128)(2,1)}, bf16[32,4224]{1,0:T(8,128)(2,1)S(1)}, u32[]{:S(2)}, u32[]{:S(2)}) collective-permute-start(bf16[32,4224]{1,0:T(8,128)(2,1)} %get-tuple-element.25.own), channel_id=1, source_target_pairs={{0,80},{1,81},{2,82},{3,83},{4,84},{5,85},{6,86},{7,87},{8,88},{9,... | collective-permute-start | bytes 811016 | tf_op jit(solution)/shard_map/ppermute | solution.py:41
  13.8 13.7 %collective-permute-start.1 = (bf16[32,4224]{1,0:T(8,128)(2,1)}, bf16[32,4224]{1,0:T(8,128)(2,1)S(1)}, u32[]{:S(2)}, u32[]{:S(2)}) collective-permute-start(bf16[32,4224]{1,0:T(8,128)(2,1)} %get-tuple-element.25.own), channel_id=1, source_target_pairs={{0,16},{1,17},{2,18},{3,19},{4,20},{5,21},{6,22},{7,23},{8,24},{9,... | collective-permute-start | bytes 811016 | tf_op jit(solution)/shard_map/ppermute | solution.py:41
  17.0 10.7 %collective-permute-start.5 = (bf16[8,160,128]{2,1,0:T(8,128)(2,1)S(1)}, bf16[8,160,128]{2,1,0:T(8,128)(2,1)S(1)}, u32[]{:S(2)}, u32[]{:S(2)}) collective-permute-start(bf16[8,160,128]{2,1,0:T(8,128)(2,1)S(1)} %all-to-all-done.pc), channel_id=1, source_target_pairs={{0,3},{1,0},{2,1},{3,2},{4,7},{5,4},{6,5},{7,6},{8,11},{9,8},{10,9... | collective-permute-start | bytes 983048 | tf_op jit(solution)/shard_map/ppermute | solution.py:41
  20.0 8.7 %collective-permute-start.4 = (bf16[8,160,128]{2,1,0:T(8,128)(2,1)S(1)}, bf16[8,160,128]{2,1,0:T(8,128)(2,1)S(1)}, u32[]{:S(2)}, u32[]{:S(2)}) collective-permute-start(bf16[8,160,128]{2,1,0:T(8,128)(2,1)S(1)} %all-to-all-done.pc), channel_id=1, source_target_pairs={{0,1},{1,2},{2,3},{3,0},{4,5},{5,6},{6,7},{7,4},{8,9},{9,10},{10,1... | collective-permute-start | bytes 983048 | tf_op jit(solution)/shard_map/ppermute | solution.py:41
  27.6 4.7 %copy-start.2 = (s32[11,2]{0,1:T(2,128)S(1)}, s32[11,2]{0,1:T(2,128)}, u32[]{:S(2)}) copy-start(s32[11,2]{0,1:T(2,128)} %param.9) | copy-start | bytes 268
  28.7 2.3 %collective-permute-start.6 = (bf16[96,4224]{1,0:T(8,128)(2,1)S(1)}, bf16[96,4224]{1,0:T(8,128)(2,1)S(1)}, u32[]{:S(2)}, u32[]{:S(2)}) collective-permute-start(bf16[96,4224]{1,0:T(8,128)(2,1)S(1)} %pad_maximum_fusion.mine), channel_id=1, source_target_pairs={{0,32},{1,33},{2,34},{3,35},{4,36},{5,37},{6,38},{7,39},{8,40},{9,... | collective-permute-start | bytes 2433032 | tf_op jit(solution)/shard_map/ppermute | solution.py:41
  28.7 8.3 %collective-permute-start.8 = (bf16[4,160,128]{2,1,0:T(8,128)(2,1)S(1)}, bf16[4,160,128]{2,1,0:T(8,128)(2,1)S(1)}, u32[]{:S(2)}, u32[]{:S(2)}) collective-permute-start(bf16[4,160,128]{2,1,0:T(8,128)(2,1)S(1)} %slice.7), channel_id=1, source_target_pairs={{0,3},{1,0},{2,1},{3,2},{4,7},{5,4},{6,5},{7,6},{8,11},{9,8},{10,9... | collective-permute-start | bytes 491528 | tf_op jit(solution)/shard_map/ppermute | solution.py:41
  30.9 7.5 %collective-permute-start.7 = (bf16[4,160,128]{2,1,0:T(8,128)(2,1)S(1)}, bf16[4,160,128]{2,1,0:T(8,128)(2,1)S(1)}, u32[]{:S(2)}, u32[]{:S(2)}) collective-permute-start(bf16[4,160,128]{2,1,0:T(8,128)(2,1)S(1)} %slice.6), channel_id=1, source_target_pairs={{0,1},{1,2},{2,3},{3,0},{4,5},{5,6},{6,7},{7,4},{8,9},{9,10},{10,1... | collective-permute-start | bytes 491528 | tf_op jit(solution)/shard_map/ppermute | solution.py:41
  32.3 6.1 %copy-start.1 = (f32[160,128]{1,0:T(8,128)S(1)}, f32[160,128]{1,0:T(8,128)}, u32[]{:S(2)}) copy-start(f32[160,128]{1,0:T(8,128)} %get-tuple-element.36.info_ref) | copy-start | bytes 245764
  52.3 12.1 %collective-permute-start.9 = (bf16[8,160,128]{2,1,0:T(8,128)(2,1)S(1)}, bf16[8,160,128]{2,1,0:T(8,128)(2,1)S(1)}, u32[]{:S(2)}, u32[]{:S(2)}) collective-permute-start(bf16[8,160,128]{2,1,0:T(8,128)(2,1)S(1)} %get-tuple-element.42), channel_id=1, source_target_pairs={{0,2},{1,3},{2,0},{3,1},{4,6},{5,7},{6,4},{7,5},{8,10},{9,11},{10,... | collective-permute-start | bytes 983048 | tf_op jit(solution)/shard_map/ppermute | solution.py:41
  57.0 12.4 %collective-permute-start.11 = (bf16[8,160,128]{2,1,0:T(8,128)(2,1)S(1)}, bf16[8,160,128]{2,1,0:T(8,128)(2,1)S(1)}, u32[]{:S(2)}, u32[]{:S(2)}) collective-permute-start(bf16[8,160,128]{2,1,0:T(8,128)(2,1)S(1)} %get-tuple-element.43), channel_id=1, source_target_pairs={{0,3},{1,0},{2,1},{3,2},{4,7},{5,4},{6,5},{7,6},{8,11},{9,8},{10,9... | collective-permute-start | bytes 983048 | tf_op jit(solution)/shard_map/ppermute | solution.py:41
  58.6 11.7 %collective-permute-start.10 = (bf16[8,160,128]{2,1,0:T(8,128)(2,1)S(1)}, bf16[8,160,128]{2,1,0:T(8,128)(2,1)S(1)}, u32[]{:S(2)}, u32[]{:S(2)}) collective-permute-start(bf16[8,160,128]{2,1,0:T(8,128)(2,1)S(1)} %get-tuple-element.41.after_ref), channel_id=1, source_target_pairs={{0,1},{1,2},{2,3},{3,0},{4,5},{5,6},{6,7},{7,4},{8,9},{9,10},{10,1... | collective-permute-start | bytes 983048 | tf_op jit(solution)/shard_map/ppermute | solution.py:41

commit v5 on v4

--- a/solution.py
+++ b/solution.py
@@ -57,8 +57,8 @@
 
 
 def prepare_kernel(*refs):
-    sources, (send_ref, out_ref, info_ref) = refs[:4], refs[4:7]
-    targets, half_ref, sems = refs[7:11], refs[11], refs[12]
+    sources, (send_out, image_out, info_out) = refs[:4], refs[4:7]
+    targets, (half_ref, send_ref, out_ref, info_ref, sems, out_sems) = refs[7:11], refs[11:]
     p_ref, x_ref, rot_ref, log_ref = targets
     _, _, x_lo, _, _ = position()
     copies = [
@@ -66,8 +66,7 @@
     ]
     for copy in copies:
         copy.start()
-    for copy in copies:
-        copy.wait()
+    copies[0].wait()
     for r in range(ROT):
         half, at = r // HALF_ROT, (r % HALF_ROT) * CLS
         half_ref[half, at : at + CLS, :] = p_ref[r].astype(jnp.float32)
@@ -77,10 +76,16 @@
         value = half_ref[half].astype(jnp.bfloat16)
         for k in range(4):
             send_ref[4 * half + k] = value
+    sent = [pltpu.make_async_copy(send_ref, send_out, out_sems.at[0])]
+    sent[0].start()
+    for copy in copies[1:]:
+        copy.wait()
     out_ref[:, 0:PIX] = x_ref[...].astype(jnp.bfloat16)
     rots = rot_ref[...].astype(jnp.float32)
     rots = jnp.concatenate([rots] * (LANES // OWN), axis=1)
     out_ref[:, PIX : PIX + LANES] = jnp.broadcast_to(rots, (OWN, LANES)).astype(jnp.bfloat16)
+    sent.append(pltpu.make_async_copy(out_ref, image_out, out_sems.at[1]))
+    sent[1].start()
     diagonal = lax.broadcasted_iota(jnp.int32, (CLS, CLS), 0) == lax.broadcasted_iota(
         jnp.int32, (CLS, CLS), 1
     )
@@ -92,6 +97,10 @@
         rows = jnp.where(lane == 1, math.cos(turn) * sign, math.sin(turn) * sign)
         info_ref[r * CLS : (r + 1) * CLS, :] = jnp.where(lane == 0, logs, rows)
     info_ref[USED:ROWS, :] = jnp.full((ROWS - USED, LANES), NEG, jnp.float32)
+    sent.append(pltpu.make_async_copy(info_ref, info_out, out_sems.at[2]))
+    sent[2].start()
+    for copy in sent:
+        copy.wait()
 
 
 def turn_kernel(own, own_other, mine, other, t_ref, rot_ref, x_ref):
@@ -172,7 +181,7 @@
     lax.fori_loop(0, SHIFTS, one_shift, 0, unroll=True)
 
 
-def last_kernel(shift_ref, t_ref, pw0, pw1, s_in, n_in, rot_ref, info_ref, e_ref, st_ref):
+def last_kernel(shift_ref, t_ref, pw0, pw1, s_in, n_in, rot_ref, info_ref, e_ref, st_ref, m_ref):
     gain = SCORE_GAIN / math.sqrt(PIX)
     pairs = pairs_of(((pw0, pw1),), (2,))
     norms = jnp.sum(n_in[...] + squares_of(pairs), axis=1, keepdims=True)
@@ -184,23 +193,21 @@
     is_panel = lax.broadcasted_iota(jnp.int32, (ROWS, 1), 0) < USED
     bias = jnp.where(is_panel, bias, NEG)
 
-    def one_shift(s, peak):
+    peaks, sums = [], []
+    for s in range(SHIFTS):
         scores = gain * (s_in[s] + add_scores(shift_ref, t_ref, pairs, s)) + bias
-        e_ref[s] = scores
-        return jnp.maximum(peak, jnp.max(scores, axis=0, keepdims=True))
-
-    peak = lax.fori_loop(
-        0, SHIFTS, one_shift, jnp.full((1, ROW_IMAGES), NEG, jnp.float32), unroll=True
-    )
-
-    def one_exp(s, total):
-        value = jnp.exp(e_ref[s] - peak)
+        peaks.append(jnp.max(scores, axis=0, keepdims=True))
+        value = jnp.exp(scores - peaks[s])
         e_ref[s] = value
-        return total + jnp.sum(value, axis=0, keepdims=True)
-
-    total = lax.fori_loop(
-        0, SHIFTS, one_exp, jnp.zeros((1, ROW_IMAGES), jnp.float32), unroll=True
-    )
+        sums.append(jnp.sum(value, axis=0, keepdims=True))
+        m_ref[s : s + 1, :] = peaks[s]
+    m_ref[SHIFTS:16, :] = jnp.zeros((16 - SHIFTS, ROW_IMAGES), jnp.float32)
+    peak = peaks[0]
+    for s in range(1, SHIFTS):
+        peak = jnp.maximum(peak, peaks[s])
+    total = jnp.zeros((1, ROW_IMAGES), jnp.float32)
+    for s in range(SHIFTS):
+        total = total + sums[s] * jnp.exp(peaks[s] - peak)
     stats = jnp.concatenate(
         [
             peak[:, :LANES],
@@ -215,7 +222,7 @@
         st_ref[k] = stats
 
 
-def far_kernel(shift_ref, e_ref, st_ref, all_ref, t_ref, out_ref, ev_ref, w_ref, tail_ref):
+def far_kernel(shift_ref, e_ref, m_ref, all_ref, t_ref, out_ref, ev_ref, w_ref, tail_ref):
     x, core, _, _, _ = position()
     stats = [all_ref[k] for k in range(8)]
     peak = stats[0][0:2]
@@ -233,10 +240,11 @@
     for k in range(1, 4):
         picked = jnp.where(at == k, groups[k], picked)
     ev_ref[...] = picked
-    factor = jnp.exp(st_ref[0][0:2] - peak) / total
-    factor = jnp.concatenate([factor[0:1], factor[1:2]], axis=1)
+    peak = jnp.concatenate([peak[0:1], peak[1:2]], axis=1)
+    total = jnp.concatenate([total[0:1], total[1:2]], axis=1)
 
     for s in range(SHIFTS):
+        factor = jnp.exp(m_ref[s : s + 1, :] - peak) / total
         weight = (e_ref[s] * factor).astype(jnp.bfloat16)
         w_ref[s * ROW_IMAGES : (s + 1) * ROW_IMAGES, :] = weight.T
 
@@ -253,9 +261,9 @@
 GROUP = 4
 
 
-def tile_sums(shift_ref, t_ref, w_ref, z, y):
+def tile_sums(shift_ref, t_ref, w_ref, z, *ys):
     tiles = []
-    for k in range(GROUP):
+    for y, k in [(y, k) for y in ys for k in range(GROUP)]:
         low = 2 * (4 * (z + k) + y)
         rows = (low, low + 1, low + 2 * 16, low + 2 * 16 + 1)
         tiles.append(
@@ -287,11 +295,12 @@
 
 def near_kernel(shift_ref, w_ref, tail_ref, t_ref, up_ref, down_ref):
     y = position()[4]
-    for step, out_ref in ((1, up_ref), (-1, down_ref)):
-        for z in range(0, 4, GROUP):
-            at = jnp.bitwise_and(y + step, 3)
-            acc = tile_sums(shift_ref, t_ref, w_ref, z, at)
-            store_sums(out_ref, z, acc, tail_ref[...])
+    ahead, behind = jnp.bitwise_and(y + 1, 3), jnp.bitwise_and(y - 1, 3)
+    size = 2 * LANES * GROUP
+    for z in range(0, 4, GROUP):
+        acc = tile_sums(shift_ref, t_ref, w_ref, z, ahead, behind)
+        store_sums(up_ref, z, acc[:size], tail_ref[...])
+        store_sums(down_ref, z, acc[size:], tail_ref[...])
 
 
 def own_kernel(shift_ref, w_ref, t_ref, after_ref, out_ref):
@@ -367,14 +376,18 @@
             jax.ShapeDtypeStruct((ROWS, LANES), jnp.float32),
         ),
         in_specs=[pl.BlockSpec(memory_space=pltpu.HBM)] * 4,
-        out_specs=(VMEM,) * 3,
+        out_specs=(pl.BlockSpec(memory_space=pltpu.HBM),) * 3,
         scratch_shapes=[
             pltpu.VMEM((ROT, CLS, LANES), jnp.bfloat16),
             pltpu.VMEM((OWN, PIX), jnp.float32),
             pltpu.VMEM((1, OWN), jnp.int32),
             pltpu.VMEM((1, CLS), jnp.float32),
             pltpu.VMEM((2, ROWS, LANES), jnp.float32),
+            pltpu.VMEM((8, ROWS, LANES), jnp.bfloat16),
+            pltpu.VMEM((OWN, PIX + LANES), jnp.bfloat16),
+            pltpu.VMEM((ROWS, LANES), jnp.float32),
             pltpu.SemaphoreType.DMA((4,)),
+            pltpu.SemaphoreType.DMA((3,)),
         ],
         compiler_params=pltpu.CompilerParams(vmem_limit_bytes=60 * 1024 * 1024),
         cost_estimate=cost(0, 1),
@@ -426,11 +439,15 @@
         name="first",
     )(shifts, turned, column, y1, y3)
 
-    scores, stats = pl.pallas_call(
+    scores, stats, peaks = pl.pallas_call(
         last_kernel,
-        out_shape=(score_shape, jax.ShapeDtypeStruct((8, 8, LANES), jnp.float32)),
+        out_shape=(
+            score_shape,
+            jax.ShapeDtypeStruct((8, 8, LANES), jnp.float32),
+            jax.ShapeDtypeStruct((16, ROW_IMAGES), jnp.float32),
+        ),
         in_specs=[SMEM] + [VMEM] * 7,
-        out_specs=(VMEM, VMEM),
+        out_specs=(VMEM,) * 3,
         input_output_aliases={4: 0},
         compiler_params=PARAMS,
         cost_estimate=cost(1, 8),
@@ -451,7 +468,7 @@
         compiler_params=PARAMS,
         cost_estimate=cost(1, 4),
         name="far",
-    )(shifts, scores, stats, all_stats, turned)
+    )(shifts, scores, peaks, all_stats, turned)
     from_far = move(far, y=2)
     up, down = pl.pallas_call(
         near_kernel,

time: 83.3 us -> 83.2 us (level)
  no operation moved by 1% of the time
where the time goes in v5:
time: 83.2 us; the launch traced here: 82.9 us
  waiting for transfers between devices  21.5 us (26%)
  Pallas kernels  21 us (25%)
  blocking collectives  20.1 us (24%)
  starting transfers between devices  19.4 us (23%)
    ppermute x12, waiting for transfers between devices, move(): return lax.ppermute(value, AXES, route)  18.5 us
    ppermute x12, starting transfers between devices, move(): return lax.ppermute(value, AXES, route)  12.9 us
    all_to_all x1, blocking collectives, shards(): lax.all_to_all(column_sums, 'img', 0, 0, axis_index_groups=XZ_GROUPS)  11.8 us
    all_to_all x1, blocking collectives, shards(): all_stats = lax.all_to_all(stats, AXES, 0, 0, axis_index_groups=X_ROWS)  8.31 us
    all_to_all x1, starting transfers between devices, shards(): column = lax.all_to_all(spread, 'img', 0, 0, axis_index_groups=XZ_GROUPS)  6.47 us
    pallas_call x1, Pallas kernels, shards(): pl.pallas_call(first_kernel, out_shape=(score_shape, norm_shape), in_spec...  4.59 us
    pallas_call x1, Pallas kernels, shards(): pl.pallas_call(near_kernel, out_shape=(block_shape,) * 2, in_specs=[SMEM]...  4.32 us
    pallas_call x1, Pallas kernels, shards(): pl.pallas_call(far_kernel, out_shape=(block_shape, jax.ShapeDtypeStruct((...  3.2 us
  transfers between devices with their start and end apart: 13, of which 10 were waited for; matrix products, arithmetic and copies ran while one was open for 0% of the time, Pallas kernels for 15%

profile of v5, /device:TPU:0, one launch (start us, length us, event | category | flops | bytes accessed | tf_op | source)
XLA Modules:
  0.0 82.9 jit_solution(4894390058671996482)
XLA Ops:
  0.6 2.0 %prepare.1 = (bf16[8,160,128]{2,1,0:T(8,128)(2,1)}, bf16[32,4224]{1,0:T(8,128)(2,1)}, f32[160,128]{1,0:T(8,128)}) custom-call(bf16[12,25,128]{2,1,0:T(8,128)(2,1)} %bitcast.12, f32[32,4096]{1,0:T(8,128)} %refs_1_.1, s32[1,32]{1,0:T(1,128)} %bitcast.13, f32[1,25]{1,0:T(1,128)} %bitcast.14), custom_call_target="tpu_custom_call" | custom-call | bytes 1000 | tf_op jit(solution)/shard_map/prepare/pallas_call | solution.py:371
  2.6 6.5 %all-to-all-start = ((bf16[8,160,128]{2,1,0:T(8,128)(2,1)}), bf16[8,160,128]{2,1,0:T(8,128)(2,1)S(1)}, u32[]{:S(2)}, u32[]{:S(2)}) async-start(bf16[8,160,128]{2,1,0:T(8,128)(2,1)} %get-tuple-element.27), calls=%async_computation | async-start | bytes 655360 | tf_op jit(solution)/shard_map/all_to_all | solution.py:405
  9.1 2.8 %collective-permute-start.3 = (bf16[32,4224]{1,0:T(8,128)(2,1)}, bf16[32,4224]{1,0:T(8,128)(2,1)S(1)}, u32[]{:S(2)}, u32[]{:S(2)}) collective-permute-start(bf16[32,4224]{1,0:T(8,128)(2,1)} %get-tuple-element.26.own), channel_id=1, source_target_pairs={{0,64},{1,65},{2,66},{3,67},{4,68},{5,69},{6,70},{7,71},{8,72},{9,... | collective-permute-start | bytes 811016 | tf_op jit(solution)/shard_map/ppermute | solution.py:41
  11.9 1.9 %collective-permute-start.2 = (bf16[32,4224]{1,0:T(8,128)(2,1)}, bf16[32,4224]{1,0:T(8,128)(2,1)S(1)}, u32[]{:S(2)}, u32[]{:S(2)}) collective-permute-start(bf16[32,4224]{1,0:T(8,128)(2,1)} %get-tuple-element.26.own), channel_id=1, source_target_pairs={{0,80},{1,81},{2,82},{3,83},{4,84},{5,85},{6,86},{7,87},{8,88},{9,... | collective-permute-start | bytes 811016 | tf_op jit(solution)/shard_map/ppermute | solution.py:41
  13.8 0.1 collective-permute-start.1
  13.9 3.0 %all-to-all-done.pc = bf16[8,160,128]{2,1,0:T(8,128)(2,1)S(1)} async-done(((bf16[8,160,128]{2,1,0:T(8,128)(2,1)}), bf16[8,160,128]{2,1,0:T(8,128)(2,1)S(1)}, u32[]{:S(2)}, u32[]{:S(2)}) %all-to-all-start) | async-done | bytes 327712 | tf_op jit(solution)/shard_map/all_to_all | solution.py:405
  16.9 3.0 %collective-permute-start.5 = (bf16[8,160,128]{2,1,0:T(8,128)(2,1)S(1)}, bf16[8,160,128]{2,1,0:T(8,128)(2,1)S(1)}, u32[]{:S(2)}, u32[]{:S(2)}) collective-permute-start(bf16[8,160,128]{2,1,0:T(8,128)(2,1)S(1)} %all-to-all-done.pc), channel_id=1, source_target_pairs={{0,3},{1,0},{2,1},{3,2},{4,7},{5,4},{6,5},{7,6},{8,11},{9,8},{10,9... | collective-permute-start | bytes 983048 | tf_op jit(solution)/shard_map/ppermute | solution.py:41
  19.9 3.0 %collective-permute-done.3 = bf16[32,4224]{1,0:T(8,128)(2,1)S(1)} collective-permute-done((bf16[32,4224]{1,0:T(8,128)(2,1)}, bf16[32,4224]{1,0:T(8,128)(2,1)S(1)}, u32[]{:S(2)}, u32[]{:S(2)}) %collective-permute-start.3) | collective-permute-done | bytes 270368 | tf_op jit(solution)/shard_map/ppermute | solution.py:41
  22.9 3.7 %collective-permute-done.2 = bf16[32,4224]{1,0:T(8,128)(2,1)S(1)} collective-permute-done((bf16[32,4224]{1,0:T(8,128)(2,1)}, bf16[32,4224]{1,0:T(8,128)(2,1)S(1)}, u32[]{:S(2)}, u32[]{:S(2)}) %collective-permute-start.2) | collective-permute-done | bytes 270368 | tf_op jit(solution)/shard_map/ppermute | solution.py:41
  26.6 0.9 %collective-permute-done.1 = bf16[32,4224]{1,0:T(8,128)(2,1)S(1)} collective-permute-done((bf16[32,4224]{1,0:T(8,128)(2,1)}, bf16[32,4224]{1,0:T(8,128)(2,1)S(1)}, u32[]{:S(2)}, u32[]{:S(2)}) %collective-permute-start.1) | collective-permute-done | bytes 270368 | tf_op jit(solution)/shard_map/ppermute | solution.py:41
  27.5 0.1 pad_maximum_fusion.mine
  27.6 0.0 copy-start.2
  27.6 1.0 %collective-permute-done.4.py1 = bf16[8,160,128]{2,1,0:T(8,128)(2,1)S(1)} collective-permute-done((bf16[8,160,128]{2,1,0:T(8,128)(2,1)S(1)}, bf16[8,160,128]{2,1,0:T(8,128)(2,1)S(1)}, u32[]{:S(2)}, u32[]{:S(2)}) %collective-permute-start.4) | collective-permute-done | bytes 327712 | tf_op jit(solution)/shard_map/ppermute | solution.py:41
  28.7 2.2 %collective-permute-start.8 = (bf16[4,160,128]{2,1,0:T(8,128)(2,1)S(1)}, bf16[4,160,128]{2,1,0:T(8,128)(2,1)S(1)}, u32[]{:S(2)}, u32[]{:S(2)}) collective-permute-start(bf16[4,160,128]{2,1,0:T(8,128)(2,1)S(1)} %slice.7), channel_id=1, source_target_pairs={{0,3},{1,0},{2,1},{3,2},{4,7},{5,4},{6,5},{7,6},{8,11},{9,8},{10,9... | collective-permute-start | bytes 491528 | tf_op jit(solution)/shard_map/ppermute | solution.py:41
  30.8 0.1 collective-permute-done.6.other
  30.9 1.3 %turn.1 = (f32[2,64,80,128]{3,2,1,0:T(8,128)S(1)}, f32[2,8,128]{2,1,0:T(8,128)S(1)}) custom-call(bf16[32,4224]{1,0:T(8,128)(2,1)S(1)} %copy-done, bf16[32,4224]{1,0:T(8,128)(2,1)S(1)} %collective-permute-done.own_other, bf16[96,4224]{1,0:T(8,128)(2,1)S(1)} %pad_maximum_fusion.mine, bf16[96,4224]{1,0:T(8,128)(2,1)S(1)} %collective-permute-done.6.other), custom_call_target="tpu_custom_call" | custom-call | bytes 8000 | tf_op jit(solution)/shard_map/turn/pallas_call | solution.py:415
  32.3 4.6 %first.1 = (f32[11,160,256]{2,1,0:T(8,128)S(1)}, f32[160,128]{1,0:T(8,128)S(1)}) custom-call(s32[2,11]{1,0:T(2,128)S(1)} %bitcast.7, f32[2,64,80,128]{3,2,1,0:T(8,128)S(1)} %get-tuple-element.31.t_ref, bf16[8,160,128]{2,1,0:T(8,128)(2,1)S(1)} %all-to-all-done.pc, bf16[8,160,128]{2,1,0:T(8,128)(2,1)S(1)} %collective-permute-done.4.py1, ...), custom_call_target="tpu_custom_call" | custom-call | flops 3000 | bytes 4000 | tf_op jit(solution)/shard_map/first/pallas_call | solution.py:432
  36.9 1.5 %collective-permute-done.7.pw0 = bf16[4,160,128]{2,1,0:T(8,128)(2,1)S(1)} collective-permute-done((bf16[4,160,128]{2,1,0:T(8,128)(2,1)S(1)}, bf16[4,160,128]{2,1,0:T(8,128)(2,1)S(1)}, u32[]{:S(2)}, u32[]{:S(2)}) %collective-permute-start.7) | collective-permute-done | bytes 163872 | tf_op jit(solution)/shard_map/ppermute | solution.py:41
  38.4 2.4 %last.1 = (f32[11,160,256]{2,1,0:T(8,128)S(1)}, f32[8,8,128]{2,1,0:T(8,128)S(1)}, f32[16,256]{1,0:T(8,128)S(1)}) custom-call(s32[2,11]{1,0:T(2,128)S(1)} %bitcast.8, f32[2,64,80,128]{3,2,1,0:T(8,128)S(1)} %get-tuple-element.31.t_ref, bf16[4,160,128]{2,1,0:T(8,128)(2,1)S(1)} %collective-permute-done.7.pw0, ...), custom_call_target="tpu_custom_call", output_to_operand_aliasing={{0}: (4, {})} | custom-call | flops 1000 | bytes 8000 | tf_op jit(solution)/shard_map/last/pallas_call | solution.py:442
  40.8 8.3 %all_to_all.15.all_ref = f32[8,8,128]{2,1,0:T(8,128)S(1)} all-to-all(f32[8,8,128]{2,1,0:T(8,128)S(1)} %get-tuple-element.40), channel_id=1, replica_groups={{0,32,16,48,64,96,80,112},{1,33,17,49,65,97,81,113},{2,34,18,50,66,98,8..., dimensions={0} | all-to-all | bytes 65536 | tf_op jit(solution)/shard_map/all_to_all | solution.py:456
  49.1 3.2 %far.1 = (bf16[8,160,128]{2,1,0:T(8,128)(2,1)S(1)}, f32[1,32]{1,0:T(1,128)}, bf16[2816,160]{1,0:T(8,128)(2,1)S(1)}, bf16[16,128]{1,0:T(8,128)(2,1)S(1)}) custom-call(s32[2,11]{1,0:T(2,128)S(1)} %bitcast.9, f32[11,160,256]{2,1,0:T(8,128)S(1)} %get-tuple-element.38.e_ref, f32[16,256]{1,0:T(8,128)S(1)} %get-tuple-element.39.m_ref, ...), custom_call_target="tpu_custom_call" | custom-call | flops 1000 | bytes 4000 | tf_op jit(solution)/shard_map/far/pallas_call | solution.py:458
  52.3 0.8 collective-permute-start.9
  53.1 4.3 %near.1 = (bf16[8,160,128]{2,1,0:T(8,128)(2,1)S(1)}, bf16[8,160,128]{2,1,0:T(8,128)(2,1)S(1)}) custom-call(s32[2,11]{1,0:T(2,128)S(1)} %bitcast.10, bf16[2816,160]{1,0:T(8,128)(2,1)S(1)} %get-tuple-element.41.w_ref, bf16[16,128]{1,0:T(8,128)(2,1)S(1)} %get-tuple-element.42.tail_ref, f32[2,64,80,128]{3,2,1,0:T(8,128)S(1)} %get-tuple-element.31.t_ref), custom_call_target="tpu_custom_call" | custom-call | flops 2000 | bytes 4000 | tf_op jit(solution)/shard_map/near/pallas_call | solution.py:473
  57.4 1.6 %collective-permute-start.11 = (bf16[8,160,128]{2,1,0:T(8,128)(2,1)S(1)}, bf16[8,160,128]{2,1,0:T(8,128)(2,1)S(1)}, u32[]{:S(2)}, u32[]{:S(2)}) collective-permute-start(bf16[8,160,128]{2,1,0:T(8,128)(2,1)S(1)} %get-tuple-element.45), channel_id=1, source_target_pairs={{0,3},{1,0},{2,1},{3,2},{4,7},{5,4},{6,5},{7,6},{8,11},{9,8},{10,9... | collective-permute-start | bytes 983048 | tf_op jit(solution)/shard_map/ppermute | solution.py:41
  59.0 0.5 collective-permute-start.10
  59.5 2.4 %own.1.own_ref = f32[8,160,128]{2,1,0:T(8,128)S(1)} custom-call(s32[2,11]{1,0:T(2,128)S(1)} %bitcast.11, bf16[2816,160]{1,0:T(8,128)(2,1)S(1)} %get-tuple-element.41.w_ref, f32[2,64,80,128]{3,2,1,0:T(8,128)S(1)} %get-tuple-element.31.t_ref, bf16[8,160,128]{2,1,0:T(8,128)(2,1)S(1)} %get-tuple-element.43.after_ref), custom_call_target="tpu_custom_call" | custom-call | flops 1000 | bytes 4000 | tf_op jit(solution)/shard_map/own/pallas_call | solution.py:484
  61.9 2.4 %collective-permute-done.9.far_ref = bf16[8,160,128]{2,1,0:T(8,128)(2,1)S(1)} collective-permute-done((bf16[8,160,128]{2,1,0:T(8,128)(2,1)S(1)}, bf16[8,160,128]{2,1,0:T(8,128)(2,1)S(1)}, u32[]{:S(2)}, u32[]{:S(2)}) %collective-permute-start.9) | collective-permute-done | bytes 327712 | tf_op jit(solution)/shard_map/ppermute | solution.py:41
  64.3 4.9 %collective-permute-done.11.down_ref = bf16[8,160,128]{2,1,0:T(8,128)(2,1)S(1)} collective-permute-done((bf16[8,160,128]{2,1,0:T(8,128)(2,1)S(1)}, bf16[8,160,128]{2,1,0:T(8,128)(2,1)S(1)}, u32[]{:S(2)}, u32[]{:S(2)}) %collective-permute-start.11) | collective-permute-done | bytes 327712 | tf_op jit(solution)/shard_map/ppermute | solution.py:41
  69.2 1.0 %collective-permute-done.10.up_ref = bf16[8,160,128]{2,1,0:T(8,128)(2,1)S(1)} collective-permute-done((bf16[8,160,128]{2,1,0:T(8,128)(2,1)S(1)}, bf16[8,160,128]{2,1,0:T(8,128)(2,1)S(1)}, u32[]{:S(2)}, u32[]{:S(2)}) %collective-permute-start.10) | collective-permute-done | bytes 327712 | tf_op jit(solution)/shard_map/ppermute | solution.py:41
  70.2 0.2 add.1
  70.4 11.8 %all_to_all.16.in_ref = bf16[8,160,128]{2,1,0:T(8,128)(2,1)S(1)} all-to-all(bf16[8,160,128]{2,1,0:T(8,128)(2,1)S(1)} %add.1), channel_id=1, replica_groups={{0,4,8,12,16,20,24,28},{1,5,9,13,17,21,25,29},{2,6,10,14,18,22,26,30},{..., dimensions={0} | all-to-all | bytes 655360 | tf_op jit(solution)/shard_map/all_to_all | solution.py:502
  82.2 0.7 finish.1
  (14 shorter events, 0.1 us)
Async XLA Ops:
  2.6 28.3 %copy-start = (bf16[32,4224]{1,0:T(8,128)(2,1)S(1)}, bf16[32,4224]{1,0:T(8,128)(2,1)}, u32[]{:S(2)}) copy-start(bf16[32,4224]{1,0:T(8,128)(2,1)} %get-tuple-element.26.own) | copy-start | bytes 811012
  2.6 14.3 %all-to-all-start = ((bf16[8,160,128]{2,1,0:T(8,128)(2,1)}), bf16[8,160,128]{2,1,0:T(8,128)(2,1)S(1)}, u32[]{:S(2)}, u32[]{:S(2)}) async-start(bf16[8,160,128]{2,1,0:T(8,128)(2,1)} %get-tuple-element.27), calls=%async_computation | async-start | bytes 655360 | tf_op jit(solution)/shard_map/all_to_all | solution.py:405
  9.1 4.8 %collective-permute-start = (bf16[32,4224]{1,0:T(8,128)(2,1)}, bf16[32,4224]{1,0:T(8,128)(2,1)S(1)}, u32[]{:S(2)}, u32[]{:S(2)}) collective-permute-start(bf16[32,4224]{1,0:T(8,128)(2,1)} %get-tuple-element.26.own), channel_id=1, source_target_pairs={{0,32},{1,33},{2,34},{3,35},{4,36},{5,37},{6,38},{7,39},{8,40},{9,... | collective-permute-start | bytes 811016 | tf_op jit(solution)/shard_map/ppermute | solution.py:41
  9.1 13.8 %collective-permute-start.3 = (bf16[32,4224]{1,0:T(8,128)(2,1)}, bf16[32,4224]{1,0:T(8,128)(2,1)S(1)}, u32[]{:S(2)}, u32[]{:S(2)}) collective-permute-start(bf16[32,4224]{1,0:T(8,128)(2,1)} %get-tuple-element.26.own), channel_id=1, source_target_pairs={{0,64},{1,65},{2,66},{3,67},{4,68},{5,69},{6,70},{7,71},{8,72},{9,... | collective-permute-start | bytes 811016 | tf_op jit(solution)/shard_map/ppermute | solution.py:41
  11.9 14.7 %collective-permute-start.2 = (bf16[32,4224]{1,0:T(8,128)(2,1)}, bf16[32,4224]{1,0:T(8,128)(2,1)S(1)}, u32[]{:S(2)}, u32[]{:S(2)}) collective-permute-start(bf16[32,4224]{1,0:T(8,128)(2,1)} %get-tuple-element.26.own), channel_id=1, source_target_pairs={{0,80},{1,81},{2,82},{3,83},{4,84},{5,85},{6,86},{7,87},{8,88},{9,... | collective-permute-start | bytes 811016 | tf_op jit(solution)/shard_map/ppermute | solution.py:41
  13.8 13.7 %collective-permute-start.1 = (bf16[32,4224]{1,0:T(8,128)(2,1)}, bf16[32,4224]{1,0:T(8,128)(2,1)S(1)}, u32[]{:S(2)}, u32[]{:S(2)}) collective-permute-start(bf16[32,4224]{1,0:T(8,128)(2,1)} %get-tuple-element.26.own), channel_id=1, source_target_pairs={{0,16},{1,17},{2,18},{3,19},{4,20},{5,21},{6,22},{7,23},{8,24},{9,... | collective-permute-start | bytes 811016 | tf_op jit(solution)/shard_map/ppermute | solution.py:41
  16.9 10.7 %collective-permute-start.5 = (bf16[8,160,128]{2,1,0:T(8,128)(2,1)S(1)}, bf16[8,160,128]{2,1,0:T(8,128)(2,1)S(1)}, u32[]{:S(2)}, u32[]{:S(2)}) collective-permute-start(bf16[8,160,128]{2,1,0:T(8,128)(2,1)S(1)} %all-to-all-done.pc), channel_id=1, source_target_pairs={{0,3},{1,0},{2,1},{3,2},{4,7},{5,4},{6,5},{7,6},{8,11},{9,8},{10,9... | collective-permute-start | bytes 983048 | tf_op jit(solution)/shard_map/ppermute | solution.py:41
  19.9 8.7 %collective-permute-start.4 = (bf16[8,160,128]{2,1,0:T(8,128)(2,1)S(1)}, bf16[8,160,128]{2,1,0:T(8,128)(2,1)S(1)}, u32[]{:S(2)}, u32[]{:S(2)}) collective-permute-start(bf16[8,160,128]{2,1,0:T(8,128)(2,1)S(1)} %all-to-all-done.pc), channel_id=1, source_target_pairs={{0,1},{1,2},{2,3},{3,0},{4,5},{5,6},{6,7},{7,4},{8,9},{9,10},{10,1... | collective-permute-start | bytes 983048 | tf_op jit(solution)/shard_map/ppermute | solution.py:41
  27.6 4.7 %copy-start.2 = (s32[11,2]{0,1:T(2,128)S(1)}, s32[11,2]{0,1:T(2,128)}, u32[]{:S(2)}) copy-start(s32[11,2]{0,1:T(2,128)} %param.9) | copy-start | bytes 268
  28.6 2.3 %collective-permute-start.6 = (bf16[96,4224]{1,0:T(8,128)(2,1)S(1)}, bf16[96,4224]{1,0:T(8,128)(2,1)S(1)}, u32[]{:S(2)}, u32[]{:S(2)}) collective-permute-start(bf16[96,4224]{1,0:T(8,128)(2,1)S(1)} %pad_maximum_fusion.mine), channel_id=1, source_target_pairs={{0,32},{1,33},{2,34},{3,35},{4,36},{5,37},{6,38},{7,39},{8,40},{9,... | collective-permute-start | bytes 2433032 | tf_op jit(solution)/shard_map/ppermute | solution.py:41
  28.7 8.2 %collective-permute-start.8 = (bf16[4,160,128]{2,1,0:T(8,128)(2,1)S(1)}, bf16[4,160,128]{2,1,0:T(8,128)(2,1)S(1)}, u32[]{:S(2)}, u32[]{:S(2)}) collective-permute-start(bf16[4,160,128]{2,1,0:T(8,128)(2,1)S(1)} %slice.7), channel_id=1, source_target_pairs={{0,3},{1,0},{2,1},{3,2},{4,7},{5,4},{6,5},{7,6},{8,11},{9,8},{10,9... | collective-permute-start | bytes 491528 | tf_op jit(solution)/shard_map/ppermute | solution.py:41
  30.8 7.5 %collective-permute-start.7 = (bf16[4,160,128]{2,1,0:T(8,128)(2,1)S(1)}, bf16[4,160,128]{2,1,0:T(8,128)(2,1)S(1)}, u32[]{:S(2)}, u32[]{:S(2)}) collective-permute-start(bf16[4,160,128]{2,1,0:T(8,128)(2,1)S(1)} %slice.6), channel_id=1, source_target_pairs={{0,1},{1,2},{2,3},{3,0},{4,5},{5,6},{6,7},{7,4},{8,9},{9,10},{10,1... | collective-permute-start | bytes 491528 | tf_op jit(solution)/shard_map/ppermute | solution.py:41
  32.3 6.1 %copy-start.1 = (f32[160,128]{1,0:T(8,128)S(1)}, f32[160,128]{1,0:T(8,128)}, u32[]{:S(2)}) copy-start(f32[160,128]{1,0:T(8,128)} %get-tuple-element.37.info_ref) | copy-start | bytes 245764
  52.3 12.0 %collective-permute-start.9 = (bf16[8,160,128]{2,1,0:T(8,128)(2,1)S(1)}, bf16[8,160,128]{2,1,0:T(8,128)(2,1)S(1)}, u32[]{:S(2)}, u32[]{:S(2)}) collective-permute-start(bf16[8,160,128]{2,1,0:T(8,128)(2,1)S(1)} %get-tuple-element.44), channel_id=1, source_target_pairs={{0,2},{1,3},{2,0},{3,1},{4,6},{5,7},{6,4},{7,5},{8,10},{9,11},{10,... | collective-permute-start | bytes 983048 | tf_op jit(solution)/shard_map/ppermute | solution.py:41
  57.4 11.8 %collective-permute-start.11 = (bf16[8,160,128]{2,1,0:T(8,128)(2,1)S(1)}, bf16[8,160,128]{2,1,0:T(8,128)(2,1)S(1)}, u32[]{:S(2)}, u32[]{:S(2)}) collective-permute-start(bf16[8,160,128]{2,1,0:T(8,128)(2,1)S(1)} %get-tuple-element.45), channel_id=1, source_target_pairs={{0,3},{1,0},{2,1},{3,2},{4,7},{5,4},{6,5},{7,6},{8,11},{9,8},{10,9... | collective-permute-start | bytes 983048 | tf_op jit(solution)/shard_map/ppermute | solution.py:41
  59.0 11.2 %collective-permute-start.10 = (bf16[8,160,128]{2,1,0:T(8,128)(2,1)S(1)}, bf16[8,160,128]{2,1,0:T(8,128)(2,1)S(1)}, u32[]{:S(2)}, u32[]{:S(2)}) collective-permute-start(bf16[8,160,128]{2,1,0:T(8,128)(2,1)S(1)} %get-tuple-element.43.after_ref), channel_id=1, source_target_pairs={{0,1},{1,2},{2,3},{3,0},{4,5},{5,6},{6,7},{7,4},{8,9},{9,10},{10,1... | collective-permute-start | bytes 983048 | tf_op jit(solution)/shard_map/ppermute | solution.py:41

commit v6 on v5

--- a/solution.py
+++ b/solution.py
@@ -248,20 +248,20 @@
         weight = (e_ref[s] * factor).astype(jnp.bfloat16)
         w_ref[s * ROW_IMAGES : (s + 1) * ROW_IMAGES, :] = weight.T
 
-    ones = jnp.ones((16, SHIFTS * ROW_IMAGES), jnp.bfloat16)
-    totals = jnp.dot(ones, w_ref[...], preferred_element_type=jnp.float32)[0:1]
+    far = jnp.bitwise_and(position()[4] + 2, 3)
+    acc = tile_sums(shift_ref, t_ref, w_ref, 0, far, ones=16)
+    size = 2 * LANES * GROUP
+    totals = acc[size : size + 1]
     totals = jnp.concatenate([totals, jnp.zeros((1, 2 * LANES - ROWS), jnp.float32)], axis=1)
     tail = split_tail(jnp.concatenate([totals[:, :LANES], totals[:, LANES:]], axis=0))
     tail_ref[...] = tail
-    far = jnp.bitwise_and(position()[4] + 2, 3)
-    for z in range(0, 4, GROUP):
-        store_sums(out_ref, z, tile_sums(shift_ref, t_ref, w_ref, z, far), tail)
+    store_sums(out_ref, 0, acc[:size], tail)
 
 
 GROUP = 4
 
 
-def tile_sums(shift_ref, t_ref, w_ref, z, *ys):
+def tile_sums(shift_ref, t_ref, w_ref, z, *ys, ones=0):
     tiles = []
     for y, k in [(y, k) for y in ys for k in range(GROUP)]:
         low = 2 * (4 * (z + k) + y)
@@ -275,6 +275,8 @@
                 axis=1,
             )
         )
+    if ones:
+        tiles.append(jnp.ones((ones, SHIFTS * ROW_IMAGES), jnp.bfloat16))
     moved = jnp.concatenate(tiles, axis=0)
     return jnp.dot(moved, w_ref[...], preferred_element_type=jnp.float32)
 

time: 83.2 us -> 83 us (level)
  no operation moved by 1% of the time
where the time goes in v6:
time: 83 us; the launch traced here: 82.7 us
  waiting for transfers between devices  21.3 us (26%)
  Pallas kernels  20.9 us (25%)
  blocking collectives  20.1 us (24%)
  starting transfers between devices  19.5 us (23%)
    ppermute x12, waiting for transfers between devices, move(): return lax.ppermute(value, AXES, route)  18.3 us
    ppermute x12, starting transfers between devices, move(): return lax.ppermute(value, AXES, route)  13 us
    all_to_all x1, blocking collectives, shards(): lax.all_to_all(column_sums, 'img', 0, 0, axis_index_groups=XZ_GROUPS)  11.8 us
    all_to_all x1, blocking collectives, shards(): all_stats = lax.all_to_all(stats, AXES, 0, 0, axis_index_groups=X_ROWS)  8.31 us
    all_to_all x1, starting transfers between devices, shards(): column = lax.all_to_all(spread, 'img', 0, 0, axis_index_groups=XZ_GROUPS)  6.47 us
    pallas_call x1, Pallas kernels, shards(): pl.pallas_call(first_kernel, out_shape=(score_shape, norm_shape), in_spec...  4.68 us
    pallas_call x1, Pallas kernels, shards(): pl.pallas_call(near_kernel, out_shape=(block_shape,) * 2, in_specs=[SMEM]...  4.34 us
    pallas_call x1, Pallas kernels, shards(): pl.pallas_call(far_kernel, out_shape=(block_shape, jax.ShapeDtypeStruct((...  2.98 us
  transfers between devices with their start and end apart: 13, of which 10 were waited for; matrix products, arithmetic and copies ran while one was open for 0% of the time, Pallas kernels for 15%

profile of v6, /device:TPU:0, one launch (start us, length us, event | category | flops | bytes accessed | tf_op | source)
XLA Modules:
  0.0 82.7 jit_solution(3355613263671907385)
XLA Ops:
  0.6 2.0 %prepare.1 = (bf16[8,160,128]{2,1,0:T(8,128)(2,1)}, bf16[32,4224]{1,0:T(8,128)(2,1)}, f32[160,128]{1,0:T(8,128)}) custom-call(bf16[12,25,128]{2,1,0:T(8,128)(2,1)} %bitcast.12, f32[32,4096]{1,0:T(8,128)} %refs_1_.1, s32[1,32]{1,0:T(1,128)} %bitcast.13, f32[1,25]{1,0:T(1,128)} %bitcast.14), custom_call_target="tpu_custom_call" | custom-call | bytes 1000 | tf_op jit(solution)/shard_map/prepare/pallas_call | solution.py:373
  2.6 6.5 %all-to-all-start = ((bf16[8,160,128]{2,1,0:T(8,128)(2,1)}), bf16[8,160,128]{2,1,0:T(8,128)(2,1)S(1)}, u32[]{:S(2)}, u32[]{:S(2)}) async-start(bf16[8,160,128]{2,1,0:T(8,128)(2,1)} %get-tuple-element.27), calls=%async_computation | async-start | bytes 655360 | tf_op jit(solution)/shard_map/all_to_all | solution.py:407
  9.1 2.8 %collective-permute-start.3 = (bf16[32,4224]{1,0:T(8,128)(2,1)}, bf16[32,4224]{1,0:T(8,128)(2,1)S(1)}, u32[]{:S(2)}, u32[]{:S(2)}) collective-permute-start(bf16[32,4224]{1,0:T(8,128)(2,1)} %get-tuple-element.26.own), channel_id=1, source_target_pairs={{0,64},{1,65},{2,66},{3,67},{4,68},{5,69},{6,70},{7,71},{8,72},{9,... | collective-permute-start | bytes 811016 | tf_op jit(solution)/shard_map/ppermute | solution.py:41
  11.9 1.9 %collective-permute-start.2 = (bf16[32,4224]{1,0:T(8,128)(2,1)}, bf16[32,4224]{1,0:T(8,128)(2,1)S(1)}, u32[]{:S(2)}, u32[]{:S(2)}) collective-permute-start(bf16[32,4224]{1,0:T(8,128)(2,1)} %get-tuple-element.26.own), channel_id=1, source_target_pairs={{0,80},{1,81},{2,82},{3,83},{4,84},{5,85},{6,86},{7,87},{8,88},{9,... | collective-permute-start | bytes 811016 | tf_op jit(solution)/shard_map/ppermute | solution.py:41
  13.8 0.1 collective-permute-start.1
  13.9 3.0 %all-to-all-done.pc = bf16[8,160,128]{2,1,0:T(8,128)(2,1)S(1)} async-done(((bf16[8,160,128]{2,1,0:T(8,128)(2,1)}), bf16[8,160,128]{2,1,0:T(8,128)(2,1)S(1)}, u32[]{:S(2)}, u32[]{:S(2)}) %all-to-all-start) | async-done | bytes 327712 | tf_op jit(solution)/shard_map/all_to_all | solution.py:407
  16.9 3.0 %collective-permute-start.5 = (bf16[8,160,128]{2,1,0:T(8,128)(2,1)S(1)}, bf16[8,160,128]{2,1,0:T(8,128)(2,1)S(1)}, u32[]{:S(2)}, u32[]{:S(2)}) collective-permute-start(bf16[8,160,128]{2,1,0:T(8,128)(2,1)S(1)} %all-to-all-done.pc), channel_id=1, source_target_pairs={{0,3},{1,0},{2,1},{3,2},{4,7},{5,4},{6,5},{7,6},{8,11},{9,8},{10,9... | collective-permute-start | bytes 983048 | tf_op jit(solution)/shard_map/ppermute | solution.py:41
  19.9 3.0 %collective-permute-done.3 = bf16[32,4224]{1,0:T(8,128)(2,1)S(1)} collective-permute-done((bf16[32,4224]{1,0:T(8,128)(2,1)}, bf16[32,4224]{1,0:T(8,128)(2,1)S(1)}, u32[]{:S(2)}, u32[]{:S(2)}) %collective-permute-start.3) | collective-permute-done | bytes 270368 | tf_op jit(solution)/shard_map/ppermute | solution.py:41
  22.9 3.7 %collective-permute-done.2 = bf16[32,4224]{1,0:T(8,128)(2,1)S(1)} collective-permute-done((bf16[32,4224]{1,0:T(8,128)(2,1)}, bf16[32,4224]{1,0:T(8,128)(2,1)S(1)}, u32[]{:S(2)}, u32[]{:S(2)}) %collective-permute-start.2) | collective-permute-done | bytes 270368 | tf_op jit(solution)/shard_map/ppermute | solution.py:41
  26.6 0.9 %collective-permute-done.1 = bf16[32,4224]{1,0:T(8,128)(2,1)S(1)} collective-permute-done((bf16[32,4224]{1,0:T(8,128)(2,1)}, bf16[32,4224]{1,0:T(8,128)(2,1)S(1)}, u32[]{:S(2)}, u32[]{:S(2)}) %collective-permute-start.1) | collective-permute-done | bytes 270368 | tf_op jit(solution)/shard_map/ppermute | solution.py:41
  27.5 0.1 pad_maximum_fusion.mine
  27.6 0.0 copy-start.2
  27.6 1.0 %collective-permute-done.4.py1 = bf16[8,160,128]{2,1,0:T(8,128)(2,1)S(1)} collective-permute-done((bf16[8,160,128]{2,1,0:T(8,128)(2,1)S(1)}, bf16[8,160,128]{2,1,0:T(8,128)(2,1)S(1)}, u32[]{:S(2)}, u32[]{:S(2)}) %collective-permute-start.4) | collective-permute-done | bytes 327712 | tf_op jit(solution)/shard_map/ppermute | solution.py:41
  28.7 2.2 %collective-permute-start.8 = (bf16[4,160,128]{2,1,0:T(8,128)(2,1)S(1)}, bf16[4,160,128]{2,1,0:T(8,128)(2,1)S(1)}, u32[]{:S(2)}, u32[]{:S(2)}) collective-permute-start(bf16[4,160,128]{2,1,0:T(8,128)(2,1)S(1)} %slice.7), channel_id=1, source_target_pairs={{0,3},{1,0},{2,1},{3,2},{4,7},{5,4},{6,5},{7,6},{8,11},{9,8},{10,9... | collective-permute-start | bytes 491528 | tf_op jit(solution)/shard_map/ppermute | solution.py:41
  30.8 0.1 collective-permute-done.6.other
  30.9 1.3 %turn.1 = (f32[2,64,80,128]{3,2,1,0:T(8,128)S(1)}, f32[2,8,128]{2,1,0:T(8,128)S(1)}) custom-call(bf16[32,4224]{1,0:T(8,128)(2,1)S(1)} %copy-done, bf16[32,4224]{1,0:T(8,128)(2,1)S(1)} %collective-permute-done.own_other, bf16[96,4224]{1,0:T(8,128)(2,1)S(1)} %pad_maximum_fusion.mine, bf16[96,4224]{1,0:T(8,128)(2,1)S(1)} %collective-permute-done.6.other), custom_call_target="tpu_custom_call" | custom-call | bytes 8000 | tf_op jit(solution)/shard_map/turn/pallas_call | solution.py:417
  32.3 4.7 %first.1 = (f32[11,160,256]{2,1,0:T(8,128)S(1)}, f32[160,128]{1,0:T(8,128)S(1)}) custom-call(s32[2,11]{1,0:T(2,128)S(1)} %bitcast.7, f32[2,64,80,128]{3,2,1,0:T(8,128)S(1)} %get-tuple-element.31.t_ref, bf16[8,160,128]{2,1,0:T(8,128)(2,1)S(1)} %all-to-all-done.pc, bf16[8,160,128]{2,1,0:T(8,128)(2,1)S(1)} %collective-permute-done.4.py1, ...), custom_call_target="tpu_custom_call" | custom-call | flops 3000 | bytes 4000 | tf_op jit(solution)/shard_map/first/pallas_call | solution.py:434
  37.0 1.4 %collective-permute-done.7.pw0 = bf16[4,160,128]{2,1,0:T(8,128)(2,1)S(1)} collective-permute-done((bf16[4,160,128]{2,1,0:T(8,128)(2,1)S(1)}, bf16[4,160,128]{2,1,0:T(8,128)(2,1)S(1)}, u32[]{:S(2)}, u32[]{:S(2)}) %collective-permute-start.7) | collective-permute-done | bytes 163872 | tf_op jit(solution)/shard_map/ppermute | solution.py:41
  38.4 2.4 %last.1 = (f32[11,160,256]{2,1,0:T(8,128)S(1)}, f32[8,8,128]{2,1,0:T(8,128)S(1)}, f32[16,256]{1,0:T(8,128)S(1)}) custom-call(s32[2,11]{1,0:T(2,128)S(1)} %bitcast.8, f32[2,64,80,128]{3,2,1,0:T(8,128)S(1)} %get-tuple-element.31.t_ref, bf16[4,160,128]{2,1,0:T(8,128)(2,1)S(1)} %collective-permute-done.7.pw0, ...), custom_call_target="tpu_custom_call", output_to_operand_aliasing={{0}: (4, {})} | custom-call | flops 1000 | bytes 8000 | tf_op jit(solution)/shard_map/last/pallas_call | solution.py:444
  40.8 8.3 %all_to_all.15.all_ref = f32[8,8,128]{2,1,0:T(8,128)S(1)} all-to-all(f32[8,8,128]{2,1,0:T(8,128)S(1)} %get-tuple-element.40), channel_id=1, replica_groups={{0,32,16,48,64,96,80,112},{1,33,17,49,65,97,81,113},{2,34,18,50,66,98,8..., dimensions={0} | all-to-all | bytes 65536 | tf_op jit(solution)/shard_map/all_to_all | solution.py:458
  49.1 3.0 %far.1 = (bf16[8,160,128]{2,1,0:T(8,128)(2,1)S(1)}, f32[1,32]{1,0:T(1,128)}, bf16[2816,160]{1,0:T(8,128)(2,1)S(1)}, bf16[16,128]{1,0:T(8,128)(2,1)S(1)}) custom-call(s32[2,11]{1,0:T(2,128)S(1)} %bitcast.9, f32[11,160,256]{2,1,0:T(8,128)S(1)} %get-tuple-element.38.e_ref, f32[16,256]{1,0:T(8,128)S(1)} %get-tuple-element.39.m_ref, ...), custom_call_target="tpu_custom_call" | custom-call | flops 1000 | bytes 4000 | tf_op jit(solution)/shard_map/far/pallas_call | solution.py:460
  52.1 0.9 %collective-permute-start.9 = (bf16[8,160,128]{2,1,0:T(8,128)(2,1)S(1)}, bf16[8,160,128]{2,1,0:T(8,128)(2,1)S(1)}, u32[]{:S(2)}, u32[]{:S(2)}) collective-permute-start(bf16[8,160,128]{2,1,0:T(8,128)(2,1)S(1)} %get-tuple-element.44), channel_id=1, source_target_pairs={{0,2},{1,3},{2,0},{3,1},{4,6},{5,7},{6,4},{7,5},{8,10},{9,11},{10,... | collective-permute-start | bytes 983048 | tf_op jit(solution)/shard_map/ppermute | solution.py:41
  53.0 4.3 %near.1 = (bf16[8,160,128]{2,1,0:T(8,128)(2,1)S(1)}, bf16[8,160,128]{2,1,0:T(8,128)(2,1)S(1)}) custom-call(s32[2,11]{1,0:T(2,128)S(1)} %bitcast.10, bf16[2816,160]{1,0:T(8,128)(2,1)S(1)} %get-tuple-element.41.w_ref, bf16[16,128]{1,0:T(8,128)(2,1)S(1)} %get-tuple-element.42.tail_ref, f32[2,64,80,128]{3,2,1,0:T(8,128)S(1)} %get-tuple-element.31.t_ref), custom_call_target="tpu_custom_call" | custom-call | flops 2000 | bytes 4000 | tf_op jit(solution)/shard_map/near/pallas_call | solution.py:475
  57.3 1.5 %collective-permute-start.11 = (bf16[8,160,128]{2,1,0:T(8,128)(2,1)S(1)}, bf16[8,160,128]{2,1,0:T(8,128)(2,1)S(1)}, u32[]{:S(2)}, u32[]{:S(2)}) collective-permute-start(bf16[8,160,128]{2,1,0:T(8,128)(2,1)S(1)} %get-tuple-element.45), channel_id=1, source_target_pairs={{0,3},{1,0},{2,1},{3,2},{4,7},{5,4},{6,5},{7,6},{8,11},{9,8},{10,9... | collective-permute-start | bytes 983048 | tf_op jit(solution)/shard_map/ppermute | solution.py:41
  58.8 0.6 collective-permute-start.10
  59.4 2.4 %own.1.own_ref = f32[8,160,128]{2,1,0:T(8,128)S(1)} custom-call(s32[2,11]{1,0:T(2,128)S(1)} %bitcast.11, bf16[2816,160]{1,0:T(8,128)(2,1)S(1)} %get-tuple-element.41.w_ref, f32[2,64,80,128]{3,2,1,0:T(8,128)S(1)} %get-tuple-element.31.t_ref, bf16[8,160,128]{2,1,0:T(8,128)(2,1)S(1)} %get-tuple-element.43.after_ref), custom_call_target="tpu_custom_call" | custom-call | flops 1000 | bytes 4000 | tf_op jit(solution)/shard_map/own/pallas_call | solution.py:486
  61.8 2.3 %collective-permute-done.9.far_ref = bf16[8,160,128]{2,1,0:T(8,128)(2,1)S(1)} collective-permute-done((bf16[8,160,128]{2,1,0:T(8,128)(2,1)S(1)}, bf16[8,160,128]{2,1,0:T(8,128)(2,1)S(1)}, u32[]{:S(2)}, u32[]{:S(2)}) %collective-permute-start.9) | collective-permute-done | bytes 327712 | tf_op jit(solution)/shard_map/ppermute | solution.py:41
  64.0 5.0 %collective-permute-done.11.down_ref = bf16[8,160,128]{2,1,0:T(8,128)(2,1)S(1)} collective-permute-done((bf16[8,160,128]{2,1,0:T(8,128)(2,1)S(1)}, bf16[8,160,128]{2,1,0:T(8,128)(2,1)S(1)}, u32[]{:S(2)}, u32[]{:S(2)}) %collective-permute-start.11) | collective-permute-done | bytes 327712 | tf_op jit(solution)/shard_map/ppermute | solution.py:41
  69.1 0.9 %collective-permute-done.10.up_ref = bf16[8,160,128]{2,1,0:T(8,128)(2,1)S(1)} collective-permute-done((bf16[8,160,128]{2,1,0:T(8,128)(2,1)S(1)}, bf16[8,160,128]{2,1,0:T(8,128)(2,1)S(1)}, u32[]{:S(2)}, u32[]{:S(2)}) %collective-permute-start.10) | collective-permute-done | bytes 327712 | tf_op jit(solution)/shard_map/ppermute | solution.py:41
  70.0 0.2 add.1
  70.2 11.8 %all_to_all.16.in_ref = bf16[8,160,128]{2,1,0:T(8,128)(2,1)S(1)} all-to-all(bf16[8,160,128]{2,1,0:T(8,128)(2,1)S(1)} %add.1), channel_id=1, replica_groups={{0,4,8,12,16,20,24,28},{1,5,9,13,17,21,25,29},{2,6,10,14,18,22,26,30},{..., dimensions={0} | all-to-all | bytes 655360 | tf_op jit(solution)/shard_map/all_to_all | solution.py:504
  81.9 0.7 finish.1
  (14 shorter events, 0.1 us)
Async XLA Ops:
  2.6 28.3 %copy-start = (bf16[32,4224]{1,0:T(8,128)(2,1)S(1)}, bf16[32,4224]{1,0:T(8,128)(2,1)}, u32[]{:S(2)}) copy-start(bf16[32,4224]{1,0:T(8,128)(2,1)} %get-tuple-element.26.own) | copy-start | bytes 811012
  2.6 14.3 %all-to-all-start = ((bf16[8,160,128]{2,1,0:T(8,128)(2,1)}), bf16[8,160,128]{2,1,0:T(8,128)(2,1)S(1)}, u32[]{:S(2)}, u32[]{:S(2)}) async-start(bf16[8,160,128]{2,1,0:T(8,128)(2,1)} %get-tuple-element.27), calls=%async_computation | async-start | bytes 655360 | tf_op jit(solution)/shard_map/all_to_all | solution.py:407
  9.1 4.8 %collective-permute-start = (bf16[32,4224]{1,0:T(8,128)(2,1)}, bf16[32,4224]{1,0:T(8,128)(2,1)S(1)}, u32[]{:S(2)}, u32[]{:S(2)}) collective-permute-start(bf16[32,4224]{1,0:T(8,128)(2,1)} %get-tuple-element.26.own), channel_id=1, source_target_pairs={{0,32},{1,33},{2,34},{3,35},{4,36},{5,37},{6,38},{7,39},{8,40},{9,... | collective-permute-start | bytes 811016 | tf_op jit(solution)/shard_map/ppermute | solution.py:41
  9.1 13.8 %collective-permute-start.3 = (bf16[32,4224]{1,0:T(8,128)(2,1)}, bf16[32,4224]{1,0:T(8,128)(2,1)S(1)}, u32[]{:S(2)}, u32[]{:S(2)}) collective-permute-start(bf16[32,4224]{1,0:T(8,128)(2,1)} %get-tuple-element.26.own), channel_id=1, source_target_pairs={{0,64},{1,65},{2,66},{3,67},{4,68},{5,69},{6,70},{7,71},{8,72},{9,... | collective-permute-start | bytes 811016 | tf_op jit(solution)/shard_map/ppermute | solution.py:41
  11.9 14.7 %collective-permute-start.2 = (bf16[32,4224]{1,0:T(8,128)(2,1)}, bf16[32,4224]{1,0:T(8,128)(2,1)S(1)}, u32[]{:S(2)}, u32[]{:S(2)}) collective-permute-start(bf16[32,4224]{1,0:T(8,128)(2,1)} %get-tuple-element.26.own), channel_id=1, source_target_pairs={{0,80},{1,81},{2,82},{3,83},{4,84},{5,85},{6,86},{7,87},{8,88},{9,... | collective-permute-start | bytes 811016 | tf_op jit(solution)/shard_map/ppermute | solution.py:41
  13.8 13.7 %collective-permute-start.1 = (bf16[32,4224]{1,0:T(8,128)(2,1)}, bf16[32,4224]{1,0:T(8,128)(2,1)S(1)}, u32[]{:S(2)}, u32[]{:S(2)}) collective-permute-start(bf16[32,4224]{1,0:T(8,128)(2,1)} %get-tuple-element.26.own), channel_id=1, source_target_pairs={{0,16},{1,17},{2,18},{3,19},{4,20},{5,21},{6,22},{7,23},{8,24},{9,... | collective-permute-start | bytes 811016 | tf_op jit(solution)/shard_map/ppermute | solution.py:41
  16.9 10.7 %collective-permute-start.5 = (bf16[8,160,128]{2,1,0:T(8,128)(2,1)S(1)}, bf16[8,160,128]{2,1,0:T(8,128)(2,1)S(1)}, u32[]{:S(2)}, u32[]{:S(2)}) collective-permute-start(bf16[8,160,128]{2,1,0:T(8,128)(2,1)S(1)} %all-to-all-done.pc), channel_id=1, source_target_pairs={{0,3},{1,0},{2,1},{3,2},{4,7},{5,4},{6,5},{7,6},{8,11},{9,8},{10,9... | collective-permute-start | bytes 983048 | tf_op jit(solution)/shard_map/ppermute | solution.py:41
  19.9 8.7 %collective-permute-start.4 = (bf16[8,160,128]{2,1,0:T(8,128)(2,1)S(1)}, bf16[8,160,128]{2,1,0:T(8,128)(2,1)S(1)}, u32[]{:S(2)}, u32[]{:S(2)}) collective-permute-start(bf16[8,160,128]{2,1,0:T(8,128)(2,1)S(1)} %all-to-all-done.pc), channel_id=1, source_target_pairs={{0,1},{1,2},{2,3},{3,0},{4,5},{5,6},{6,7},{7,4},{8,9},{9,10},{10,1... | collective-permute-start | bytes 983048 | tf_op jit(solution)/shard_map/ppermute | solution.py:41
  27.6 4.7 %copy-start.2 = (s32[11,2]{0,1:T(2,128)S(1)}, s32[11,2]{0,1:T(2,128)}, u32[]{:S(2)}) copy-start(s32[11,2]{0,1:T(2,128)} %param.9) | copy-start | bytes 268
  28.6 2.3 %collective-permute-start.6 = (bf16[96,4224]{1,0:T(8,128)(2,1)S(1)}, bf16[96,4224]{1,0:T(8,128)(2,1)S(1)}, u32[]{:S(2)}, u32[]{:S(2)}) collective-permute-start(bf16[96,4224]{1,0:T(8,128)(2,1)S(1)} %pad_maximum_fusion.mine), channel_id=1, source_target_pairs={{0,32},{1,33},{2,34},{3,35},{4,36},{5,37},{6,38},{7,39},{8,40},{9,... | collective-permute-start | bytes 2433032 | tf_op jit(solution)/shard_map/ppermute | solution.py:41
  28.7 8.3 %collective-permute-start.8 = (bf16[4,160,128]{2,1,0:T(8,128)(2,1)S(1)}, bf16[4,160,128]{2,1,0:T(8,128)(2,1)S(1)}, u32[]{:S(2)}, u32[]{:S(2)}) collective-permute-start(bf16[4,160,128]{2,1,0:T(8,128)(2,1)S(1)} %slice.7), channel_id=1, source_target_pairs={{0,3},{1,0},{2,1},{3,2},{4,7},{5,4},{6,5},{7,6},{8,11},{9,8},{10,9... | collective-permute-start | bytes 491528 | tf_op jit(solution)/shard_map/ppermute | solution.py:41
  30.8 7.5 %collective-permute-start.7 = (bf16[4,160,128]{2,1,0:T(8,128)(2,1)S(1)}, bf16[4,160,128]{2,1,0:T(8,128)(2,1)S(1)}, u32[]{:S(2)}, u32[]{:S(2)}) collective-permute-start(bf16[4,160,128]{2,1,0:T(8,128)(2,1)S(1)} %slice.6), channel_id=1, source_target_pairs={{0,1},{1,2},{2,3},{3,0},{4,5},{5,6},{6,7},{7,4},{8,9},{9,10},{10,1... | collective-permute-start | bytes 491528 | tf_op jit(solution)/shard_map/ppermute | solution.py:41
  32.3 6.1 %copy-start.1 = (f32[160,128]{1,0:T(8,128)S(1)}, f32[160,128]{1,0:T(8,128)}, u32[]{:S(2)}) copy-start(f32[160,128]{1,0:T(8,128)} %get-tuple-element.37.info_ref) | copy-start | bytes 245764
  52.1 12.0 %collective-permute-start.9 = (bf16[8,160,128]{2,1,0:T(8,128)(2,1)S(1)}, bf16[8,160,128]{2,1,0:T(8,128)(2,1)S(1)}, u32[]{:S(2)}, u32[]{:S(2)}) collective-permute-start(bf16[8,160,128]{2,1,0:T(8,128)(2,1)S(1)} %get-tuple-element.44), channel_id=1, source_target_pairs={{0,2},{1,3},{2,0},{3,1},{4,6},{5,7},{6,4},{7,5},{8,10},{9,11},{10,... | collective-permute-start | bytes 983048 | tf_op jit(solution)/shard_map/ppermute | solution.py:41
  57.3 11.8 %collective-permute-start.11 = (bf16[8,160,128]{2,1,0:T(8,128)(2,1)S(1)}, bf16[8,160,128]{2,1,0:T(8,128)(2,1)S(1)}, u32[]{:S(2)}, u32[]{:S(2)}) collective-permute-start(bf16[8,160,128]{2,1,0:T(8,128)(2,1)S(1)} %get-tuple-element.45), channel_id=1, source_target_pairs={{0,3},{1,0},{2,1},{3,2},{4,7},{5,4},{6,5},{7,6},{8,11},{9,8},{10,9... | collective-permute-start | bytes 983048 | tf_op jit(solution)/shard_map/ppermute | solution.py:41
  58.8 11.1 %collective-permute-start.10 = (bf16[8,160,128]{2,1,0:T(8,128)(2,1)S(1)}, bf16[8,160,128]{2,1,0:T(8,128)(2,1)S(1)}, u32[]{:S(2)}, u32[]{:S(2)}) collective-permute-start(bf16[8,160,128]{2,1,0:T(8,128)(2,1)S(1)} %get-tuple-element.43.after_ref), channel_id=1, source_target_pairs={{0,1},{1,2},{2,3},{3,0},{4,5},{5,6},{6,7},{7,4},{8,9},{9,10},{10,1... | collective-permute-start | bytes 983048 | tf_op jit(solution)/shard_map/ppermute | solution.py:41
